TPU v7x, 32 devices: a whole 2x2x4 slice. The times are simulated.
32 devices in a mesh: tile: 8 (over z, y), grp: 4 (over x, core).
Axes of the slice: x: 2, y: 2, z: 4, core: 2. Of those that a mesh axis runs over, the one named last changes fastest.
Arguments:
- velocity: float32 [3, 64, 256, 512], P(None, 'grp', 'tile'), may hold values from -6 to 6
- modes: float32 [128, 98304], P(None, ('tile', 'grp')), may hold values from -6 to 6
- mode_weights: float32 [128], replicated, may hold values from 1 to 10
- history: float32 [63, 98304], P(None, ('tile', 'grp')), may hold values from -6 to 6
- slab_ids: int32 [32768], P(('tile', 'grp')), may hold values from 0 to 262143
- snap_steps: int32 [64], replicated, may hold values from 0 to 63, each once
Outputs:
- advanced: float32 [3, 64, 256, 512], P(None, 'grp', 'tile')
- basis: float32 [192, 98304], P(None, ('tile', 'grp'))
- factor: float32 [192, 192], replicated
Inputs may be any that keep to these rules, and one draw needn't show every extreme that they name: `slab_ids`: each id is a cell of the owning device's block. `snap_steps`: each step index appears once.
All inputs are finite; a program needn't handle non-finite values.
Results may differ from a plain program's by a relative error of at most 0.000098.
Values sent between devices are 32-bit elements; how exact they have to be, the bound alone decides.
No kernel may reach another device: no remote copies, remote signals or barrier semaphores. Data moves between devices by JAX's collectives and lax.ppermute only.
A program may use at most 320 MiB of HBM per device.

v0:
```python
import jax
import jax.numpy as jnp
from jax import lax
from jax.sharding import PartitionSpec as P

time_step = 0.1
viscosity = 0.5


def with_halo(block, sides, width):
    for axis, dim in sides:
        count = lax.axis_size(axis)
        forward = [(i, i + 1) for i in range(count - 1)]
        forward.append((count - 1, 0))
        backward = [(target, source) for source, target in forward]
        low = lax.ppermute(
            lax.slice_in_dim(block, block.shape[dim] - width, None, axis=dim), axis, forward
        )
        high = lax.ppermute(lax.slice_in_dim(block, 0, width, axis=dim), axis, backward)
        block = jnp.concatenate([low, block, high], axis=dim)
    return block


def advance(padded):
    center = padded[:, 1:-1, 1:-1, :]
    x_plus = padded[:, 2:, 1:-1, :]
    x_minus = padded[:, :-2, 1:-1, :]
    y_plus = padded[:, 1:-1, 2:, :]
    y_minus = padded[:, 1:-1, :-2, :]
    z_plus = jnp.roll(center, -1, axis=3)
    z_minus = jnp.roll(center, 1, axis=3)
    laplace = x_plus + x_minus + y_plus + y_minus + z_plus + z_minus - 6.0 * center
    carried = (
        center[0:1] * (0.5 * (x_plus - x_minus))
        + center[1:2] * (0.5 * (y_plus - y_minus))
        + center[2:3] * (0.5 * (z_plus - z_minus))
    )
    return center + time_step * (viscosity * laplace - carried)


def per_device(velocity, modes, mode_weights, history, slab_ids, snap_steps):
    field = velocity
    for step in range(2):
        padded = with_halo(field, (("tile", 2), ("grp", 1)), 1)
        field = advance(padded)
    flat_cells = field.reshape(3, -1)
    sample = jnp.take(flat_cells, slab_ids, axis=1).reshape(1, -1)
    stacked = jnp.concatenate([history, sample], axis=0)
    count = stacked.shape[0]
    selector = (snap_steps[:, None] == jnp.arange(count, dtype=jnp.int32)[None, :]).astype(
        jnp.float32
    )
    snapshots = jnp.dot(selector, stacked, precision=lax.Precision.HIGHEST)
    combined = jnp.concatenate([mode_weights[:, None] * modes, snapshots], axis=0)
    local_gram = jnp.dot(combined, combined.T, precision=lax.Precision.HIGHEST)
    gram = lax.psum(local_gram, ("tile", "grp"))
    lower = jnp.linalg.cholesky(gram)
    total_rows = combined.shape[1] * lax.axis_size("tile") * lax.axis_size("grp")
    root = jnp.sqrt(jnp.float32(total_rows))
    basis = lax.linalg.triangular_solve(lower, combined, left_side=True, lower=True) * root
    factor = lower.T / root
    return (field, basis, factor)


def solution(mesh):
    return jax.shard_map(
        per_device,
        mesh=mesh,
        in_specs=(
            P(None, "grp", "tile", None),
            P(None, ("tile", "grp")),
            P(),
            P(None, ("tile", "grp")),
            P(("tile", "grp")),
            P(),
        ),
        out_specs=(P(None, "grp", "tile", None), P(None, ("tile", "grp")), P()),
        check_vma=False,
    )
```

profile of v0, /device:TPU:0, one launch (start us, length us, event | category | flops | bytes accessed | tf_op | source)
XLA Modules:
  0.0 326.7 jit_solution(11916782456812139431)
XLA Ops:
  7.2 0.0 all-reduce.5.cloned.1.call-start
  7.2 1.6 fusion.27
  8.8 3.0 collective-permute-start
  11.8 3.1 collective-permute-start.1
  14.9 2.2 multiply_bitcast_fusion.2
  17.2 1.2 fusion.28
  18.4 0.0 copy-start.4
  18.5 0.0 copy-start.3
  18.5 0.0 copy-start.6
  18.5 0.3 fusion.29
  18.8 0.4 copy-done.4
  19.1 0.7 copy-done.3
  19.9 1.3 broadcast_multiply_fusion
  21.2 0.0 collective-permute-done
  21.2 0.1 copy.40
  21.4 0.0 collective-permute-done.1
  21.4 0.1 copy.41
  21.5 0.1 pad_maximum_fusion.23
  21.6 0.7 collective-permute-start.2
  22.3 0.0 collective-permute-start.3
  22.3 5.9 %collective-permute-done.2 = f32[3,1,34,512]{3,2,1,0:T(8,128)S(1)} collective-permute-done((f32[3,1,34,512]{3,2,1,0:T(8,128)S(1)}, f32[3,1,34,512]{3,2,1,0:T(8,128)S(1)}, u32[]{:S(2)}, u32[]{:S(2)}) %collective-permute-start.2) | collective-permute-done | bytes 208928 | tf_op jit(solution)/shard_map/ppermute | solution.py:19
  28.2 1.8 collective-permute-done.3
  30.0 5.2 %multiply_add_fusion.1 = f32[3,16,32,512]{3,2,1,0:T(8,128)S(1)} fusion(f32[3,16,32,512]{3,2,1,0:T(8,128)S(1)} %copy-done, f32[3,16,32,511]{3,2,1,0:T(8,128)S(1)} %get-tuple-element.54, f32[3,16,32,1]{3,2,1,0:T(8,128)S(1)} %get-tuple-element.56, f32[3,16,32,1]{3,2,1,0:T(8,128)S(1)} %get-tuple-element.55, f32[3,16,32,511]{3,2,1,0:T(8,128)S(1)} %get-tuple-element.53, ...), kind=kLoop, calls=%fused_computation.23 | loop fusion | flops 22806528 | bytes 16343040 | tf_op jit(solution)/shard_map/add | solution.py:38
  35.3 0.2 fusion.24
  35.4 1.2 fusion.25
  36.7 0.1 collective-permute-start.4
  36.8 4.7 %collective-permute-start.5 = (f32[3,16,1,512]{3,1,2,0:T(8,128)S(1)}, f32[3,16,1,512]{3,1,2,0:T(8,128)S(1)}, u32[]{:S(2)}, u32[]{:S(2)}) collective-permute-start(f32[3,16,1,512]{3,1,2,0:T(8,128)S(1)} %copy.45), channel_id=1, source_target_pairs={{4,0},{8,4},{12,8},{16,12},{20,16},{24,20},{28,24},{0,28},{5,1},{9... | collective-permute-start | bytes 294920 | tf_op jit(solution)/shard_map/ppermute | solution.py:19
  41.5 0.6 fusion.6
  42.2 1.9 collective-permute-done.4
  44.1 0.1 copy.46
  44.2 0.1 copy.47
  44.3 0.1 pad_maximum_fusion.20
  44.4 0.1 collective-permute-start.6
  44.5 0.5 collective-permute-start.7
  44.9 0.3 fusion.26
  45.2 5.1 %collective-permute-done.6 = f32[3,1,34,512]{3,2,1,0:T(8,128)S(1)} collective-permute-done((f32[3,1,34,512]{3,2,1,0:T(8,128)S(1)}, f32[3,1,34,512]{3,2,1,0:T(8,128)S(1)}, u32[]{:S(2)}, u32[]{:S(2)}) %collective-permute-start.6) | collective-permute-done | bytes 208928 | tf_op jit(solution)/shard_map/ppermute | solution.py:19
  50.3 2.0 collective-permute-done.7
  52.3 5.2 %multiply_add_fusion = f32[3,16,32,512]{3,2,1,0:T(8,128)S(1)} fusion(f32[3,16,32,512]{3,2,1,0:T(8,128)S(1)} %multiply_add_fusion.1, f32[3,16,32,511]{3,2,1,0:T(8,128)S(1)} %get-tuple-element.45, f32[3,16,32,1]{3,2,1,0:T(8,128)S(1)} %get-tuple-element.47, f32[3,16,32,1]{3,2,1,0:T(8,128)S(1)} %get-tuple-element.46, ...), kind=kLoop, calls=%fused_computation.22 | loop fusion | flops 22806528 | bytes 16343040 | tf_op jit(solution)/shard_map/add | solution.py:38
  57.5 0.0 copy-start.1
  57.5 0.0 copy-start.5
  57.5 64.5 %copy.50 = f32[3,16,32,512]{0,3,2,1:T(8,128)} copy(f32[3,16,32,512]{3,2,1,0:T(8,128)S(1)} %multiply_add_fusion) | data formatting | bytes 6291456 | tf_op jit(solution)/shard_map/add | solution.py:38
  122.1 10.6 %gather_fusion = f32[1024,3]{1,0:T(8,128)S(1)} fusion(f32[3,262144]{0,1:T(8,128)} %bitcast.6, s32[1024]{0:T(1024)S(1)} %fusion.21), kind=kCustom, calls=%fused_computation | custom fusion | bytes 28672 | tf_op jit(solution)/shard_map/jit(_take)/gather | solution.py:47
  132.7 0.2 select_bitcast_fusion
  132.9 0.2 copy.51
  133.2 1.7 fusion.7
  134.9 2.7 fusion
  137.6 0.0 all-reduce.5.cloned.1.call-update
  137.6 124.0 %all-reduce.5.cloned.1.call-done = f32[192,192]{0,1:T(8,128)} async-done(((f32[192,192]{0,1:T(8,128)}), f32[192,192]{0,1:T(8,128)}) %all-reduce.5.cloned.1.call-update) | async-done | bytes 147472 | tf_op jit(solution)/shard_map/psum | solution.py:56
  261.6 1.0 copy.53
  262.7 1.0 fusion.11
  263.7 11.7 %cholesky.51 = f32[128,128]{1,0:T(8,128)S(1)} custom-call(f32[128,128]{1,0:T(8,128)S(1)} %cholesky.124), custom_call_target="Cholesky" | custom-call | tf_op jit(solution)/shard_map/jit(cholesky)/cholesky | solution.py:57
  275.4 9.8 %custom-call.14 = f32[1,128,128]{1,2,0:T(8,128)S(1)} custom-call(f32[1,128,128]{2,1,0:T(8,128)S(1)} %get-tuple-element.60), custom_call_target="InvertDiagBlocksLowerTriangular" | custom-call | tf_op jit(solution)/shard_map/jit(cholesky)/cholesky | solution.py:57
  285.2 0.2 constant_dynamic-update-slice_fusion.1
  285.4 0.2 convolution_subtract_fusion.1
  285.6 5.8 %cholesky.110 = f32[64,64]{1,0:T(8,128)S(1)} custom-call(f32[64,64]{1,0:T(8,128)S(1)} %convolution_subtract_fusion.1), custom_call_target="Cholesky" | custom-call | tf_op jit(solution)/shard_map/jit(cholesky)/cholesky | solution.py:57
  291.5 0.6 compare_reduce_fusion
  292.1 0.6 compare_reduce_fusion.1
  294.1 0.1 fusion.14
  294.2 19.9 %custom-call.15 = f32[2,128,128]{1,2,0:T(8,128)S(1)} custom-call(f32[2,128,128]{2,1,0:T(8,128)S(1)} %pad_maximum_fusion.26), custom_call_target="InvertDiagBlocksLowerTriangular" | custom-call | tf_op jit(solution)/shard_map/triangular_solve | solution.py:60
  314.1 1.5 fusion.13
  315.6 0.9 convolution_subtract_fusion
  316.6 0.8 fusion.18
  317.4 1.6 maximum_multiply_fusion
  319.0 0.8 copy.54
  (24 shorter events, 0.2 us)
Async XLA Ops:
  7.2 254.5 %all-reduce.5.cloned.1.call-start = ((), (), s32[]{:S(2)}) async-start(), calls=%async_computation | async-start | bytes 393216 | tf_op jit(solution)/shard_map/psum | solution.py:56
  8.8 12.5 %collective-permute-start = (f32[3,16,1,512]{3,1,2,0:T(8,128)S(1)}, f32[3,16,1,512]{3,1,2,0:T(8,128)S(1)}, u32[]{:S(2)}, u32[]{:S(2)}) collective-permute-start(f32[3,16,1,512]{3,1,2,0:T(8,128)S(1)} %copy.56), channel_id=1, source_target_pairs={{0,4},{4,8},{8,12},{12,16},{16,20},{20,24},{24,28},{28,0},{1,5},{5... | collective-permute-start | bytes 294920 | tf_op jit(solution)/shard_map/ppermute | solution.py:16
  11.8 5.4 %copy-start = (f32[3,16,32,512]{3,2,1,0:T(8,128)S(1)}, f32[3,16,32,512]{3,2,1,0:T(8,128)}, u32[]{:S(2)}) copy-start(f32[3,16,32,512]{3,2,1,0:T(8,128)} %param.6) | copy-start | bytes 9437188
  11.8 9.5 %collective-permute-start.1 = (f32[3,16,1,512]{3,1,2,0:T(8,128)S(1)}, f32[3,16,1,512]{3,1,2,0:T(8,128)S(1)}, u32[]{:S(2)}, u32[]{:S(2)}) collective-permute-start(f32[3,16,1,512]{3,1,2,0:T(8,128)S(1)} %copy.57), channel_id=1, source_target_pairs={{4,0},{8,4},{12,8},{16,12},{20,16},{24,20},{28,24},{0,28},{5,1},{9... | collective-permute-start | bytes 294920 | tf_op jit(solution)/shard_map/ppermute | solution.py:19
  18.4 0.7 copy-start.4
  18.5 1.4 copy-start.3
  18.5 1.4 copy-start.6
  21.6 6.7 %collective-permute-start.2 = (f32[3,1,34,512]{3,2,1,0:T(8,128)S(1)}, f32[3,1,34,512]{3,2,1,0:T(8,128)S(1)}, u32[]{:S(2)}, u32[]{:S(2)}) collective-permute-start(f32[3,1,34,512]{3,2,1,0:T(8,128)S(1)} %get-tuple-element.38), channel_id=1, source_target_pairs={{1,0},{2,1},{3,2},{0,3},{5,4},{6,5},{7,6},{4,7},{9,8},{10,9},{11,1... | collective-permute-start | bytes 626696 | tf_op jit(solution)/shard_map/ppermute | solution.py:19
  22.3 7.8 %collective-permute-start.3 = (f32[3,1,34,512]{3,2,1,0:T(8,128)S(1)}, f32[3,1,34,512]{3,2,1,0:T(8,128)S(1)}, u32[]{:S(2)}, u32[]{:S(2)}) collective-permute-start(f32[3,1,34,512]{3,2,1,0:T(8,128)S(1)} %get-tuple-element.37), channel_id=1, source_target_pairs={{0,1},{1,2},{2,3},{3,0},{4,5},{5,6},{6,7},{7,4},{8,9},{9,10},{10,1... | collective-permute-start | bytes 626696 | tf_op jit(solution)/shard_map/ppermute | solution.py:16
  36.7 7.4 %collective-permute-start.4 = (f32[3,16,1,512]{3,1,2,0:T(8,128)S(1)}, f32[3,16,1,512]{3,1,2,0:T(8,128)S(1)}, u32[]{:S(2)}, u32[]{:S(2)}) collective-permute-start(f32[3,16,1,512]{3,1,2,0:T(8,128)S(1)} %copy.44), channel_id=1, source_target_pairs={{0,4},{4,8},{8,12},{12,16},{16,20},{20,24},{24,28},{28,0},{1,5},{5... | collective-permute-start | bytes 294920 | tf_op jit(solution)/shard_map/ppermute | solution.py:16
  36.8 7.4 %collective-permute-start.5 = (f32[3,16,1,512]{3,1,2,0:T(8,128)S(1)}, f32[3,16,1,512]{3,1,2,0:T(8,128)S(1)}, u32[]{:S(2)}, u32[]{:S(2)}) collective-permute-start(f32[3,16,1,512]{3,1,2,0:T(8,128)S(1)} %copy.45), channel_id=1, source_target_pairs={{4,0},{8,4},{12,8},{16,12},{20,16},{24,20},{28,24},{0,28},{5,1},{9... | collective-permute-start | bytes 294920 | tf_op jit(solution)/shard_map/ppermute | solution.py:19
  44.4 6.0 %collective-permute-start.6 = (f32[3,1,34,512]{3,2,1,0:T(8,128)S(1)}, f32[3,1,34,512]{3,2,1,0:T(8,128)S(1)}, u32[]{:S(2)}, u32[]{:S(2)}) collective-permute-start(f32[3,1,34,512]{3,2,1,0:T(8,128)S(1)} %get-tuple-element.36), channel_id=1, source_target_pairs={{1,0},{2,1},{3,2},{0,3},{5,4},{6,5},{7,6},{4,7},{9,8},{10,9},{11,1... | collective-permute-start | bytes 626696 | tf_op jit(solution)/shard_map/ppermute | solution.py:19
  44.5 7.8 %collective-permute-start.7 = (f32[3,1,34,512]{3,2,1,0:T(8,128)S(1)}, f32[3,1,34,512]{3,2,1,0:T(8,128)S(1)}, u32[]{:S(2)}, u32[]{:S(2)}) collective-permute-start(f32[3,1,34,512]{3,2,1,0:T(8,128)S(1)} %get-tuple-element.35), channel_id=1, source_target_pairs={{0,1},{1,2},{2,3},{3,0},{4,5},{5,6},{6,7},{7,4},{8,9},{9,10},{10,1... | collective-permute-start | bytes 626696 | tf_op jit(solution)/shard_map/ppermute | solution.py:16
  57.5 64.6 %copy-start.1 = (f32[3,16,32,512]{3,2,1,0:T(8,128)}, f32[3,16,32,512]{3,2,1,0:T(8,128)S(1)}, u32[]{:S(2)}) copy-start(f32[3,16,32,512]{3,2,1,0:T(8,128)S(1)} %multiply_add_fusion) | copy-start | bytes 9437188
  57.5 75.7 %copy-start.5 = (s32[64]{0:T(128)S(1)}, s32[64]{0:T(128)}, u32[]{:S(2)}) copy-start(s32[64]{0:T(128)} %param.11) | copy-start | bytes 772
  122.1 12.8 %copy-start.2 = (f32[128,3072]{1,0:T(8,128)S(1)}, f32[128,3072]{1,0:T(8,128)}, u32[]{:S(2)}) copy-start(f32[128,3072]{1,0:T(8,128)} %broadcast_multiply_fusion) | copy-start | bytes 4718596
Sparse Core Ops, SparseCore 0:
  137.7 123.8 all-reduce.4
where the time goes:
time: 327 us
  waiting for transfers between devices  141 us (43%)
  local copies, waits for them, and re-layouts  83.6 us (26%)
  other arithmetic  66.3 us (20%)
  between operations  15.7 us (5%)
  starting transfers between devices  12.2 us (4%)
  matrix products  8.02 us (2%)
    psum x1, waiting for transfers between devices, per_device(): gram = lax.psum(local_gram, ('tile', 'grp'))  124 us
    add x1, local copies, waits for them, and re-layouts, advance(): return center + time_step * (viscosity * laplace - carried)  64.5 us
    another operation x7, other arithmetic, per_device(): lower = jnp.linalg.cholesky(gram)  28.7 us
    another operation x5, other arithmetic, per_device(): lax.linalg.triangular_solve(lower, combined, left_side=True, lower=True)  20 us
    ppermute x4, waiting for transfers between devices, with_halo(): lax.ppermute(lax.slice_in_dim(block, 0, width, axis=dim), axis, backward)  11 us
    gather x1, local copies, waits for them, and re-layouts, per_device(): sample = jnp.take(flat_cells, slab_ids, axis=1).reshape(1, -1)  10.6 us
    add x2, other arithmetic, advance(): return center + time_step * (viscosity * laplace - carried)  10.4 us
    ppermute x4, starting transfers between devices, with_halo(): lax.ppermute(lax.slice_in_dim(block, 0, width, axis=dim), axis, backward)  8.62 us
  transfers between devices with their start and end apart: 9, of which 6 were waited for; matrix products, arithmetic and copies ran while one was open for 2% of the time, Pallas kernels for 0%

commit v1 on v0

v1 whole, which is shorter than its diff:
```python
import functools
import math

import jax
import jax.numpy as jnp
from jax import lax
from jax.experimental import pallas as pl
from jax.experimental.pallas import tpu as pltpu
from jax.sharding import PartitionSpec as P

time_step = 0.1
viscosity = 0.5
HIGHEST = lax.Precision.HIGHEST
LANES = 128
GROUP = 16


def in_hbm(array):
    return pltpu.with_memory_space_constraint(array, pltpu.HBM)


def in_vmem(array):
    return pltpu.with_memory_space_constraint(array, pltpu.VMEM)


def dot(a, b, ca=1, cb=0):
    return lax.dot_general(
        a, b, (((ca,), (cb,)), ((), ())), precision=HIGHEST, preferred_element_type=jnp.float32
    )


def faces_kernel(velocity_ref, xlow_ref, xhigh_ref, ylow_ref, yhigh_ref, low, high, sems):
    nx, ny = velocity_ref.shape[1:3]
    copies = [
        pltpu.make_async_copy(velocity_ref.at[:, 0:2], xlow_ref, sems.at[0]),
        pltpu.make_async_copy(velocity_ref.at[:, nx - 2 : nx], xhigh_ref, sems.at[1]),
        pltpu.make_async_copy(velocity_ref.at[:, :, 0:8, :], low, sems.at[2]),
        pltpu.make_async_copy(velocity_ref.at[:, :, ny - 8 : ny, :], high, sems.at[3]),
    ]
    for copy in copies:
        copy.start()
    copies[2].wait()
    ylow_ref[...] = low[:, :, 0:2, :]
    copies[3].wait()
    yhigh_ref[...] = high[:, :, 6:8, :]
    copies[0].wait()
    copies[1].wait()


def faces(velocity):
    comps, nx, ny, nz = velocity.shape
    hbm = pl.BlockSpec(memory_space=pl.ANY)
    vmem = pl.BlockSpec(memory_space=pltpu.VMEM)
    across_x = pltpu.VMEM((comps, 2, ny, nz), jnp.float32)
    across_y = pltpu.VMEM((comps, nx, 2, nz), jnp.float32)
    return pl.pallas_call(
        faces_kernel,
        in_specs=[hbm],
        out_specs=[vmem, vmem, vmem, vmem],
        out_shape=[across_x, across_x, across_y, across_y],
        scratch_shapes=[
            pltpu.VMEM((comps, nx, 8, nz), jnp.float32),
            pltpu.VMEM((comps, nx, 8, nz), jnp.float32),
            pltpu.SemaphoreType.DMA((4,)),
        ],
        compiler_params=pltpu.CompilerParams(vmem_limit_bytes=16 * 2**20),
        name="faces",
    )(in_hbm(velocity))


def corners_kernel(ylo_ref, yhi_ref, gram_ref, low_ref, high_ref):
    nx = ylo_ref.shape[1]
    for c in range(ylo_ref.shape[0]):
        low_ref[c, 0:1, :] = ylo_ref[c, 0, 1:2, :]
        low_ref[c, 1:2, :] = yhi_ref[c, 0, 0:1, :]
        high_ref[c, 0:1, :] = ylo_ref[c, nx - 1, 1:2, :]
        high_ref[c, 1:2, :] = yhi_ref[c, nx - 1, 0:1, :]


def corners(ylo, yhi, gram):
    comps, _, _, nz = ylo.shape
    vmem = pl.BlockSpec(memory_space=pltpu.VMEM)
    return pl.pallas_call(
        corners_kernel,
        in_specs=[vmem, vmem, pl.BlockSpec(memory_space=pl.ANY)],
        out_specs=[vmem, vmem],
        out_shape=[pltpu.VMEM((comps, 2, nz), jnp.float32)] * 2,
        compiler_params=pltpu.CompilerParams(vmem_limit_bytes=4 * 2**20),
        name="corners",
    )(in_vmem(ylo), in_vmem(yhi), in_vmem(gram))


def gram_kernel(steps_ref, w_ref, modes_ref, history_ref, gram_ref, snaps_ref):
    k = modes_ref.shape[0]
    count = snaps_ref.shape[0]
    last = count - 1
    for j in range(count):
        step = steps_ref[j]
        source = jnp.minimum(step, last - 1)
        row = history_ref[pl.ds(source, 1), :]
        snaps_ref[j : j + 1, :] = jnp.where(step == last, 0.0, row)
    modes = modes_ref[...]
    snaps = snaps_ref[...]
    wide = jnp.broadcast_to(w_ref[...], (k, k))
    tall = jnp.transpose(wide)
    gram_ref[0:k, 0:k] = dot(modes, modes, 1, 1) * wide * tall
    gram_ref[0:k, k:] = dot(modes, snaps, 1, 1) * tall[:, 0:count]
    gram_ref[k:, 0:k] = jnp.zeros((count, k), jnp.float32)
    gram_ref[k:, k:] = dot(snaps, snaps, 1, 1)


def early_gram(steps, weights, modes, history):
    k, width = modes.shape
    count = steps.shape[0]
    total = k + count
    return pl.pallas_call(
        gram_kernel,
        in_specs=[pl.BlockSpec(memory_space=pltpu.SMEM)] + [pl.BlockSpec(memory_space=pltpu.VMEM)] * 3,
        out_specs=[pl.BlockSpec(memory_space=pltpu.VMEM)] * 2,
        out_shape=[
            pltpu.VMEM((total, total), jnp.float32),
            pltpu.VMEM((count, width), jnp.float32),
        ],
        compiler_params=pltpu.CompilerParams(vmem_limit_bytes=24 * 2**20),
        cost_estimate=pl.CostEstimate(
            flops=12 * total * total * width, bytes_accessed=12 * total * width, transcendentals=0
        ),
        name="early_gram",
    )(in_vmem(steps), in_vmem(weights), in_vmem(modes), in_vmem(history))


def substep(src, dst, rows, src_x, dst_x, tiles, store):
    diff = time_step * viscosity
    adv = 0.5 * time_step
    for t in range(tiles):
        lo, hi = 8 * t, 8 * t + 8
        mid = [src[c, src_x, lo:hi, :] for c in range(3)]
        ax = [diff - adv * v for v in mid]
        bx = [diff + adv * v for v in mid]
        for c in range(3):
            v = mid[c]
            if lo == 0:
                y_minus = jnp.concatenate([src[c, src_x, rows - 1 : rows, :], src[c, src_x, 0:7, :]], axis=0)
            else:
                y_minus = src[c, src_x, lo - 1 : hi - 1, :]
            if hi == rows:
                y_plus = jnp.concatenate([src[c, src_x, lo + 1 : hi, :], src[c, src_x, 0:1, :]], axis=0)
            else:
                y_plus = src[c, src_x, lo + 1 : hi + 1, :]
            x_plus = src[c, src_x + 1, lo:hi, :]
            x_minus = src[c, src_x - 1, lo:hi, :]
            z_plus = pltpu.roll(v, v.shape[1] - 1, 1)
            z_minus = pltpu.roll(v, 1, 1)
            out = (1.0 - 6.0 * diff) * v
            out = out + ax[0] * x_plus + bx[0] * x_minus
            out = out + ax[1] * y_plus + bx[1] * y_minus
            out = out + ax[2] * z_plus + bx[2] * z_minus
            store(c, dst_x, lo, hi, out)


def field_kernel(
    ids_ref, steps_ref, core_ref, w_ref, velocity_ref, xlo_ref, xhi_ref, ylo_ref, yhi_ref, clo_ref, chi_ref,
    modes_ref, snaps_ref, gram_ref,
    advanced_ref, snaps_out_ref, mine_ref, other_ref,
    p0, p1, u2, flat, picked, packed, sem, out_sems,
):
    comps, nx, ny, nz = u2.shape
    rows = ny + 8
    inner = pltpu.make_async_copy(velocity_ref, p0.at[:, 2 : nx + 2, 0:ny, :], sem)
    inner.start()
    p0[:, 0:2, 0:ny, :] = xlo_ref[...]
    p0[:, nx + 2 : nx + 4, 0:ny, :] = xhi_ref[...]
    for c in range(comps):
        for x in range(nx):
            p0[c, x + 2, ny : ny + 2, :] = yhi_ref[c, x]
            p0[c, x + 2, rows - 2 : rows, :] = ylo_ref[c, x]
        p0[c, 1, rows - 1 : rows, :] = clo_ref[c, 0:1, :]
        p0[c, 1, ny : ny + 1, :] = clo_ref[c, 1:2, :]
        p0[c, nx + 2, rows - 1 : rows, :] = chi_ref[c, 0:1, :]
        p0[c, nx + 2, ny : ny + 1, :] = chi_ref[c, 1:2, :]
    inner.wait()

    def keep1(c, x, lo, hi, out):
        p1[c, x, lo:hi, :] = out

    tiles = nz // LANES

    def keep2(c, x, lo, hi, out):
        u2[c, x, lo:hi, :] = out
        for k in range(tiles):
            at = pl.multiple_of((k * nx + x) * ny + lo, 8)
            flat[c, pl.ds(at, 8), :] = out[:, k * LANES : (k + 1) * LANES]

    @pl.loop(0, nx + 2)
    def _(x):
        substep(p0, p1, rows, x + 1, x, rows // 8, keep1)

    def out_copy(x):
        return pltpu.make_async_copy(u2.at[:, x], advanced_ref.at[:, x], out_sems.at[x])

    @pl.loop(0, nx)
    def _(x):
        substep(p1, u2, rows, x + 1, x, ny // 8, keep2)
        out_copy(x).start()

    count = ids_ref.shape[0]
    lane = lax.broadcasted_iota(jnp.int32, (1, LANES), 1)

    @pl.loop(0, count // 8)
    def _(i):
        for k in range(8):
            cell = ids_ref[i * 8 + k]
            line = lax.shift_right_logical(cell, int(math.log2(LANES)))
            at = (line & (tiles - 1)) * (nx * ny) + lax.shift_right_logical(line, int(math.log2(tiles)))
            hit = lane == (cell & (LANES - 1))
            for c in range(comps):
                row = flat[c, pl.ds(at, 1), :]
                picked[c, pl.ds(i * 8 + k, 1), :] = jnp.where(hit, row, 0.0)

    ones = jnp.ones((8, LANES), jnp.float32)
    parts = [dot(ones, picked[c], 1, 1)[0:1] for c in range(comps)]
    sample = jnp.concatenate(parts, axis=1)

    snaps_count = steps_ref.shape[0]
    place = jnp.int32(0)
    for j in range(snaps_count):
        place = jnp.where(steps_ref[j] == snaps_count - 1, j, place)
    snaps_out_ref[...] = snaps_ref[...]
    snaps_out_ref[pl.ds(place, 1), :] = sample

    k = modes_ref.shape[0]
    half = snaps_count
    tall = jnp.transpose(jnp.broadcast_to(w_ref[...], (k, k)))
    with_modes = jnp.sum(modes_ref[...] * sample, axis=1, keepdims=True) * tall
    with_snaps = jnp.sum(snaps_out_ref[...] * sample, axis=1, keepdims=True)
    col = lax.broadcasted_iota(jnp.int32, (half, half), 1)
    row = lax.broadcasted_iota(jnp.int32, (half, half), 0)
    col_k = lax.broadcasted_iota(jnp.int32, (k, half), 1)
    cross = jnp.where(col_k == place, with_modes[:, 0:half], gram_ref[0:k, k:])
    splat = jnp.broadcast_to(with_snaps, (half, LANES))[:, 0:half]
    low = jnp.where(col == place, splat, gram_ref[k:, k:])
    low = jnp.where(row == place, jnp.transpose(splat), low)
    packed[0:half, 0:half] = gram_ref[0:half, half:k]
    packed[0:half, half:k] = cross[0:half]
    packed[half:k, 0:half] = gram_ref[half:k, half:k]
    packed[half:k, half:k] = cross[half:k]
    packed[k:, 0:half] = gram_ref[0:half, 0:half]
    packed[k:, half:k] = low
    part = mine_ref.shape[0]
    core = core_ref[0]
    mine_ref[...] = packed[pl.ds(pl.multiple_of(core * part, 8), part), :]
    other_ref[...] = packed[pl.ds(pl.multiple_of((1 - core) * part, 8), part), :]

    @pl.loop(0, nx)
    def _(x):
        out_copy(x).wait()


def field_call(ids, steps, core, weights, velocity, xlo, xhi, ylo, yhi, clo, chi, modes, snaps, gram):
    comps, nx, ny, nz = velocity.shape
    total = gram.shape[0]
    part = total // 2
    smem = pl.BlockSpec(memory_space=pltpu.SMEM)
    vmem = pl.BlockSpec(memory_space=pltpu.VMEM)
    hbm = pl.BlockSpec(memory_space=pl.ANY)
    return pl.pallas_call(
        field_kernel,
        in_specs=[smem, smem, smem, vmem, hbm] + [vmem] * 9,
        out_specs=[hbm, vmem, vmem, vmem],
        out_shape=[
            pltpu.HBM(velocity.shape, jnp.float32),
            pltpu.VMEM(snaps.shape, jnp.float32),
            pltpu.VMEM((part, LANES), jnp.float32),
            pltpu.VMEM((part, LANES), jnp.float32),
        ],
        scratch_shapes=[
            pltpu.VMEM((comps, nx + 4, ny + 8, nz), jnp.float32),
            pltpu.VMEM((comps, nx + 2, ny + 8, nz), jnp.float32),
            pltpu.VMEM((comps, nx, ny, nz), jnp.float32),
            pltpu.VMEM((comps, nx * ny * nz // LANES, LANES), jnp.float32),
            pltpu.VMEM((comps, ids.shape[0], LANES), jnp.float32),
            pltpu.VMEM((total, LANES), jnp.float32),
            pltpu.SemaphoreType.DMA,
            pltpu.SemaphoreType.DMA((nx,)),
        ],
        compiler_params=pltpu.CompilerParams(vmem_limit_bytes=26 * 2**20),
        cost_estimate=pl.CostEstimate(
            flops=60 * velocity.size, bytes_accessed=8 * velocity.size, transcendentals=0
        ),
        name="substeps_and_sample",
    )(
        in_vmem(ids), in_vmem(steps), core, in_vmem(weights), in_hbm(velocity), in_vmem(xlo), in_vmem(xhi),
        in_vmem(ylo), in_vmem(yhi), in_vmem(clo), in_vmem(chi), in_vmem(modes), in_vmem(snaps), in_vmem(gram),
    )


def eliminate(block):
    n = block.shape[0]
    eye = (
        lax.broadcasted_iota(jnp.int32, (n, n), 0) == lax.broadcasted_iota(jnp.int32, (n, n), 1)
    ).astype(jnp.float32)
    table = jnp.concatenate([block, eye], axis=1)
    width = table.shape[1]
    done = []
    base = 0
    for j in range(0, n, GROUP):
        first = (j // 8) * 8
        if first > base:
            done.append(table[: first - base])
            table = table[first - base :]
            base = first
        h = n - base
        rows = lax.broadcasted_iota(jnp.int32, (h, width), 0) + base
        spread = [jnp.broadcast_to(table[:, j + k : j + k + 1], (h, width)) for k in range(GROUP)]
        for k in range(GROUP):
            i = j + k - base
            ratio = jnp.where(rows > j + k, spread[k] * (1.0 / spread[k][i : i + 1, :]), 0.0)
            for l in range(k + 1, GROUP):
                spread[l] = spread[l] - ratio * spread[l][i : i + 1, :]
            table = table - ratio * table[i : i + 1, :]
    done.append(table)
    table = jnp.concatenate(done, axis=0)
    pivots = jnp.sum(table[:, :n] * eye, axis=1, keepdims=True)
    table = table * lax.rsqrt(pivots)
    upper = lax.broadcasted_iota(jnp.int32, (n, n), 1) >= lax.broadcasted_iota(jnp.int32, (n, n), 0)
    return jnp.where(upper, table[:, :n], 0.0), table[:, n:]


def basis_kernel(root, core_ref, w_ref, mine_ref, other_ref, modes_ref, snaps_ref, factor_ref, basis_ref, packed, inverse):
    total = factor_ref.shape[0]
    half = total // 3
    two = 2 * half

    @pl.when(pl.program_id(0) == 0)
    def _():
        part = mine_ref.shape[0]
        core = core_ref[0]
        packed[pl.ds(pl.multiple_of(core * part, 8), part), :] = mine_ref[...]
        packed[pl.ds(pl.multiple_of((1 - core) * part, 8), part), :] = other_ref[...]
        a00 = packed[two:, 0:half]
        a22 = packed[two:, half:two]
        u00, m00 = eliminate(a00)
        w0 = dot(m00, packed[0:half, :])
        w01, w02 = w0[:, 0:half], w0[:, half:two]
        a1 = packed[half:two, :] - dot(w01, w0, 0, 0)
        u11, m11 = eliminate(a1[:, 0:half])
        w12 = dot(m11, a1[:, half:two])
        a22 = a22 - dot(w02, w02, 0, 0) - dot(w12, w12, 0, 0)
        m10 = -dot(m11, dot(w01, m00, 0, 0))
        u22, m22 = eliminate(a22)
        m20 = -dot(m22, dot(w02, m00, 0, 0) + dot(w12, m10, 0, 0))
        m21 = -dot(m22, dot(w12, m11, 0, 0))
        zero = jnp.zeros((half, half), jnp.float32)
        scale = 1.0 / root
        factor_ref[0:half, 0:half] = u00 * scale
        factor_ref[0:half, half:two] = w01 * scale
        factor_ref[0:half, two:] = w02 * scale
        factor_ref[half:two, 0:half] = zero
        factor_ref[half:two, half:two] = u11 * scale
        factor_ref[half:two, two:] = w12 * scale
        factor_ref[two:, 0:half] = zero
        factor_ref[two:, half:two] = zero
        factor_ref[two:, two:] = u22 * scale
        wide = w_ref[...] * root
        inverse[0:half, 0:two] = jnp.concatenate([m00, zero], axis=1) * wide
        inverse[half:two, 0:two] = jnp.concatenate([m10, m11], axis=1) * wide
        inverse[two:, 0:two] = jnp.concatenate([m20, m21], axis=1) * wide
        inverse[0:half, two:total] = zero
        inverse[half:two, two:total] = zero
        inverse[two:, two:total] = m22 * root

    rows = jnp.concatenate([modes_ref[...], snaps_ref[...]], axis=0)
    basis_ref[...] = dot(inverse[:, 0:total], rows)


def basis_call(root, core, weights, mine, other, modes, snaps):
    k, width = modes.shape
    count = snaps.shape[0]
    total = k + count
    chunk = 512
    smem = pl.BlockSpec(memory_space=pltpu.SMEM)
    whole = lambda shape: pl.BlockSpec(shape, lambda i: (0, 0))
    return pl.pallas_call(
        functools.partial(basis_kernel, root),
        grid=(width // chunk,),
        in_specs=[
            smem,
            whole(weights.shape),
            whole(mine.shape),
            whole(other.shape),
            pl.BlockSpec((k, chunk), lambda i: (0, i)),
            pl.BlockSpec((count, chunk), lambda i: (0, i)),
        ],
        out_specs=[whole((total, total)), pl.BlockSpec((total, chunk), lambda i: (0, i))],
        out_shape=[
            jax.ShapeDtypeStruct((total, total), jnp.float32),
            jax.ShapeDtypeStruct((total, width), jnp.float32),
        ],
        scratch_shapes=[
            pltpu.VMEM((total, LANES), jnp.float32),
            pltpu.VMEM((total, 2 * LANES), jnp.float32),
        ],
        compiler_params=pltpu.CompilerParams(vmem_limit_bytes=24 * 2**20),
        cost_estimate=pl.CostEstimate(
            flops=12 * total * total * width, bytes_accessed=8 * total * width, transcendentals=0
        ),
        name="factor_and_basis",
    )(core, in_vmem(weights), in_vmem(mine), in_vmem(other), in_vmem(modes), in_vmem(snaps))


def ring(axis):
    count = lax.axis_size(axis)
    forward = [(i, (i + 1) % count) for i in range(count)]
    backward = [(i, (i - 1) % count) for i in range(count)]
    return forward, backward


def swap(axis, bit):
    return [(i, i ^ bit) for i in range(lax.axis_size(axis))]


def per_device(velocity, modes, mode_weights, history, slab_ids, snap_steps):
    xlow, xhigh, ylow, yhigh = faces(velocity)
    up, down = ring("grp")
    xlo = lax.ppermute(xhigh, "grp", up)
    xhi = lax.ppermute(xlow, "grp", down)
    up_y, down_y = ring("tile")
    ylo = lax.ppermute(yhigh, "tile", up_y)
    yhi = lax.ppermute(ylow, "tile", down_y)

    weights = mode_weights.reshape(1, -1)
    gram, snaps = early_gram(snap_steps, weights, modes, history)

    clow, chigh = corners(ylo, yhi, gram)
    clo = lax.ppermute(chigh, "grp", up)
    chi = lax.ppermute(clow, "grp", down)

    core = (lax.axis_index("grp") & 1).astype(jnp.int32).reshape(1)
    advanced, snaps, mine, other = field_call(
        slab_ids, snap_steps, core, weights, velocity, xlo, xhi, ylo, yhi, clo, chi, modes, snaps, gram
    )

    mine = mine + lax.ppermute(other, "grp", swap("grp", 1))
    for axis, first in (("grp", 2), ("tile", 1)):
        bit = first
        while bit < lax.axis_size(axis):
            mine = mine + lax.ppermute(mine, axis, swap(axis, bit))
            bit *= 2
    other = lax.ppermute(mine, "grp", swap("grp", 1))

    total_rows = modes.shape[1] * lax.axis_size("tile") * lax.axis_size("grp")
    root = math.sqrt(total_rows)
    factor, basis = basis_call(root, core, weights, mine, other, modes, snaps)
    return (advanced, basis, factor)


def solution(mesh):
    return jax.shard_map(
        per_device,
        mesh=mesh,
        in_specs=(
            P(None, "grp", "tile", None),
            P(None, ("tile", "grp")),
            P(),
            P(None, ("tile", "grp")),
            P(("tile", "grp")),
            P(),
        ),
        out_specs=(P(None, "grp", "tile", None), P(None, ("tile", "grp")), P()),
        check_vma=False,
    )
```

time: 327 us -> 67.9 us (0.21)
  waiting for transfers between devices: 141 us -> 18.5 us
  local copies, waits for them, and re-layouts: 83.6 us -> 0.02 us
  other arithmetic: 66.3 us -> 0.04 us
  Pallas kernels: 0 us -> 32.2 us
  between operations: 15.7 us -> 0.73 us
  matrix products: 8.02 us -> 0 us
  starting transfers between devices: 12.2 us -> 16.3 us
    psum x1 -> x0, waiting for transfers between devices: 124 us -> none  [per_device(): gram = lax.psum(local_gram, ('tile', 'grp'))]
    add x1 -> x0, local copies, waits for them, and re-layouts: 64.5 us -> none  [advance(): return center + time_step * (viscosity * laplace - carried)]
    another operation x12 -> x0, other arithmetic: 48.7 us -> none  [the longest x7 28.7 us: per_device(): lower = jnp.linalg.cholesky(gram)]
    pallas_call x0 -> x5, Pallas kernels: none -> 32.2 us  [the longest x1 14.7 us: field_call(): pl.pallas_call(field_kernel, in_specs=[smem, smem, smem, vmem, hbm] + [vm...]
    gather x1 -> x0, local copies, waits for them, and re-layouts: 10.6 us -> none  [per_device(): sample = jnp.take(flat_cells, slab_ids, axis=1).reshape(1, -1)]
    add x2 -> x5, other arithmetic: 10.4 us -> 0.04 us  [the longest x4 0.03 us: per_device(): mine = mine + lax.ppermute(mine, axis, swap(axis, bit))]
    mul x4 -> x0, other arithmetic: 5.82 us -> none  [the longest x2 2.85 us: advance(): center[0:1] * (0.5 * (x_plus - x_minus))]
    slice x8 -> x0, local copies, waits for them, and re-layouts: 4.83 us -> none  [the longest x4 3.07 us: advance(): z_plus = jnp.roll(center, -1, axis=3)]
  transfers between devices with their start and end apart: 9 -> 12, of which waited for: 6 -> 9; matrix products, arithmetic and copies ran while one was open for 2% -> 0% of each run, Pallas kernels for 0% -> 6%
where the time goes in v1:
time: 67.9 us; the launch traced here: 67.8 us
  Pallas kernels  32.2 us (47%)
  waiting for transfers between devices  18.5 us (27%)
  starting transfers between devices  16.3 us (24%)
  between operations  0.73 us (1%)
    pallas_call x1, Pallas kernels, field_call(): pl.pallas_call(field_kernel, in_specs=[smem, smem, smem, vmem, hbm] + [vm...  14.7 us
    ppermute x4, waiting for transfers between devices, per_device(): mine = mine + lax.ppermute(mine, axis, swap(axis, bit))  11.5 us
    pallas_call x1, Pallas kernels, basis_call(): pl.pallas_call(functools.partial(basis_kernel, root), grid=(width // chun...  10.7 us
    ppermute x4, starting transfers between devices, per_device(): mine = mine + lax.ppermute(mine, axis, swap(axis, bit))  5.92 us
    pallas_call x1, Pallas kernels, early_gram(): pl.pallas_call(gram_kernel, in_specs=[pl.BlockSpec(memory_space=pltpu.SME...  4.12 us
    ppermute x1, starting transfers between devices, per_device(): yhi = lax.ppermute(ylow, 'tile', down_y)  3.04 us
    pallas_call x1, Pallas kernels, faces(): pl.pallas_call(faces_kernel, in_specs=[hbm], out_specs=[vmem, vmem, vmem,...  2.71 us
    ppermute x1, starting transfers between devices, per_device(): ylo = lax.ppermute(yhigh, 'tile', up_y)  2.27 us
  transfers between devices with their start and end apart: 12, of which 9 were waited for; matrix products, arithmetic and copies ran while one was open for 0% of the time, Pallas kernels for 6%

profile of v1, /device:TPU:0, one launch (start us, length us, event | category | flops | bytes accessed | tf_op | source)
XLA Modules:
  0.0 67.8 jit_solution(2486731850173398769)
XLA Ops:
  0.6 0.0 copy-start
  0.6 0.0 copy-start.2
  0.7 0.0 copy-start.4
  0.7 0.0 copy-start.3
  0.7 2.7 %faces.1 = (f32[3,2,32,512]{3,2,1,0:T(8,128)}, f32[3,2,32,512]{3,2,1,0:T(8,128)}, f32[3,16,2,512]{3,2,1,0:T(2,128)S(1)}, f32[3,16,2,512]{3,2,1,0:T(2,128)S(1)}) custom-call(f32[3,16,32,512]{3,2,1,0:T(8,128)} %velocity_ref.3), custom_call_target="tpu_custom_call" | custom-call | tf_op jit(solution)/shard_map/faces/pallas_call | solution.py:56
  3.4 0.0 copy-start.1
  3.4 0.5 collective-permute-start
  3.9 2.0 %collective-permute-start.1 = (f32[3,2,32,512]{3,2,1,0:T(8,128)}, f32[3,2,32,512]{3,2,1,0:T(8,128)}, u32[]{:S(2)}, u32[]{:S(2)}) collective-permute-start(f32[3,2,32,512]{3,2,1,0:T(8,128)} %get-tuple-element.18), channel_id=1, source_target_pairs={{0,3},{1,0},{2,1},{3,2},{4,7},{5,4},{6,5},{7,6},{8,11},{9,8},{10,9... | collective-permute-start | bytes 1179656 | tf_op jit(solution)/shard_map/ppermute | solution.py:426
  5.9 2.3 %collective-permute-start.2 = (f32[3,16,2,512]{3,2,1,0:T(2,128)S(1)}, f32[3,16,2,512]{3,2,1,0:T(2,128)S(1)}, u32[]{:S(2)}, u32[]{:S(2)}) collective-permute-start(f32[3,16,2,512]{3,2,1,0:T(2,128)S(1)} %get-tuple-element.19), channel_id=1, source_target_pairs={{0,4},{4,8},{8,12},{12,16},{16,20},{20,24},{24,28},{28,0},{1,5},{5... | collective-permute-start | bytes 589832 | tf_op jit(solution)/shard_map/ppermute | solution.py:428
  8.2 3.0 %collective-permute-start.3 = (f32[3,16,2,512]{3,2,1,0:T(2,128)S(1)}, f32[3,16,2,512]{3,2,1,0:T(2,128)S(1)}, u32[]{:S(2)}, u32[]{:S(2)}) collective-permute-start(f32[3,16,2,512]{3,2,1,0:T(2,128)S(1)} %get-tuple-element.20), channel_id=1, source_target_pairs={{0,28},{4,0},{8,4},{12,8},{16,12},{20,16},{24,20},{28,24},{1,29},{... | collective-permute-start | bytes 589832 | tf_op jit(solution)/shard_map/ppermute | solution.py:429
  11.2 0.0 copy-done
  11.2 0.0 copy-done.2
  11.2 0.0 copy-done.4
  11.2 0.0 copy-done.3
  11.2 4.1 %early_gram.1 = (f32[192,192]{1,0:T(8,128)S(1)}, f32[64,3072]{1,0:T(8,128)S(1)}) custom-call(s32[64]{0:T(128)S(1)} %copy-done.2, f32[1,128]{1,0:T(1,128)S(1)} %bitcast.2, f32[128,3072]{1,0:T(8,128)S(1)} %copy-done, f32[63,3072]{1,0:T(8,128)S(1)} %copy-done.4), custom_call_target="tpu_custom_call" | custom-call | flops 1358954496 | bytes 7077888 | tf_op jit(solution)/shard_map/early_gram/pallas_call | solution.py:116
  15.3 1.2 %collective-permute-done.2.ylo_ref = f32[3,16,2,512]{3,2,1,0:T(2,128)S(1)} collective-permute-done((f32[3,16,2,512]{3,2,1,0:T(2,128)S(1)}, f32[3,16,2,512]{3,2,1,0:T(2,128)S(1)}, u32[]{:S(2)}, u32[]{:S(2)}) %collective-permute-start.2) | collective-permute-done | bytes 196640 | tf_op jit(solution)/shard_map/ppermute | solution.py:428
  16.6 2.2 %collective-permute-done.3.yhi_ref = f32[3,16,2,512]{3,2,1,0:T(2,128)S(1)} collective-permute-done((f32[3,16,2,512]{3,2,1,0:T(2,128)S(1)}, f32[3,16,2,512]{3,2,1,0:T(2,128)S(1)}, u32[]{:S(2)}, u32[]{:S(2)}) %collective-permute-start.3) | collective-permute-done | bytes 196640 | tf_op jit(solution)/shard_map/ppermute | solution.py:429
  18.8 0.1 collective-permute-start.4
  18.8 1.7 %collective-permute-start.5 = (f32[3,2,512]{2,1,0:T(2,128)S(1)}, f32[3,2,512]{2,1,0:T(2,128)S(1)}, u32[]{:S(2)}, u32[]{:S(2)}) collective-permute-start(f32[3,2,512]{2,1,0:T(2,128)S(1)} %get-tuple-element.23), channel_id=1, source_target_pairs={{0,3},{1,0},{2,1},{3,2},{4,7},{5,4},{6,5},{7,6},{8,11},{9,8},{10,9... | collective-permute-start | bytes 36872 | tf_op jit(solution)/shard_map/ppermute | solution.py:436
  20.6 1.4 %collective-permute-done.4.clo_ref = f32[3,2,512]{2,1,0:T(2,128)S(1)} collective-permute-done((f32[3,2,512]{2,1,0:T(2,128)S(1)}, f32[3,2,512]{2,1,0:T(2,128)S(1)}, u32[]{:S(2)}, u32[]{:S(2)}) %collective-permute-start.4) | collective-permute-done | bytes 12320 | tf_op jit(solution)/shard_map/ppermute | solution.py:435
  22.0 0.0 collective-permute-done.5.chi_ref
  22.0 0.0 collective-permute-done.xlo_ref
  22.0 0.0 collective-permute-done.1.xhi_ref
  22.0 0.0 copy-done.1
  22.0 14.7 %substeps_and_sample.1 = (f32[3,16,32,512]{3,2,1,0:T(8,128)}, f32[64,3072]{1,0:T(8,128)S(1)}, f32[96,128]{1,0:T(8,128)S(1)}, f32[96,128]{1,0:T(8,128)S(1)}) custom-call(s32[1024]{0:T(1024)S(1)} %copy-done.1, s32[64]{0:T(128)S(1)} %copy-done.2, s32[1]{0:T(128)} %bitcast.core_ref, f32[1,128]{1,0:T(1,128)S(1)} %bitcast.3, f32[3,16,32,512]{3,2,1,0:T(8,128)} %velocity_ref.3, ...), custom_call_target="tpu_custom_call" | custom-call | flops 47185920 | bytes 6291456 | tf_op jit(solution)/shard_map/substeps_and_sample/pallas_call | solution.py:266
  36.7 0.7 %collective-permute-start.6 = (f32[96,128]{1,0:T(8,128)S(1)}, f32[96,128]{1,0:T(8,128)S(1)}, u32[]{:S(2)}, u32[]{:S(2)}) collective-permute-start(f32[96,128]{1,0:T(8,128)S(1)} %get-tuple-element.27), channel_id=1, source_target_pairs={{0,1},{1,0},{2,3},{3,2},{4,5},{5,4},{6,7},{7,6},{8,9},{9,8},{10,11... | collective-permute-start | bytes 147464 | tf_op jit(solution)/shard_map/ppermute | solution.py:443
  37.4 0.9 %collective-permute-done.6 = f32[96,128]{1,0:T(8,128)S(1)} collective-permute-done((f32[96,128]{1,0:T(8,128)S(1)}, f32[96,128]{1,0:T(8,128)S(1)}, u32[]{:S(2)}, u32[]{:S(2)}) %collective-permute-start.6) | collective-permute-done | bytes 49184 | tf_op jit(solution)/shard_map/ppermute | solution.py:443
  38.2 1.5 %collective-permute-start.7 = (f32[96,128]{1,0:T(8,128)S(1)}, f32[96,128]{1,0:T(8,128)S(1)}, u32[]{:S(2)}, u32[]{:S(2)}) collective-permute-start(f32[96,128]{1,0:T(8,128)S(1)} %add.15), channel_id=1, source_target_pairs={{0,2},{1,3},{2,0},{3,1},{4,6},{5,7},{6,4},{7,5},{8,10},{9,11},{10,... | collective-permute-start | bytes 147464 | tf_op jit(solution)/shard_map/ppermute | solution.py:447
  39.7 2.6 %collective-permute-done.7 = f32[96,128]{1,0:T(8,128)S(1)} collective-permute-done((f32[96,128]{1,0:T(8,128)S(1)}, f32[96,128]{1,0:T(8,128)S(1)}, u32[]{:S(2)}, u32[]{:S(2)}) %collective-permute-start.7) | collective-permute-done | bytes 49184 | tf_op jit(solution)/shard_map/ppermute | solution.py:447
  42.3 0.3 collective-permute-start.8
  42.7 3.8 %collective-permute-done.8 = f32[96,128]{1,0:T(8,128)S(1)} collective-permute-done((f32[96,128]{1,0:T(8,128)S(1)}, f32[96,128]{1,0:T(8,128)S(1)}, u32[]{:S(2)}, u32[]{:S(2)}) %collective-permute-start.8) | collective-permute-done | bytes 49184 | tf_op jit(solution)/shard_map/ppermute | solution.py:447
  46.5 1.3 %collective-permute-start.9 = (f32[96,128]{1,0:T(8,128)S(1)}, f32[96,128]{1,0:T(8,128)S(1)}, u32[]{:S(2)}, u32[]{:S(2)}) collective-permute-start(f32[96,128]{1,0:T(8,128)S(1)} %add.17), channel_id=1, source_target_pairs={{0,8},{4,12},{8,0},{12,4},{16,24},{20,28},{24,16},{28,20},{1,9},{5... | collective-permute-start | bytes 147464 | tf_op jit(solution)/shard_map/ppermute | solution.py:447
  47.8 2.9 %collective-permute-done.9 = f32[96,128]{1,0:T(8,128)S(1)} collective-permute-done((f32[96,128]{1,0:T(8,128)S(1)}, f32[96,128]{1,0:T(8,128)S(1)}, u32[]{:S(2)}, u32[]{:S(2)}) %collective-permute-start.9) | collective-permute-done | bytes 49184 | tf_op jit(solution)/shard_map/ppermute | solution.py:447
  50.7 2.8 %collective-permute-start.10 = (f32[96,128]{1,0:T(8,128)S(1)}, f32[96,128]{1,0:T(8,128)S(1)}, u32[]{:S(2)}, u32[]{:S(2)}) collective-permute-start(f32[96,128]{1,0:T(8,128)S(1)} %add.18), channel_id=1, source_target_pairs={{0,16},{4,20},{8,24},{12,28},{16,0},{20,4},{24,8},{28,12},{1,17},{... | collective-permute-start | bytes 147464 | tf_op jit(solution)/shard_map/ppermute | solution.py:447
  53.4 2.3 %collective-permute-done.10 = f32[96,128]{1,0:T(8,128)S(1)} collective-permute-done((f32[96,128]{1,0:T(8,128)S(1)}, f32[96,128]{1,0:T(8,128)S(1)}, u32[]{:S(2)}, u32[]{:S(2)}) %collective-permute-start.10) | collective-permute-done | bytes 49184 | tf_op jit(solution)/shard_map/ppermute | solution.py:447
  55.7 0.1 collective-permute-start.11
  55.8 1.2 %collective-permute-done.11.other_ref = f32[96,128]{1,0:T(8,128)S(1)} collective-permute-done((f32[96,128]{1,0:T(8,128)S(1)}, f32[96,128]{1,0:T(8,128)S(1)}, u32[]{:S(2)}, u32[]{:S(2)}) %collective-permute-start.11) | collective-permute-done | bytes 49184 | tf_op jit(solution)/shard_map/ppermute | solution.py:449
  57.0 10.7 %factor_and_basis.1 = (f32[192,192]{1,0:T(8,128)}, f32[192,3072]{1,0:T(8,128)}) custom-call(s32[1]{0:T(128)} %bitcast.core_ref, f32[1,128]{1,0:T(1,128)S(1)} %bitcast.4, f32[96,128]{1,0:T(8,128)S(1)} %add.19.mine_ref, f32[96,128]{1,0:T(8,128)S(1)} %collective-permute-done.11.other_ref, f32[128,3072]{1,0:T(8,128)S(1)} %copy-done, ...), custom_call_target="tpu_custom_call" | custom-call | flops 1358954496 | bytes 4718592 | tf_op jit(solution)/shard_map/factor_and_basis/pallas_call | solution.py:383
  (6 shorter events, 0.0 us)
Async XLA Ops:
  0.6 10.6 %copy-start = (f32[128,3072]{1,0:T(8,128)S(1)}, f32[128,3072]{1,0:T(8,128)}, u32[]{:S(2)}) copy-start(f32[128,3072]{1,0:T(8,128)} %modes_ref.5) | copy-start | bytes 4718596
  0.6 10.6 %copy-start.2 = (s32[64]{0:T(128)S(1)}, s32[64]{0:T(128)}, u32[]{:S(2)}) copy-start(s32[64]{0:T(128)} %steps_ref.3) | copy-start | bytes 772
  0.7 10.6 %copy-start.4 = (f32[63,3072]{1,0:T(8,128)S(1)}, f32[63,3072]{1,0:T(8,128)}, u32[]{:S(2)}) copy-start(f32[63,3072]{1,0:T(8,128)} %history_ref.1) | copy-start | bytes 2322436
  0.7 10.6 %copy-start.3 = (f32[128]{0:T(128)S(1)}, f32[128]{0:T(128)}, u32[]{:S(2)}) copy-start(f32[128]{0:T(128)} %param.8) | copy-start | bytes 1540
  3.4 18.6 %copy-start.1 = (s32[1024]{0:T(1024)S(1)}, s32[1024]{0:T(1024)}, u32[]{:S(2)}) copy-start(s32[1024]{0:T(1024)} %ids_ref.1) | copy-start | bytes 12292
  3.4 18.6 %collective-permute-start = (f32[3,2,32,512]{3,2,1,0:T(8,128)}, f32[3,2,32,512]{3,2,1,0:T(8,128)S(1)}, u32[]{:S(2)}, u32[]{:S(2)}) collective-permute-start(f32[3,2,32,512]{3,2,1,0:T(8,128)} %get-tuple-element.17), channel_id=1, source_target_pairs={{0,1},{1,2},{2,3},{3,0},{4,5},{5,6},{6,7},{7,4},{8,9},{9,10},{10,1... | collective-permute-start | bytes 1179656 | tf_op jit(solution)/shard_map/ppermute | solution.py:425
  3.9 18.1 %collective-permute-start.1 = (f32[3,2,32,512]{3,2,1,0:T(8,128)}, f32[3,2,32,512]{3,2,1,0:T(8,128)}, u32[]{:S(2)}, u32[]{:S(2)}) collective-permute-start(f32[3,2,32,512]{3,2,1,0:T(8,128)} %get-tuple-element.18), channel_id=1, source_target_pairs={{0,3},{1,0},{2,1},{3,2},{4,7},{5,4},{6,5},{7,6},{8,11},{9,8},{10,9... | collective-permute-start | bytes 1179656 | tf_op jit(solution)/shard_map/ppermute | solution.py:426
  5.9 10.7 %collective-permute-start.2 = (f32[3,16,2,512]{3,2,1,0:T(2,128)S(1)}, f32[3,16,2,512]{3,2,1,0:T(2,128)S(1)}, u32[]{:S(2)}, u32[]{:S(2)}) collective-permute-start(f32[3,16,2,512]{3,2,1,0:T(2,128)S(1)} %get-tuple-element.19), channel_id=1, source_target_pairs={{0,4},{4,8},{8,12},{12,16},{16,20},{20,24},{24,28},{28,0},{1,5},{5... | collective-permute-start | bytes 589832 | tf_op jit(solution)/shard_map/ppermute | solution.py:428
  8.2 10.6 %collective-permute-start.3 = (f32[3,16,2,512]{3,2,1,0:T(2,128)S(1)}, f32[3,16,2,512]{3,2,1,0:T(2,128)S(1)}, u32[]{:S(2)}, u32[]{:S(2)}) collective-permute-start(f32[3,16,2,512]{3,2,1,0:T(2,128)S(1)} %get-tuple-element.20), channel_id=1, source_target_pairs={{0,28},{4,0},{8,4},{12,8},{16,12},{20,16},{24,20},{28,24},{1,29},{... | collective-permute-start | bytes 589832 | tf_op jit(solution)/shard_map/ppermute | solution.py:429
  18.8 3.2 %collective-permute-start.4 = (f32[3,2,512]{2,1,0:T(2,128)S(1)}, f32[3,2,512]{2,1,0:T(2,128)S(1)}, u32[]{:S(2)}, u32[]{:S(2)}) collective-permute-start(f32[3,2,512]{2,1,0:T(2,128)S(1)} %get-tuple-element.22), channel_id=1, source_target_pairs={{0,1},{1,2},{2,3},{3,0},{4,5},{5,6},{6,7},{7,4},{8,9},{9,10},{10,1... | collective-permute-start | bytes 36872 | tf_op jit(solution)/shard_map/ppermute | solution.py:435
  18.8 3.1 %collective-permute-start.5 = (f32[3,2,512]{2,1,0:T(2,128)S(1)}, f32[3,2,512]{2,1,0:T(2,128)S(1)}, u32[]{:S(2)}, u32[]{:S(2)}) collective-permute-start(f32[3,2,512]{2,1,0:T(2,128)S(1)} %get-tuple-element.23), channel_id=1, source_target_pairs={{0,3},{1,0},{2,1},{3,2},{4,7},{5,4},{6,5},{7,6},{8,11},{9,8},{10,9... | collective-permute-start | bytes 36872 | tf_op jit(solution)/shard_map/ppermute | solution.py:436
  36.7 1.6 %collective-permute-start.6 = (f32[96,128]{1,0:T(8,128)S(1)}, f32[96,128]{1,0:T(8,128)S(1)}, u32[]{:S(2)}, u32[]{:S(2)}) collective-permute-start(f32[96,128]{1,0:T(8,128)S(1)} %get-tuple-element.27), channel_id=1, source_target_pairs={{0,1},{1,0},{2,3},{3,2},{4,5},{5,4},{6,7},{7,6},{8,9},{9,8},{10,11... | collective-permute-start | bytes 147464 | tf_op jit(solution)/shard_map/ppermute | solution.py:443
  38.2 4.1 %collective-permute-start.7 = (f32[96,128]{1,0:T(8,128)S(1)}, f32[96,128]{1,0:T(8,128)S(1)}, u32[]{:S(2)}, u32[]{:S(2)}) collective-permute-start(f32[96,128]{1,0:T(8,128)S(1)} %add.15), channel_id=1, source_target_pairs={{0,2},{1,3},{2,0},{3,1},{4,6},{5,7},{6,4},{7,5},{8,10},{9,11},{10,... | collective-permute-start | bytes 147464 | tf_op jit(solution)/shard_map/ppermute | solution.py:447
  42.3 4.2 %collective-permute-start.8 = (f32[96,128]{1,0:T(8,128)S(1)}, f32[96,128]{1,0:T(8,128)S(1)}, u32[]{:S(2)}, u32[]{:S(2)}) collective-permute-start(f32[96,128]{1,0:T(8,128)S(1)} %add.16), channel_id=1, source_target_pairs={{0,4},{4,0},{8,12},{12,8},{16,20},{20,16},{24,28},{28,24},{1,5},{5... | collective-permute-start | bytes 147464 | tf_op jit(solution)/shard_map/ppermute | solution.py:447
  46.5 4.2 %collective-permute-start.9 = (f32[96,128]{1,0:T(8,128)S(1)}, f32[96,128]{1,0:T(8,128)S(1)}, u32[]{:S(2)}, u32[]{:S(2)}) collective-permute-start(f32[96,128]{1,0:T(8,128)S(1)} %add.17), channel_id=1, source_target_pairs={{0,8},{4,12},{8,0},{12,4},{16,24},{20,28},{24,16},{28,20},{1,9},{5... | collective-permute-start | bytes 147464 | tf_op jit(solution)/shard_map/ppermute | solution.py:447
  50.7 5.0 %collective-permute-start.10 = (f32[96,128]{1,0:T(8,128)S(1)}, f32[96,128]{1,0:T(8,128)S(1)}, u32[]{:S(2)}, u32[]{:S(2)}) collective-permute-start(f32[96,128]{1,0:T(8,128)S(1)} %add.18), channel_id=1, source_target_pairs={{0,16},{4,20},{8,24},{12,28},{16,0},{20,4},{24,8},{28,12},{1,17},{... | collective-permute-start | bytes 147464 | tf_op jit(solution)/shard_map/ppermute | solution.py:447
  55.7 1.3 %collective-permute-start.11 = (f32[96,128]{1,0:T(8,128)S(1)}, f32[96,128]{1,0:T(8,128)S(1)}, u32[]{:S(2)}, u32[]{:S(2)}) collective-permute-start(f32[96,128]{1,0:T(8,128)S(1)} %add.19.mine_ref), channel_id=1, source_target_pairs={{0,1},{1,0},{2,3},{3,2},{4,5},{5,4},{6,7},{7,6},{8,9},{9,8},{10,11... | collective-permute-start | bytes 147464 | tf_op jit(solution)/shard_map/ppermute | solution.py:449

commit v2 on v1

--- a/solution.py
+++ b/solution.py
@@ -29,41 +29,32 @@
     )
 
 
-def faces_kernel(velocity_ref, xlow_ref, xhigh_ref, ylow_ref, yhigh_ref, low, high, sems):
+def faces_kernel(velocity_ref, ylow_ref, yhigh_ref, xlow_ref, xhigh_ref, sems):
     nx, ny = velocity_ref.shape[1:3]
     copies = [
-        pltpu.make_async_copy(velocity_ref.at[:, 0:2], xlow_ref, sems.at[0]),
-        pltpu.make_async_copy(velocity_ref.at[:, nx - 2 : nx], xhigh_ref, sems.at[1]),
-        pltpu.make_async_copy(velocity_ref.at[:, :, 0:8, :], low, sems.at[2]),
-        pltpu.make_async_copy(velocity_ref.at[:, :, ny - 8 : ny, :], high, sems.at[3]),
+        pltpu.make_async_copy(velocity_ref.at[:, :, 0:2, :], ylow_ref, sems.at[0]),
+        pltpu.make_async_copy(velocity_ref.at[:, :, ny - 2 : ny, :], yhigh_ref, sems.at[1]),
+        pltpu.make_async_copy(velocity_ref.at[:, 0:2], xlow_ref, sems.at[2]),
+        pltpu.make_async_copy(velocity_ref.at[:, nx - 2 : nx], xhigh_ref, sems.at[3]),
     ]
     for copy in copies:
         copy.start()
-    copies[2].wait()
-    ylow_ref[...] = low[:, :, 0:2, :]
-    copies[3].wait()
-    yhigh_ref[...] = high[:, :, 6:8, :]
-    copies[0].wait()
-    copies[1].wait()
+    for copy in copies:
+        copy.wait()
 
 
 def faces(velocity):
     comps, nx, ny, nz = velocity.shape
-    hbm = pl.BlockSpec(memory_space=pl.ANY)
     vmem = pl.BlockSpec(memory_space=pltpu.VMEM)
     across_x = pltpu.VMEM((comps, 2, ny, nz), jnp.float32)
     across_y = pltpu.VMEM((comps, nx, 2, nz), jnp.float32)
     return pl.pallas_call(
         faces_kernel,
-        in_specs=[hbm],
-        out_specs=[vmem, vmem, vmem, vmem],
-        out_shape=[across_x, across_x, across_y, across_y],
-        scratch_shapes=[
-            pltpu.VMEM((comps, nx, 8, nz), jnp.float32),
-            pltpu.VMEM((comps, nx, 8, nz), jnp.float32),
-            pltpu.SemaphoreType.DMA((4,)),
-        ],
-        compiler_params=pltpu.CompilerParams(vmem_limit_bytes=16 * 2**20),
+        in_specs=[pl.BlockSpec(memory_space=pl.ANY)],
+        out_specs=[vmem] * 4,
+        out_shape=[across_y, across_y, across_x, across_x],
+        scratch_shapes=[pltpu.SemaphoreType.DMA((4,))],
+        compiler_params=pltpu.CompilerParams(vmem_limit_bytes=2 * 2**20),
         name="faces",
     )(in_hbm(velocity))
 
@@ -121,7 +112,7 @@
             pltpu.VMEM((total, total), jnp.float32),
             pltpu.VMEM((count, width), jnp.float32),
         ],
-        compiler_params=pltpu.CompilerParams(vmem_limit_bytes=24 * 2**20),
+        compiler_params=pltpu.CompilerParams(vmem_limit_bytes=10 * 2**20),
         cost_estimate=pl.CostEstimate(
             flops=12 * total * total * width, bytes_accessed=12 * total * width, transcendentals=0
         ),
@@ -129,79 +120,171 @@
     )(in_vmem(steps), in_vmem(weights), in_vmem(modes), in_vmem(history))
 
 
-def substep(src, dst, rows, src_x, dst_x, tiles, store):
+def stencil(tile, which, inner, store):
+    adv = 0.5 * time_step
     diff = time_step * viscosity
-    adv = 0.5 * time_step
-    for t in range(tiles):
-        lo, hi = 8 * t, 8 * t + 8
-        mid = [src[c, src_x, lo:hi, :] for c in range(3)]
-        ax = [diff - adv * v for v in mid]
-        bx = [diff + adv * v for v in mid]
+    sub = lax.broadcasted_iota(jnp.int32, tile(0, 0, 0).shape, 0)
+    first, last = sub == 0, sub == 7
+    for t in which:
+        before, after = (t - 1) % (inner + 1), (t + 1) % (inner + 1)
+        mid = [tile(0, c, t) for c in range(3)]
+        scaled = [adv * v for v in mid]
+        plus = [diff - v for v in scaled]
+        minus = [diff + v for v in scaled]
         for c in range(3):
             v = mid[c]
-            if lo == 0:
-                y_minus = jnp.concatenate([src[c, src_x, rows - 1 : rows, :], src[c, src_x, 0:7, :]], axis=0)
-            else:
-                y_minus = src[c, src_x, lo - 1 : hi - 1, :]
-            if hi == rows:
-                y_plus = jnp.concatenate([src[c, src_x, lo + 1 : hi, :], src[c, src_x, 0:1, :]], axis=0)
-            else:
-                y_plus = src[c, src_x, lo + 1 : hi + 1, :]
-            x_plus = src[c, src_x + 1, lo:hi, :]
-            x_minus = src[c, src_x - 1, lo:hi, :]
-            z_plus = pltpu.roll(v, v.shape[1] - 1, 1)
-            z_minus = pltpu.roll(v, 1, 1)
+            y_plus = jnp.where(last, pltpu.roll(tile(0, c, after), 7, 0), pltpu.roll(v, 7, 0))
+            y_minus = jnp.where(first, pltpu.roll(tile(0, c, before), 1, 0), pltpu.roll(v, 1, 0))
             out = (1.0 - 6.0 * diff) * v
-            out = out + ax[0] * x_plus + bx[0] * x_minus
-            out = out + ax[1] * y_plus + bx[1] * y_minus
-            out = out + ax[2] * z_plus + bx[2] * z_minus
-            store(c, dst_x, lo, hi, out)
+            out = out + plus[0] * tile(1, c, t) + minus[0] * tile(-1, c, t)
+            out = out + plus[1] * y_plus + minus[1] * y_minus
+            out = out + plus[2] * pltpu.roll(v, v.shape[1] - 1, 1) + minus[2] * pltpu.roll(v, 1, 1)
+            store(c, t, out)
 
 
 def field_kernel(
-    ids_ref, steps_ref, core_ref, w_ref, velocity_ref, xlo_ref, xhi_ref, ylo_ref, yhi_ref, clo_ref, chi_ref,
-    modes_ref, snaps_ref, gram_ref,
-    advanced_ref, snaps_out_ref, mine_ref, other_ref,
-    p0, p1, u2, flat, picked, packed, sem, out_sems,
+    velocity_ref, xlo_ref, xhi_ref, ylo_ref, yhi_ref,
+    advanced_ref, p1, ends_ref, flat, ring_tile, u2, out_sems,
 ):
-    comps, nx, ny, nz = u2.shape
-    rows = ny + 8
-    inner = pltpu.make_async_copy(velocity_ref, p0.at[:, 2 : nx + 2, 0:ny, :], sem)
-    inner.start()
-    p0[:, 0:2, 0:ny, :] = xlo_ref[...]
-    p0[:, nx + 2 : nx + 4, 0:ny, :] = xhi_ref[...]
+    comps, nx, ny, nz = velocity_ref.shape
+    inner = ny // 8
+    tiles = nz // LANES
     for c in range(comps):
         for x in range(nx):
-            p0[c, x + 2, ny : ny + 2, :] = yhi_ref[c, x]
-            p0[c, x + 2, rows - 2 : rows, :] = ylo_ref[c, x]
-        p0[c, 1, rows - 1 : rows, :] = clo_ref[c, 0:1, :]
-        p0[c, 1, ny : ny + 1, :] = clo_ref[c, 1:2, :]
-        p0[c, nx + 2, rows - 1 : rows, :] = chi_ref[c, 0:1, :]
-        p0[c, nx + 2, ny : ny + 1, :] = chi_ref[c, 1:2, :]
-    inner.wait()
-
-    def keep1(c, x, lo, hi, out):
-        p1[c, x, lo:hi, :] = out
-
-    tiles = nz // LANES
-
-    def keep2(c, x, lo, hi, out):
-        u2[c, x, lo:hi, :] = out
-        for k in range(tiles):
-            at = pl.multiple_of((k * nx + x) * ny + lo, 8)
-            flat[c, pl.ds(at, 8), :] = out[:, k * LANES : (k + 1) * LANES]
-
-    @pl.loop(0, nx + 2)
+            ring_tile[c, x, 0:2, :] = yhi_ref[c, x]
+            ring_tile[c, x, 6:8, :] = ylo_ref[c, x]
+
+    def first_layer(x, refs, layers, count):
+        def tile(k, c, t):
+            if t == inner:
+                if isinstance(x, int) and not 0 <= x + k < nx:
+                    return jnp.zeros((8, nz), jnp.float32)
+                return ring_tile[c, x + k]
+            return refs[k + 1][c, layers[k + 1], 8 * t : 8 * t + 8, :]
+
+        def store(c, t, value):
+            p1[c, x + 1, 8 * t : 8 * t + 8, :] = value
+
+        stencil(tile, range(count), inner, store)
+
+    vel = velocity_ref
+    first_layer(-1, (xlo_ref, xlo_ref, vel), (0, 1, 0), inner)
+    first_layer(0, (xlo_ref, vel, vel), (1, 0, 1), inner + 1)
+
+    @pl.loop(1, nx - 1)
     def _(x):
-        substep(p0, p1, rows, x + 1, x, rows // 8, keep1)
+        first_layer(x, (vel, vel, vel), (x - 1, x, x + 1), inner + 1)
+
+    first_layer(nx - 1, (vel, vel, xhi_ref), (nx - 2, nx - 1, 0), inner + 1)
+    first_layer(nx, (vel, xhi_ref, xhi_ref), (nx - 1, 0, 1), inner)
+
+    def second_layer(x, out, layer):
+        def tile(k, c, t):
+            return p1[c, x + 1 + k, 8 * t : 8 * t + 8, :]
+
+        def store(c, t, value):
+            out[c, layer, 8 * t : 8 * t + 8, :] = value
+            for k in range(tiles):
+                at = pl.multiple_of((k * nx + x) * ny + 8 * t, 8)
+                flat[c, pl.ds(at, 8), :] = value[:, k * LANES : (k + 1) * LANES]
+
+        stencil(tile, range(inner), inner, store)
 
     def out_copy(x):
         return pltpu.make_async_copy(u2.at[:, x], advanced_ref.at[:, x], out_sems.at[x])
 
-    @pl.loop(0, nx)
+    @pl.loop(1, nx - 1)
     def _(x):
-        substep(p1, u2, rows, x + 1, x, ny // 8, keep2)
+        second_layer(x, u2, x)
         out_copy(x).start()
+
+    second_layer(0, ends_ref, 0)
+    second_layer(nx - 1, ends_ref, 1)
+
+    @pl.loop(1, nx - 1)
+    def _(x):
+        out_copy(x).wait()
+
+
+def field_call(velocity, xlo, xhi, ylo, yhi):
+    comps, nx, ny, nz = velocity.shape
+    vmem = pl.BlockSpec(memory_space=pltpu.VMEM)
+    return pl.pallas_call(
+        field_kernel,
+        in_specs=[vmem] * 5,
+        out_specs=[pl.BlockSpec(memory_space=pl.ANY), vmem, vmem, vmem],
+        out_shape=[
+            pltpu.HBM(velocity.shape, jnp.float32),
+            pltpu.VMEM((comps, nx + 2, ny + 8, nz), jnp.float32),
+            pltpu.VMEM((comps, 2, ny, nz), jnp.float32),
+            pltpu.VMEM((comps, nx * ny * nz // LANES, LANES), jnp.float32),
+        ],
+        scratch_shapes=[
+            pltpu.VMEM((comps, nx, 8, nz), jnp.float32),
+            pltpu.VMEM((comps, nx, ny, nz), jnp.float32),
+            pltpu.SemaphoreType.DMA((nx,)),
+        ],
+        compiler_params=pltpu.CompilerParams(vmem_limit_bytes=8 * 2**20),
+        cost_estimate=pl.CostEstimate(
+            flops=60 * velocity.size, bytes_accessed=8 * velocity.size, transcendentals=0
+        ),
+        name="substeps",
+    )(*(in_vmem(a) for a in (velocity, xlo, xhi, ylo, yhi)))
+
+
+def sample_kernel(
+    ids_ref, steps_ref, w_ref, xlo_ref, xhi_ref, clo_ref, chi_ref, own_lo_ref, own_hi_ref,
+    p1, modes_ref, snaps_ref, gram_ref, advanced_in, ends_in, flat_in,
+    advanced_ref, ends_ref, flat, snaps_out_ref, mine_ref, other_ref,
+    fixed, picked, packed, sems,
+):
+    comps, _, ny, nz = xlo_ref.shape
+    nx = flat.shape[1] * LANES // (ny * nz)
+    inner = ny // 8
+    tiles = nz // LANES
+    sub = lax.broadcasted_iota(jnp.int32, (8, nz), 0)
+    adv = 0.5 * time_step
+    diff = time_step * viscosity
+
+    def halo_tile(line, c):
+        return jnp.where(sub == 0, line[c, 1:2, :], line[c, 0:1, :])
+
+    for end, layer, mid, line, own in (
+        (0, 0, xlo_ref.at[:, 1], clo_ref, own_lo_ref),
+        (1, nx - 1, xhi_ref.at[:, 0], chi_ref, own_hi_ref),
+    ):
+        sign = 1.0 if end == 0 else -1.0
+        outside = layer if end == 0 else layer + 2
+        own_x = diff + sign * adv * halo_tile(own, 0)
+        low_y = diff + adv * mid[1, 0:8, :]
+        high_y = diff - adv * mid[1, ny - 8 : ny, :]
+        for c in range(comps):
+            corner = halo_tile(line, c)
+            halo = p1[c, layer + 1, ny : ny + 8, :] + own_x * corner
+            fixed[c, end, 2] = halo
+            fixed[c, end, 0] = p1[c, outside, 0:8, :] + jnp.where(sub == 0, low_y * line[c, 0:1, :], 0.0)
+            fixed[c, end, 1] = p1[c, outside, ny - 8 : ny, :] + jnp.where(sub == 7, high_y * line[c, 1:2, :], 0.0)
+
+        def tile(k, c, t):
+            if k == (-1 if end == 0 else 1):
+                return fixed[c, end, 0 if t == 0 else 1]
+            if t == inner:
+                return fixed[c, end, 2]
+            return p1[c, layer + 1 + k, 8 * t : 8 * t + 8, :]
+
+        def store(c, t, value):
+            ends_ref[c, end, 8 * t : 8 * t + 8, :] = value
+            for k in range(tiles):
+                at = (k * nx + layer) * ny + 8 * t
+                flat[c, at : at + 8, :] = value[:, k * LANES : (k + 1) * LANES]
+
+        stencil(tile, (0, inner - 1), inner, store)
+    out_copies = [
+        pltpu.make_async_copy(ends_ref.at[:, 0], advanced_ref.at[:, 0], sems.at[0]),
+        pltpu.make_async_copy(ends_ref.at[:, 1], advanced_ref.at[:, nx - 1], sems.at[1]),
+    ]
+    for copy in out_copies:
+        copy.start()
 
     count = ids_ref.shape[0]
     lane = lax.broadcasted_iota(jnp.int32, (1, LANES), 1)
@@ -247,50 +330,50 @@
     packed[k:, 0:half] = gram_ref[0:half, 0:half]
     packed[k:, half:k] = low
     part = mine_ref.shape[0]
-    core = core_ref[0]
+    core = lax.axis_index("grp") & 1
     mine_ref[...] = packed[pl.ds(pl.multiple_of(core * part, 8), part), :]
     other_ref[...] = packed[pl.ds(pl.multiple_of((1 - core) * part, 8), part), :]
-
-    @pl.loop(0, nx)
-    def _(x):
-        out_copy(x).wait()
-
-
-def field_call(ids, steps, core, weights, velocity, xlo, xhi, ylo, yhi, clo, chi, modes, snaps, gram):
-    comps, nx, ny, nz = velocity.shape
+    for copy in out_copies:
+        copy.wait()
+
+
+def sample_call(
+    ids, steps, weights, xlo, xhi, clo, chi, own_lo, own_hi, p1, modes, snaps, gram, advanced, ends, flat
+):
+    comps, _, _, nz = xlo.shape
     total = gram.shape[0]
     part = total // 2
     smem = pl.BlockSpec(memory_space=pltpu.SMEM)
     vmem = pl.BlockSpec(memory_space=pltpu.VMEM)
     hbm = pl.BlockSpec(memory_space=pl.ANY)
+    tail = (weights, xlo, xhi, clo, chi, own_lo, own_hi, p1, modes, snaps, gram)
     return pl.pallas_call(
-        field_kernel,
-        in_specs=[smem, smem, smem, vmem, hbm] + [vmem] * 9,
-        out_specs=[hbm, vmem, vmem, vmem],
+        sample_kernel,
+        in_specs=[smem] * 2 + [vmem] * 11 + [hbm, vmem, vmem],
+        out_specs=[hbm, vmem, vmem, vmem, vmem, vmem],
         out_shape=[
-            pltpu.HBM(velocity.shape, jnp.float32),
+            pltpu.HBM(advanced.shape, jnp.float32),
+            pltpu.VMEM(ends.shape, jnp.float32),
+            pltpu.VMEM(flat.shape, jnp.float32),
             pltpu.VMEM(snaps.shape, jnp.float32),
             pltpu.VMEM((part, LANES), jnp.float32),
             pltpu.VMEM((part, LANES), jnp.float32),
         ],
+        input_output_aliases={13: 0, 14: 1, 15: 2},
         scratch_shapes=[
-            pltpu.VMEM((comps, nx + 4, ny + 8, nz), jnp.float32),
-            pltpu.VMEM((comps, nx + 2, ny + 8, nz), jnp.float32),
-            pltpu.VMEM((comps, nx, ny, nz), jnp.float32),
-            pltpu.VMEM((comps, nx * ny * nz // LANES, LANES), jnp.float32),
+            pltpu.VMEM((comps, 2, 3, 8, nz), jnp.float32),
             pltpu.VMEM((comps, ids.shape[0], LANES), jnp.float32),
             pltpu.VMEM((total, LANES), jnp.float32),
-            pltpu.SemaphoreType.DMA,
-            pltpu.SemaphoreType.DMA((nx,)),
-        ],
-        compiler_params=pltpu.CompilerParams(vmem_limit_bytes=26 * 2**20),
+            pltpu.SemaphoreType.DMA((2,)),
+        ],
+        compiler_params=pltpu.CompilerParams(vmem_limit_bytes=6 * 2**20),
         cost_estimate=pl.CostEstimate(
-            flops=60 * velocity.size, bytes_accessed=8 * velocity.size, transcendentals=0
+            flops=20 * flat.size, bytes_accessed=2 * flat.size, transcendentals=0
         ),
-        name="substeps_and_sample",
+        name="sample_and_gram",
     )(
-        in_vmem(ids), in_vmem(steps), core, in_vmem(weights), in_hbm(velocity), in_vmem(xlo), in_vmem(xhi),
-        in_vmem(ylo), in_vmem(yhi), in_vmem(clo), in_vmem(chi), in_vmem(modes), in_vmem(snaps), in_vmem(gram),
+        in_vmem(ids), in_vmem(steps), *(in_vmem(a) for a in tail),
+        in_hbm(advanced), in_vmem(ends), in_vmem(flat),
     )
 
 
@@ -326,7 +409,7 @@
     return jnp.where(upper, table[:, :n], 0.0), table[:, n:]
 
 
-def basis_kernel(root, core_ref, w_ref, mine_ref, other_ref, modes_ref, snaps_ref, factor_ref, basis_ref, packed, inverse):
+def basis_kernel(root, w_ref, mine_ref, other_ref, modes_ref, snaps_ref, factor_ref, basis_ref, packed, inverse):
     total = factor_ref.shape[0]
     half = total // 3
     two = 2 * half
@@ -334,7 +417,7 @@
     @pl.when(pl.program_id(0) == 0)
     def _():
         part = mine_ref.shape[0]
-        core = core_ref[0]
+        core = lax.axis_index("grp") & 1
         packed[pl.ds(pl.multiple_of(core * part, 8), part), :] = mine_ref[...]
         packed[pl.ds(pl.multiple_of((1 - core) * part, 8), part), :] = other_ref[...]
         a00 = packed[two:, 0:half]
@@ -373,18 +456,16 @@
     basis_ref[...] = dot(inverse[:, 0:total], rows)
 
 
-def basis_call(root, core, weights, mine, other, modes, snaps):
+def basis_call(root, weights, mine, other, modes, snaps):
     k, width = modes.shape
     count = snaps.shape[0]
     total = k + count
     chunk = 512
-    smem = pl.BlockSpec(memory_space=pltpu.SMEM)
     whole = lambda shape: pl.BlockSpec(shape, lambda i: (0, 0))
     return pl.pallas_call(
         functools.partial(basis_kernel, root),
         grid=(width // chunk,),
         in_specs=[
-            smem,
             whole(weights.shape),
             whole(mine.shape),
             whole(other.shape),
@@ -400,12 +481,12 @@
             pltpu.VMEM((total, LANES), jnp.float32),
             pltpu.VMEM((total, 2 * LANES), jnp.float32),
         ],
-        compiler_params=pltpu.CompilerParams(vmem_limit_bytes=24 * 2**20),
+        compiler_params=pltpu.CompilerParams(vmem_limit_bytes=10 * 2**20),
         cost_estimate=pl.CostEstimate(
             flops=12 * total * total * width, bytes_accessed=8 * total * width, transcendentals=0
         ),
         name="factor_and_basis",
-    )(core, in_vmem(weights), in_vmem(mine), in_vmem(other), in_vmem(modes), in_vmem(snaps))
+    )(in_vmem(weights), in_vmem(mine), in_vmem(other), in_vmem(modes), in_vmem(snaps))
 
 
 def ring(axis):
@@ -420,13 +501,13 @@
 
 
 def per_device(velocity, modes, mode_weights, history, slab_ids, snap_steps):
-    xlow, xhigh, ylow, yhigh = faces(velocity)
+    ylow, yhigh, xlow, xhigh = faces(velocity)
+    up_y, down_y = ring("tile")
     up, down = ring("grp")
+    ylo = lax.ppermute(yhigh, "tile", up_y)
+    yhi = lax.ppermute(ylow, "tile", down_y)
     xlo = lax.ppermute(xhigh, "grp", up)
     xhi = lax.ppermute(xlow, "grp", down)
-    up_y, down_y = ring("tile")
-    ylo = lax.ppermute(yhigh, "tile", up_y)
-    yhi = lax.ppermute(ylow, "tile", down_y)
 
     weights = mode_weights.reshape(1, -1)
     gram, snaps = early_gram(snap_steps, weights, modes, history)
@@ -435,9 +516,9 @@
     clo = lax.ppermute(chigh, "grp", up)
     chi = lax.ppermute(clow, "grp", down)
 
-    core = (lax.axis_index("grp") & 1).astype(jnp.int32).reshape(1)
-    advanced, snaps, mine, other = field_call(
-        slab_ids, snap_steps, core, weights, velocity, xlo, xhi, ylo, yhi, clo, chi, modes, snaps, gram
+    advanced, p1, ends, flat = field_call(velocity, xlo, xhi, ylo, yhi)
+    advanced, _, _, snaps, mine, other = sample_call(
+        slab_ids, snap_steps, weights, xlo, xhi, clo, chi, clow, chigh, p1, modes, snaps, gram, advanced, ends, flat
     )
 
     mine = mine + lax.ppermute(other, "grp", swap("grp", 1))
@@ -450,7 +531,7 @@
 
     total_rows = modes.shape[1] * lax.axis_size("tile") * lax.axis_size("grp")
     root = math.sqrt(total_rows)
-    factor, basis = basis_call(root, core, weights, mine, other, modes, snaps)
+    factor, basis = basis_call(root, weights, mine, other, modes, snaps)
     return (advanced, basis, factor)
 
 

time: 67.9 us -> 63.3 us (0.932)
  Pallas kernels: 32.2 us -> 29.3 us
  starting transfers between devices: 16.3 us -> 14.5 us
    pallas_call x2 -> x3, Pallas kernels: 17.4 us -> 14.4 us  [the longest x1 6.99 us: field_call(): pl.pallas_call(field_kernel, in_specs=[vmem] * 5, out_specs=[pl.BlockSpec...]
    ppermute x1, waiting for transfers between devices: 1.37 us -> 0.01 us  [per_device(): clo = lax.ppermute(chigh, 'grp', up)]
    ppermute x4, waiting for transfers between devices: 11.5 us -> 12.7 us  [per_device(): mine = mine + lax.ppermute(mine, axis, swap(axis, bit))]
    ppermute x4, starting transfers between devices: 5.92 us -> 4.8 us  [per_device(): mine = mine + lax.ppermute(mine, axis, swap(axis, bit))]
  transfers between devices with their start and end apart: 12 -> 12, of which waited for: 9 -> 8; matrix products, arithmetic and copies ran while one was open for 0% -> 0% of each run, Pallas kernels for 6% -> 18%
where the time goes in v2:
time: 63.3 us; the launch traced here: 63.2 us
  Pallas kernels  29.3 us (46%)
  waiting for transfers between devices  18.5 us (29%)
  starting transfers between devices  14.5 us (23%)
  between operations  0.77 us (1%)
    ppermute x4, waiting for transfers between devices, per_device(): mine = mine + lax.ppermute(mine, axis, swap(axis, bit))  12.7 us
    pallas_call x1, Pallas kernels, basis_call(): pl.pallas_call(functools.partial(basis_kernel, root), grid=(width // chun...  10.8 us
    pallas_call x1, Pallas kernels, field_call(): pl.pallas_call(field_kernel, in_specs=[vmem] * 5, out_specs=[pl.BlockSpec...  6.99 us
    pallas_call x1, Pallas kernels, sample_call(): pl.pallas_call(sample_kernel, in_specs=[smem] * 2 + [vmem] * 11 + [hbm, v...  5.89 us
    ppermute x4, starting transfers between devices, per_device(): mine = mine + lax.ppermute(mine, axis, swap(axis, bit))  4.8 us
    pallas_call x1, Pallas kernels, early_gram(): pl.pallas_call(gram_kernel, in_specs=[pl.BlockSpec(memory_space=pltpu.SME...  4.14 us
    ppermute x1, starting transfers between devices, per_device(): yhi = lax.ppermute(ylow, 'tile', down_y)  3.04 us
    ppermute x1, starting transfers between devices, per_device(): ylo = lax.ppermute(yhigh, 'tile', up_y)  2.27 us
  transfers between devices with their start and end apart: 12, of which 8 were waited for; matrix products, arithmetic and copies ran while one was open for 0% of the time, Pallas kernels for 18%

profile of v2, /device:TPU:0, one launch (start us, length us, event | category | flops | bytes accessed | tf_op | source)
XLA Modules:
  0.0 63.2 jit_solution(16045101463914445139)
XLA Ops:
  0.6 0.0 copy-start.1
  0.6 0.0 copy-start.3
  0.7 0.0 copy-start.5
  0.7 0.0 copy-start.4
  0.7 1.5 %faces.1 = (f32[3,16,2,512]{3,2,1,0:T(2,128)S(1)}, f32[3,16,2,512]{3,2,1,0:T(2,128)S(1)}, f32[3,2,32,512]{3,2,1,0:T(8,128)S(1)}, f32[3,2,32,512]{3,2,1,0:T(8,128)S(1)}) custom-call(f32[3,16,32,512]{3,2,1,0:T(8,128)} %velocity_ref.3), custom_call_target="tpu_custom_call" | custom-call | tf_op jit(solution)/shard_map/faces/pallas_call | solution.py:51
  2.2 0.0 copy-start
  2.2 0.5 collective-permute-start
  2.7 2.0 %collective-permute-start.1 = (f32[3,2,32,512]{3,2,1,0:T(8,128)S(1)}, f32[3,2,32,512]{3,2,1,0:T(8,128)S(1)}, u32[]{:S(2)}, u32[]{:S(2)}) collective-permute-start(f32[3,2,32,512]{3,2,1,0:T(8,128)S(1)} %get-tuple-element.22), channel_id=1, source_target_pairs={{0,3},{1,0},{2,1},{3,2},{4,7},{5,4},{6,5},{7,6},{8,11},{9,8},{10,9... | collective-permute-start | bytes 1179656 | tf_op jit(solution)/shard_map/ppermute | solution.py:510
  4.7 2.3 %collective-permute-start.2 = (f32[3,16,2,512]{3,2,1,0:T(2,128)S(1)}, f32[3,16,2,512]{3,2,1,0:T(2,128)S(1)}, u32[]{:S(2)}, u32[]{:S(2)}) collective-permute-start(f32[3,16,2,512]{3,2,1,0:T(2,128)S(1)} %get-tuple-element.23), channel_id=1, source_target_pairs={{0,4},{4,8},{8,12},{12,16},{16,20},{20,24},{24,28},{28,0},{1,5},{5... | collective-permute-start | bytes 589832 | tf_op jit(solution)/shard_map/ppermute | solution.py:507
  7.0 3.0 %collective-permute-start.3 = (f32[3,16,2,512]{3,2,1,0:T(2,128)S(1)}, f32[3,16,2,512]{3,2,1,0:T(2,128)S(1)}, u32[]{:S(2)}, u32[]{:S(2)}) collective-permute-start(f32[3,16,2,512]{3,2,1,0:T(2,128)S(1)} %get-tuple-element.24), channel_id=1, source_target_pairs={{0,28},{4,0},{8,4},{12,8},{16,12},{20,16},{24,20},{28,24},{1,29},{... | collective-permute-start | bytes 589832 | tf_op jit(solution)/shard_map/ppermute | solution.py:508
  10.0 0.0 copy-done.1
  10.0 0.0 copy-done.3
  10.0 0.0 copy-done.5
  10.0 0.0 copy-done.4
  10.0 4.1 %early_gram.1 = (f32[192,192]{1,0:T(8,128)S(1)}, f32[64,3072]{1,0:T(8,128)S(1)}) custom-call(s32[64]{0:T(128)S(1)} %copy-done.3, f32[1,128]{1,0:T(1,128)S(1)} %bitcast.1, f32[128,3072]{1,0:T(8,128)S(1)} %copy-done.1, f32[63,3072]{1,0:T(8,128)S(1)} %copy-done.5), custom_call_target="tpu_custom_call" | custom-call | flops 1358954496 | bytes 7077888 | tf_op jit(solution)/shard_map/early_gram/pallas_call | solution.py:107
  14.2 0.0 copy-start.2
  14.2 1.2 %collective-permute-done.2.ylo_ref = f32[3,16,2,512]{3,2,1,0:T(2,128)S(1)} collective-permute-done((f32[3,16,2,512]{3,2,1,0:T(2,128)S(1)}, f32[3,16,2,512]{3,2,1,0:T(2,128)S(1)}, u32[]{:S(2)}, u32[]{:S(2)}) %collective-permute-start.2) | collective-permute-done | bytes 196640 | tf_op jit(solution)/shard_map/ppermute | solution.py:507
  15.4 2.2 %collective-permute-done.3.yhi_ref = f32[3,16,2,512]{3,2,1,0:T(2,128)S(1)} collective-permute-done((f32[3,16,2,512]{3,2,1,0:T(2,128)S(1)}, f32[3,16,2,512]{3,2,1,0:T(2,128)S(1)}, u32[]{:S(2)}, u32[]{:S(2)}) %collective-permute-start.3) | collective-permute-done | bytes 196640 | tf_op jit(solution)/shard_map/ppermute | solution.py:508
  17.6 0.1 collective-permute-start.4
  17.6 1.7 %collective-permute-start.5 = (f32[3,2,512]{2,1,0:T(2,128)S(1)}, f32[3,2,512]{2,1,0:T(2,128)S(1)}, u32[]{:S(2)}, u32[]{:S(2)}) collective-permute-start(f32[3,2,512]{2,1,0:T(2,128)S(1)} %get-tuple-element.27.own_lo_ref), channel_id=1, source_target_pairs={{0,3},{1,0},{2,1},{3,2},{4,7},{5,4},{6,5},{7,6},{8,11},{9,8},{10,9... | collective-permute-start | bytes 36872 | tf_op jit(solution)/shard_map/ppermute | solution.py:517
  19.4 0.0 collective-permute-done.xlo_ref
  19.4 0.0 collective-permute-done.1.xhi_ref
  19.4 0.0 copy-done
  19.4 7.0 %substeps.1 = (f32[3,16,32,512]{3,2,1,0:T(8,128)}, f32[3,18,40,512]{3,2,1,0:T(8,128)S(1)}, f32[3,2,32,512]{3,2,1,0:T(8,128)S(1)}, f32[3,2048,128]{2,1,0:T(8,128)S(1)}) custom-call(f32[3,16,32,512]{3,2,1,0:T(8,128)S(1)} %copy-done, f32[3,2,32,512]{3,2,1,0:T(8,128)S(1)} %collective-permute-done.xlo_ref, f32[3,2,32,512]{3,2,1,0:T(8,128)S(1)} %collective-permute-done.1.xhi_ref, ...), custom_call_target="tpu_custom_call" | custom-call | flops 47185920 | bytes 6291456 | tf_op jit(solution)/shard_map/substeps/pallas_call | solution.py:212
  26.4 0.0 collective-permute-done.4.clo_ref
  26.4 0.0 collective-permute-done.5.chi_ref
  26.4 0.0 copy-done.2
  26.4 5.9 %sample_and_gram.1 = (f32[3,16,32,512]{3,2,1,0:T(8,128)}, f32[3,2,32,512]{3,2,1,0:T(8,128)S(1)}, f32[3,2048,128]{2,1,0:T(8,128)S(1)}, f32[64,3072]{1,0:T(8,128)S...) custom-call(s32[1024]{0:T(1024)S(1)} %copy-done.2, ...), custom_call_target="tpu_custom_call", output_to_operand_aliasing={{0}: (13, {}), {1}: (14, {}), {2}: (15, {})} | custom-call | flops 15728640 | bytes 1572864 | tf_op jit(solution)/shard_map/sample_and_gram/pallas_call | solution.py:350
  32.3 0.1 collective-permute-start.6
  32.4 1.2 %collective-permute-done.6 = f32[96,128]{1,0:T(8,128)S(1)} collective-permute-done((f32[96,128]{1,0:T(8,128)S(1)}, f32[96,128]{1,0:T(8,128)S(1)}, u32[]{:S(2)}, u32[]{:S(2)}) %collective-permute-start.6) | collective-permute-done | bytes 49184 | tf_op jit(solution)/shard_map/ppermute | solution.py:524
  33.6 0.6 collective-permute-start.7
  34.2 3.6 %collective-permute-done.7 = f32[96,128]{1,0:T(8,128)S(1)} collective-permute-done((f32[96,128]{1,0:T(8,128)S(1)}, f32[96,128]{1,0:T(8,128)S(1)}, u32[]{:S(2)}, u32[]{:S(2)}) %collective-permute-start.7) | collective-permute-done | bytes 49184 | tf_op jit(solution)/shard_map/ppermute | solution.py:528
  37.8 0.3 collective-permute-start.8
  38.1 3.8 %collective-permute-done.8 = f32[96,128]{1,0:T(8,128)S(1)} collective-permute-done((f32[96,128]{1,0:T(8,128)S(1)}, f32[96,128]{1,0:T(8,128)S(1)}, u32[]{:S(2)}, u32[]{:S(2)}) %collective-permute-start.8) | collective-permute-done | bytes 49184 | tf_op jit(solution)/shard_map/ppermute | solution.py:528
  41.9 1.3 %collective-permute-start.9 = (f32[96,128]{1,0:T(8,128)S(1)}, f32[96,128]{1,0:T(8,128)S(1)}, u32[]{:S(2)}, u32[]{:S(2)}) collective-permute-start(f32[96,128]{1,0:T(8,128)S(1)} %add.17), channel_id=1, source_target_pairs={{0,8},{4,12},{8,0},{12,4},{16,24},{20,28},{24,16},{28,20},{1,9},{5... | collective-permute-start | bytes 147464 | tf_op jit(solution)/shard_map/ppermute | solution.py:528
  43.2 2.9 %collective-permute-done.9 = f32[96,128]{1,0:T(8,128)S(1)} collective-permute-done((f32[96,128]{1,0:T(8,128)S(1)}, f32[96,128]{1,0:T(8,128)S(1)}, u32[]{:S(2)}, u32[]{:S(2)}) %collective-permute-start.9) | collective-permute-done | bytes 49184 | tf_op jit(solution)/shard_map/ppermute | solution.py:528
  46.1 2.6 %collective-permute-start.10 = (f32[96,128]{1,0:T(8,128)S(1)}, f32[96,128]{1,0:T(8,128)S(1)}, u32[]{:S(2)}, u32[]{:S(2)}) collective-permute-start(f32[96,128]{1,0:T(8,128)S(1)} %add.18), channel_id=1, source_target_pairs={{0,16},{4,20},{8,24},{12,28},{16,0},{20,4},{24,8},{28,12},{1,17},{... | collective-permute-start | bytes 147464 | tf_op jit(solution)/shard_map/ppermute | solution.py:528
  48.6 2.5 %collective-permute-done.10 = f32[96,128]{1,0:T(8,128)S(1)} collective-permute-done((f32[96,128]{1,0:T(8,128)S(1)}, f32[96,128]{1,0:T(8,128)S(1)}, u32[]{:S(2)}, u32[]{:S(2)}) %collective-permute-start.10) | collective-permute-done | bytes 49184 | tf_op jit(solution)/shard_map/ppermute | solution.py:528
  51.1 0.1 collective-permute-start.11
  51.2 1.2 %collective-permute-done.11.other_ref = f32[96,128]{1,0:T(8,128)S(1)} collective-permute-done((f32[96,128]{1,0:T(8,128)S(1)}, f32[96,128]{1,0:T(8,128)S(1)}, u32[]{:S(2)}, u32[]{:S(2)}) %collective-permute-start.11) | collective-permute-done | bytes 49184 | tf_op jit(solution)/shard_map/ppermute | solution.py:530
  52.4 10.8 %factor_and_basis.1 = (f32[192,192]{1,0:T(8,128)}, f32[192,3072]{1,0:T(8,128)}) custom-call(f32[1,128]{1,0:T(1,128)S(1)} %bitcast.3, f32[96,128]{1,0:T(8,128)S(1)} %add.19.mine_ref, f32[96,128]{1,0:T(8,128)S(1)} %collective-permute-done.11.other_ref, f32[128,3072]{1,0:T(8,128)S(1)} %copy-done.1, f32[64,3072]{1,0:T(8,128)S(1)} %get-tuple-element.36.snaps_ref), custom_call_target="tpu_custom_call" | custom-call | flops 1358954496 | bytes 4718592 | tf_op jit(solution)/shard_map/factor_and_basis/pallas_call | solution.py:465
  (6 shorter events, 0.0 us)
Async XLA Ops:
  0.6 9.4 %copy-start.1 = (f32[128,3072]{1,0:T(8,128)S(1)}, f32[128,3072]{1,0:T(8,128)}, u32[]{:S(2)}) copy-start(f32[128,3072]{1,0:T(8,128)} %modes_ref.5) | copy-start | bytes 4718596
  0.6 9.4 %copy-start.3 = (s32[64]{0:T(128)S(1)}, s32[64]{0:T(128)}, u32[]{:S(2)}) copy-start(s32[64]{0:T(128)} %steps_ref.3) | copy-start | bytes 772
  0.7 9.4 %copy-start.5 = (f32[63,3072]{1,0:T(8,128)S(1)}, f32[63,3072]{1,0:T(8,128)}, u32[]{:S(2)}) copy-start(f32[63,3072]{1,0:T(8,128)} %history_ref.1) | copy-start | bytes 2322436
  0.7 9.3 %copy-start.4 = (f32[128]{0:T(128)S(1)}, f32[128]{0:T(128)}, u32[]{:S(2)}) copy-start(f32[128]{0:T(128)} %param.8) | copy-start | bytes 1540
  2.2 17.2 %copy-start = (f32[3,16,32,512]{3,2,1,0:T(8,128)S(1)}, f32[3,16,32,512]{3,2,1,0:T(8,128)}, u32[]{:S(2)}) copy-start(f32[3,16,32,512]{3,2,1,0:T(8,128)} %velocity_ref.3) | copy-start | bytes 9437188
  2.2 17.2 %collective-permute-start = (f32[3,2,32,512]{3,2,1,0:T(8,128)S(1)}, f32[3,2,32,512]{3,2,1,0:T(8,128)S(1)}, u32[]{:S(2)}, u32[]{:S(2)}) collective-permute-start(f32[3,2,32,512]{3,2,1,0:T(8,128)S(1)} %get-tuple-element.21), channel_id=1, source_target_pairs={{0,1},{1,2},{2,3},{3,0},{4,5},{5,6},{6,7},{7,4},{8,9},{9,10},{10,1... | collective-permute-start | bytes 1179656 | tf_op jit(solution)/shard_map/ppermute | solution.py:509
  2.7 16.7 %collective-permute-start.1 = (f32[3,2,32,512]{3,2,1,0:T(8,128)S(1)}, f32[3,2,32,512]{3,2,1,0:T(8,128)S(1)}, u32[]{:S(2)}, u32[]{:S(2)}) collective-permute-start(f32[3,2,32,512]{3,2,1,0:T(8,128)S(1)} %get-tuple-element.22), channel_id=1, source_target_pairs={{0,3},{1,0},{2,1},{3,2},{4,7},{5,4},{6,5},{7,6},{8,11},{9,8},{10,9... | collective-permute-start | bytes 1179656 | tf_op jit(solution)/shard_map/ppermute | solution.py:510
  4.7 10.7 %collective-permute-start.2 = (f32[3,16,2,512]{3,2,1,0:T(2,128)S(1)}, f32[3,16,2,512]{3,2,1,0:T(2,128)S(1)}, u32[]{:S(2)}, u32[]{:S(2)}) collective-permute-start(f32[3,16,2,512]{3,2,1,0:T(2,128)S(1)} %get-tuple-element.23), channel_id=1, source_target_pairs={{0,4},{4,8},{8,12},{12,16},{16,20},{20,24},{24,28},{28,0},{1,5},{5... | collective-permute-start | bytes 589832 | tf_op jit(solution)/shard_map/ppermute | solution.py:507
  7.0 10.6 %collective-permute-start.3 = (f32[3,16,2,512]{3,2,1,0:T(2,128)S(1)}, f32[3,16,2,512]{3,2,1,0:T(2,128)S(1)}, u32[]{:S(2)}, u32[]{:S(2)}) collective-permute-start(f32[3,16,2,512]{3,2,1,0:T(2,128)S(1)} %get-tuple-element.24), channel_id=1, source_target_pairs={{0,28},{4,0},{8,4},{12,8},{16,12},{20,16},{24,20},{28,24},{1,29},{... | collective-permute-start | bytes 589832 | tf_op jit(solution)/shard_map/ppermute | solution.py:508
  14.2 12.2 %copy-start.2 = (s32[1024]{0:T(1024)S(1)}, s32[1024]{0:T(1024)}, u32[]{:S(2)}) copy-start(s32[1024]{0:T(1024)} %ids_ref.1) | copy-start | bytes 12292
  17.6 8.8 %collective-permute-start.4 = (f32[3,2,512]{2,1,0:T(2,128)S(1)}, f32[3,2,512]{2,1,0:T(2,128)S(1)}, u32[]{:S(2)}, u32[]{:S(2)}) collective-permute-start(f32[3,2,512]{2,1,0:T(2,128)S(1)} %get-tuple-element.26.own_hi_ref), channel_id=1, source_target_pairs={{0,1},{1,2},{2,3},{3,0},{4,5},{5,6},{6,7},{7,4},{8,9},{9,10},{10,1... | collective-permute-start | bytes 36872 | tf_op jit(solution)/shard_map/ppermute | solution.py:516
  17.6 8.8 %collective-permute-start.5 = (f32[3,2,512]{2,1,0:T(2,128)S(1)}, f32[3,2,512]{2,1,0:T(2,128)S(1)}, u32[]{:S(2)}, u32[]{:S(2)}) collective-permute-start(f32[3,2,512]{2,1,0:T(2,128)S(1)} %get-tuple-element.27.own_lo_ref), channel_id=1, source_target_pairs={{0,3},{1,0},{2,1},{3,2},{4,7},{5,4},{6,5},{7,6},{8,11},{9,8},{10,9... | collective-permute-start | bytes 36872 | tf_op jit(solution)/shard_map/ppermute | solution.py:517
  32.3 1.3 %collective-permute-start.6 = (f32[96,128]{1,0:T(8,128)S(1)}, f32[96,128]{1,0:T(8,128)S(1)}, u32[]{:S(2)}, u32[]{:S(2)}) collective-permute-start(f32[96,128]{1,0:T(8,128)S(1)} %get-tuple-element.35), channel_id=1, source_target_pairs={{0,1},{1,0},{2,3},{3,2},{4,5},{5,4},{6,7},{7,6},{8,9},{9,8},{10,11... | collective-permute-start | bytes 147464 | tf_op jit(solution)/shard_map/ppermute | solution.py:524
  33.6 4.2 %collective-permute-start.7 = (f32[96,128]{1,0:T(8,128)S(1)}, f32[96,128]{1,0:T(8,128)S(1)}, u32[]{:S(2)}, u32[]{:S(2)}) collective-permute-start(f32[96,128]{1,0:T(8,128)S(1)} %add.15), channel_id=1, source_target_pairs={{0,2},{1,3},{2,0},{3,1},{4,6},{5,7},{6,4},{7,5},{8,10},{9,11},{10,... | collective-permute-start | bytes 147464 | tf_op jit(solution)/shard_map/ppermute | solution.py:528
  37.8 4.2 %collective-permute-start.8 = (f32[96,128]{1,0:T(8,128)S(1)}, f32[96,128]{1,0:T(8,128)S(1)}, u32[]{:S(2)}, u32[]{:S(2)}) collective-permute-start(f32[96,128]{1,0:T(8,128)S(1)} %add.16), channel_id=1, source_target_pairs={{0,4},{4,0},{8,12},{12,8},{16,20},{20,16},{24,28},{28,24},{1,5},{5... | collective-permute-start | bytes 147464 | tf_op jit(solution)/shard_map/ppermute | solution.py:528
  41.9 4.2 %collective-permute-start.9 = (f32[96,128]{1,0:T(8,128)S(1)}, f32[96,128]{1,0:T(8,128)S(1)}, u32[]{:S(2)}, u32[]{:S(2)}) collective-permute-start(f32[96,128]{1,0:T(8,128)S(1)} %add.17), channel_id=1, source_target_pairs={{0,8},{4,12},{8,0},{12,4},{16,24},{20,28},{24,16},{28,20},{1,9},{5... | collective-permute-start | bytes 147464 | tf_op jit(solution)/shard_map/ppermute | solution.py:528
  46.1 5.0 %collective-permute-start.10 = (f32[96,128]{1,0:T(8,128)S(1)}, f32[96,128]{1,0:T(8,128)S(1)}, u32[]{:S(2)}, u32[]{:S(2)}) collective-permute-start(f32[96,128]{1,0:T(8,128)S(1)} %add.18), channel_id=1, source_target_pairs={{0,16},{4,20},{8,24},{12,28},{16,0},{20,4},{24,8},{28,12},{1,17},{... | collective-permute-start | bytes 147464 | tf_op jit(solution)/shard_map/ppermute | solution.py:528
  51.1 1.3 %collective-permute-start.11 = (f32[96,128]{1,0:T(8,128)S(1)}, f32[96,128]{1,0:T(8,128)S(1)}, u32[]{:S(2)}, u32[]{:S(2)}) collective-permute-start(f32[96,128]{1,0:T(8,128)S(1)} %add.19.mine_ref), channel_id=1, source_target_pairs={{0,1},{1,0},{2,3},{3,2},{4,5},{5,4},{6,7},{7,6},{8,9},{9,8},{10,11... | collective-permute-start | bytes 147464 | tf_op jit(solution)/shard_map/ppermute | solution.py:530

commit v3 on v2

--- a/solution.py
+++ b/solution.py
@@ -13,6 +13,7 @@
 HIGHEST = lax.Precision.HIGHEST
 LANES = 128
 GROUP = 16
+PARTS = 3
 
 
 def in_hbm(array):
@@ -377,111 +378,112 @@
     )
 
 
-def eliminate(block):
-    n = block.shape[0]
-    eye = (
-        lax.broadcasted_iota(jnp.int32, (n, n), 0) == lax.broadcasted_iota(jnp.int32, (n, n), 1)
-    ).astype(jnp.float32)
-    table = jnp.concatenate([block, eye], axis=1)
-    width = table.shape[1]
+def eliminate(pieces, start):
+    n = pieces[0].shape[0]
     done = []
     base = 0
     for j in range(0, n, GROUP):
-        first = (j // 8) * 8
-        if first > base:
-            done.append(table[: first - base])
-            table = table[first - base :]
-            base = first
+        if j > base:
+            done.append([piece[: j - base] for piece in pieces])
+            pieces = [piece[j - base :] for piece in pieces]
+            base = j
         h = n - base
-        rows = lax.broadcasted_iota(jnp.int32, (h, width), 0) + base
-        spread = [jnp.broadcast_to(table[:, j + k : j + k + 1], (h, width)) for k in range(GROUP)]
+        rows = lax.broadcasted_iota(jnp.int32, (h, LANES), 0) + base
+        spread = []
         for k in range(GROUP):
-            i = j + k - base
-            ratio = jnp.where(rows > j + k, spread[k] * (1.0 / spread[k][i : i + 1, :]), 0.0)
+            column = start + j + k
+            spread.append(jnp.broadcast_to(pieces[0][:, column : column + 1], (h, LANES)))
+        for k in range(GROUP):
+            pivot = spread[k][k : k + 1, :]
+            ratio = jnp.where(rows > j + k, spread[k], 0.0) * (1.0 / pivot)
             for l in range(k + 1, GROUP):
-                spread[l] = spread[l] - ratio * spread[l][i : i + 1, :]
-            table = table - ratio * table[i : i + 1, :]
-    done.append(table)
-    table = jnp.concatenate(done, axis=0)
-    pivots = jnp.sum(table[:, :n] * eye, axis=1, keepdims=True)
-    table = table * lax.rsqrt(pivots)
-    upper = lax.broadcasted_iota(jnp.int32, (n, n), 1) >= lax.broadcasted_iota(jnp.int32, (n, n), 0)
-    return jnp.where(upper, table[:, :n], 0.0), table[:, n:]
-
-
-def basis_kernel(root, w_ref, mine_ref, other_ref, modes_ref, snaps_ref, factor_ref, basis_ref, packed, inverse):
-    total = factor_ref.shape[0]
+                spread[l] = spread[l] - ratio * spread[l][k : k + 1, :]
+            pieces = [piece - ratio * piece[k : k + 1, :] for piece in pieces]
+    done.append(pieces)
+    pieces = [jnp.concatenate([d[q] for d in done], axis=0) for q in range(len(pieces))]
+    row = lax.broadcasted_iota(jnp.int32, (n, LANES), 0)
+    lane = lax.broadcasted_iota(jnp.int32, (n, LANES), 1)
+    pivots = jnp.sum(jnp.where(lane == row + start, pieces[0], 0.0), axis=1, keepdims=True)
+    scale = lax.rsqrt(pivots)
+    return [piece * scale for piece in pieces]
+
+
+def basis_kernel(
+    root, w_ref, mine_ref, other_ref, modes_ref, snaps_ref, factor_ref, basis_ref, packed, inverse, factor, basis, sems
+):
+    total = factor.shape[0]
     half = total // 3
     two = 2 * half
-
-    @pl.when(pl.program_id(0) == 0)
-    def _():
-        part = mine_ref.shape[0]
-        core = lax.axis_index("grp") & 1
-        packed[pl.ds(pl.multiple_of(core * part, 8), part), :] = mine_ref[...]
-        packed[pl.ds(pl.multiple_of((1 - core) * part, 8), part), :] = other_ref[...]
-        a00 = packed[two:, 0:half]
-        a22 = packed[two:, half:two]
-        u00, m00 = eliminate(a00)
-        w0 = dot(m00, packed[0:half, :])
-        w01, w02 = w0[:, 0:half], w0[:, half:two]
-        a1 = packed[half:two, :] - dot(w01, w0, 0, 0)
-        u11, m11 = eliminate(a1[:, 0:half])
-        w12 = dot(m11, a1[:, half:two])
-        a22 = a22 - dot(w02, w02, 0, 0) - dot(w12, w12, 0, 0)
-        m10 = -dot(m11, dot(w01, m00, 0, 0))
-        u22, m22 = eliminate(a22)
-        m20 = -dot(m22, dot(w02, m00, 0, 0) + dot(w12, m10, 0, 0))
-        m21 = -dot(m22, dot(w12, m11, 0, 0))
-        zero = jnp.zeros((half, half), jnp.float32)
-        scale = 1.0 / root
-        factor_ref[0:half, 0:half] = u00 * scale
-        factor_ref[0:half, half:two] = w01 * scale
-        factor_ref[0:half, two:] = w02 * scale
-        factor_ref[half:two, 0:half] = zero
-        factor_ref[half:two, half:two] = u11 * scale
-        factor_ref[half:two, two:] = w12 * scale
-        factor_ref[two:, 0:half] = zero
-        factor_ref[two:, half:two] = zero
-        factor_ref[two:, two:] = u22 * scale
-        wide = w_ref[...] * root
-        inverse[0:half, 0:two] = jnp.concatenate([m00, zero], axis=1) * wide
-        inverse[half:two, 0:two] = jnp.concatenate([m10, m11], axis=1) * wide
-        inverse[two:, 0:two] = jnp.concatenate([m20, m21], axis=1) * wide
-        inverse[0:half, two:total] = zero
-        inverse[half:two, two:total] = zero
-        inverse[two:, two:total] = m22 * root
-
-    rows = jnp.concatenate([modes_ref[...], snaps_ref[...]], axis=0)
-    basis_ref[...] = dot(inverse[:, 0:total], rows)
+    part = mine_ref.shape[0]
+    core = lax.axis_index("grp") & 1
+    packed[pl.ds(pl.multiple_of(core * part, 8), part), :] = mine_ref[...]
+    packed[pl.ds(pl.multiple_of((1 - core) * part, 8), part), :] = other_ref[...]
+    row = lax.broadcasted_iota(jnp.int32, (half, LANES), 0)
+    lane = lax.broadcasted_iota(jnp.int32, (half, LANES), 1)
+    left = lane < half
+    eye = (row == lane).astype(jnp.float32)
+    eye_right = (row + half == lane).astype(jnp.float32)
+    ends = packed[two:, :]
+    r0, w0 = eliminate([jnp.where(left, ends, eye_right), packed[0:half, :]], 0)
+    d = dot(w0, jnp.concatenate([r0, w0], axis=1), 0, 0)
+    r1, m1 = eliminate([packed[half:two, :] - d[0:half, LANES:], jnp.where(left, eye, -d[0:half, 0:LANES])], 0)
+    e = dot(r1, jnp.concatenate([r1, m1], axis=1), 0, 0)[half:two]
+    r2, m2 = eliminate(
+        [
+            jnp.where(left, eye, ends - d[half:two, LANES:] - e[:, 0:LANES]),
+            jnp.where(left, 0.0, -d[half:two, 0:LANES]) - e[:, LANES:],
+        ],
+        half,
+    )
+    wide = pltpu.roll(w_ref[...], half, 1) * root
+    inverse[0:half, 0:two] = jnp.where(left, 0.0, r0) * wide
+    inverse[half:two, 0:two] = m1 * wide
+    inverse[two:, 0:two] = m2 * wide
+    zero = jnp.zeros((half, half), jnp.float32)
+    inverse[0:half, two:total] = zero
+    inverse[half:two, two:total] = zero
+    inverse[two:, two:total] = r2[:, 0:half] * root
+    scale = 1.0 / root
+    factor[0:half, 0:half] = jnp.where(row <= lane, r0, 0.0)[:, 0:half] * scale
+    factor[0:half, half:] = w0 * scale
+    factor[half:two, 0:half] = zero
+    factor[half:two, half:] = jnp.where(row <= lane, r1, 0.0) * scale
+    factor[two:, 0:half] = zero
+    factor[two:, half:two] = zero
+    factor[two:, two:] = jnp.where(row + half <= lane, r2, 0.0)[:, half:] * scale
+    copies = [pltpu.make_async_copy(factor, factor_ref, sems.at[0])]
+    copies[0].start()
+    width = basis.shape[1]
+    parts = sems.shape[0] - 1
+    chunk = width // parts
+    for i in range(parts):
+        at = slice(i * chunk, (i + 1) * chunk)
+        rows = jnp.concatenate([modes_ref[half:two, at], modes_ref[0:half, at], snaps_ref[:, at]], axis=0)
+        basis[:, at] = dot(inverse[:, 0:total], rows)
+        copies.append(pltpu.make_async_copy(basis.at[:, at], basis_ref.at[:, at], sems.at[i + 1]))
+        copies[-1].start()
+    for copy in copies:
+        copy.wait()
 
 
 def basis_call(root, weights, mine, other, modes, snaps):
     k, width = modes.shape
-    count = snaps.shape[0]
-    total = k + count
-    chunk = 512
-    whole = lambda shape: pl.BlockSpec(shape, lambda i: (0, 0))
+    total = k + snaps.shape[0]
+    vmem = pl.BlockSpec(memory_space=pltpu.VMEM)
+    hbm = pl.BlockSpec(memory_space=pl.ANY)
     return pl.pallas_call(
         functools.partial(basis_kernel, root),
-        grid=(width // chunk,),
-        in_specs=[
-            whole(weights.shape),
-            whole(mine.shape),
-            whole(other.shape),
-            pl.BlockSpec((k, chunk), lambda i: (0, i)),
-            pl.BlockSpec((count, chunk), lambda i: (0, i)),
-        ],
-        out_specs=[whole((total, total)), pl.BlockSpec((total, chunk), lambda i: (0, i))],
-        out_shape=[
-            jax.ShapeDtypeStruct((total, total), jnp.float32),
-            jax.ShapeDtypeStruct((total, width), jnp.float32),
-        ],
+        in_specs=[vmem] * 5,
+        out_specs=[hbm, hbm],
+        out_shape=[pltpu.HBM((total, total), jnp.float32), pltpu.HBM((total, width), jnp.float32)],
         scratch_shapes=[
             pltpu.VMEM((total, LANES), jnp.float32),
             pltpu.VMEM((total, 2 * LANES), jnp.float32),
-        ],
-        compiler_params=pltpu.CompilerParams(vmem_limit_bytes=10 * 2**20),
+            pltpu.VMEM((total, total), jnp.float32),
+            pltpu.VMEM((total, width), jnp.float32),
+            pltpu.SemaphoreType.DMA((PARTS + 1,)),
+        ],
+        compiler_params=pltpu.CompilerParams(vmem_limit_bytes=16 * 2**20),
         cost_estimate=pl.CostEstimate(
             flops=12 * total * total * width, bytes_accessed=8 * total * width, transcendentals=0
         ),
@@ -496,8 +498,9 @@
     return forward, backward
 
 
-def swap(axis, bit):
-    return [(i, i ^ bit) for i in range(lax.axis_size(axis))]
+def swap(array, bits):
+    devices = lax.axis_size("tile") * lax.axis_size("grp")
+    return lax.ppermute(array, ("tile", "grp"), [(i, i ^ bits) for i in range(devices)])
 
 
 def per_device(velocity, modes, mode_weights, history, slab_ids, snap_steps):
@@ -521,16 +524,18 @@
         slab_ids, snap_steps, weights, xlo, xhi, clo, chi, clow, chigh, p1, modes, snaps, gram, advanced, ends, flat
     )
 
-    mine = mine + lax.ppermute(other, "grp", swap("grp", 1))
-    for axis, first in (("grp", 2), ("tile", 1)):
-        bit = first
-        while bit < lax.axis_size(axis):
-            mine = mine + lax.ppermute(mine, axis, swap(axis, bit))
-            bit *= 2
-    other = lax.ppermute(mine, "grp", swap("grp", 1))
-
-    total_rows = modes.shape[1] * lax.axis_size("tile") * lax.axis_size("grp")
-    root = math.sqrt(total_rows)
+    devices = lax.axis_size("tile") * lax.axis_size("grp")
+    mine = mine + swap(other, 1)
+    bit = 2
+    while bit < devices:
+        total = mine + swap(mine, bit)
+        if 2 * bit < devices:
+            total = total + (swap(mine, 2 * bit) + swap(mine, 3 * bit))
+        mine = total
+        bit *= 4
+    other = swap(mine, 1)
+
+    root = math.sqrt(modes.shape[1] * devices)
     factor, basis = basis_call(root, weights, mine, other, modes, snaps)
     return (advanced, basis, factor)
 

time: 63.3 us -> 57.9 us (0.915)
  waiting for transfers between devices: 18.5 us -> 12.3 us
  starting transfers between devices: 14.5 us -> 17.7 us
  Pallas kernels: 29.3 us -> 26.7 us
    ppermute x6 -> x8, waiting for transfers between devices: 15.1 us -> 8.9 us  [swap(): lax.ppermute(array, ('tile', 'grp'), [(i, i ^ bits) for i in range(device...]
    ppermute x6 -> x8, starting transfers between devices: 4.94 us -> 8.14 us  [swap(): lax.ppermute(array, ('tile', 'grp'), [(i, i ^ bits) for i in range(device...]
    pallas_call x1, Pallas kernels: 10.8 us -> 8.21 us  [basis_call(): pl.pallas_call(functools.partial(basis_kernel, root), in_specs=[vmem] * 5...]
  transfers between devices with their start and end apart: 12 -> 14, of which waited for: 8 -> 8; matrix products, arithmetic and copies ran while one was open for 0% -> 0% of each run, Pallas kernels for 18% -> 19%
where the time goes in v3:
time: 57.9 us; the launch traced here: 57.8 us
  Pallas kernels  26.7 us (46%)
  starting transfers between devices  17.7 us (31%)
  waiting for transfers between devices  12.3 us (21%)
  between operations  0.94 us (2%)
    ppermute x8, waiting for transfers between devices, swap(): lax.ppermute(array, ('tile', 'grp'), [(i, i ^ bits) for i in range(device...  8.9 us
    pallas_call x1, Pallas kernels, basis_call(): pl.pallas_call(functools.partial(basis_kernel, root), in_specs=[vmem] * 5...  8.21 us
    ppermute x8, starting transfers between devices, swap(): lax.ppermute(array, ('tile', 'grp'), [(i, i ^ bits) for i in range(device...  8.14 us
    pallas_call x1, Pallas kernels, field_call(): pl.pallas_call(field_kernel, in_specs=[vmem] * 5, out_specs=[pl.BlockSpec...  6.99 us
    pallas_call x1, Pallas kernels, sample_call(): pl.pallas_call(sample_kernel, in_specs=[smem] * 2 + [vmem] * 11 + [hbm, v...  5.89 us
    pallas_call x1, Pallas kernels, early_gram(): pl.pallas_call(gram_kernel, in_specs=[pl.BlockSpec(memory_space=pltpu.SME...  4.12 us
    ppermute x1, starting transfers between devices, per_device(): yhi = lax.ppermute(ylow, 'tile', down_y)  3.04 us
    ppermute x1, starting transfers between devices, per_device(): ylo = lax.ppermute(yhigh, 'tile', up_y)  2.27 us
  transfers between devices with their start and end apart: 14, of which 8 were waited for; matrix products, arithmetic and copies ran while one was open for 0% of the time, Pallas kernels for 19%

profile of v3, /device:TPU:0, one launch (start us, length us, event | category | flops | bytes accessed | tf_op | source)
XLA Modules:
  0.0 57.8 jit_solution(6198525516418568252)
XLA Ops:
  0.6 0.0 copy-start.1
  0.6 0.0 copy-start.3
  0.7 0.0 copy-start.5
  0.7 0.0 copy-start.4
  0.7 1.5 %faces.1 = (f32[3,16,2,512]{3,2,1,0:T(2,128)S(1)}, f32[3,16,2,512]{3,2,1,0:T(2,128)S(1)}, f32[3,2,32,512]{3,2,1,0:T(8,128)S(1)}, f32[3,2,32,512]{3,2,1,0:T(8,128)S(1)}) custom-call(f32[3,16,32,512]{3,2,1,0:T(8,128)} %velocity_ref.3), custom_call_target="tpu_custom_call" | custom-call | tf_op jit(solution)/shard_map/faces/pallas_call | solution.py:52
  2.2 0.0 copy-start
  2.2 0.5 collective-permute-start
  2.7 2.0 %collective-permute-start.1 = (f32[3,2,32,512]{3,2,1,0:T(8,128)S(1)}, f32[3,2,32,512]{3,2,1,0:T(8,128)S(1)}, u32[]{:S(2)}, u32[]{:S(2)}) collective-permute-start(f32[3,2,32,512]{3,2,1,0:T(8,128)S(1)} %get-tuple-element.22), channel_id=1, source_target_pairs={{0,3},{1,0},{2,1},{3,2},{4,7},{5,4},{6,5},{7,6},{8,11},{9,8},{10,9... | collective-permute-start | bytes 1179656 | tf_op jit(solution)/shard_map/ppermute | solution.py:513
  4.7 2.3 %collective-permute-start.2 = (f32[3,16,2,512]{3,2,1,0:T(2,128)S(1)}, f32[3,16,2,512]{3,2,1,0:T(2,128)S(1)}, u32[]{:S(2)}, u32[]{:S(2)}) collective-permute-start(f32[3,16,2,512]{3,2,1,0:T(2,128)S(1)} %get-tuple-element.23), channel_id=1, source_target_pairs={{0,4},{4,8},{8,12},{12,16},{16,20},{20,24},{24,28},{28,0},{1,5},{5... | collective-permute-start | bytes 589832 | tf_op jit(solution)/shard_map/ppermute | solution.py:510
  7.0 3.0 %collective-permute-start.3 = (f32[3,16,2,512]{3,2,1,0:T(2,128)S(1)}, f32[3,16,2,512]{3,2,1,0:T(2,128)S(1)}, u32[]{:S(2)}, u32[]{:S(2)}) collective-permute-start(f32[3,16,2,512]{3,2,1,0:T(2,128)S(1)} %get-tuple-element.24), channel_id=1, source_target_pairs={{0,28},{4,0},{8,4},{12,8},{16,12},{20,16},{24,20},{28,24},{1,29},{... | collective-permute-start | bytes 589832 | tf_op jit(solution)/shard_map/ppermute | solution.py:511
  10.0 0.0 copy-done.1
  10.0 0.0 copy-done.3
  10.0 0.0 copy-done.5
  10.0 0.0 copy-done.4
  10.0 4.1 %early_gram.1 = (f32[192,192]{1,0:T(8,128)S(1)}, f32[64,3072]{1,0:T(8,128)S(1)}) custom-call(s32[64]{0:T(128)S(1)} %copy-done.3, f32[1,128]{1,0:T(1,128)S(1)} %bitcast.1, f32[128,3072]{1,0:T(8,128)S(1)} %copy-done.1, f32[63,3072]{1,0:T(8,128)S(1)} %copy-done.5), custom_call_target="tpu_custom_call" | custom-call | flops 1358954496 | bytes 7077888 | tf_op jit(solution)/shard_map/early_gram/pallas_call | solution.py:108
  14.1 0.0 copy-start.2
  14.1 1.2 %collective-permute-done.2.ylo_ref = f32[3,16,2,512]{3,2,1,0:T(2,128)S(1)} collective-permute-done((f32[3,16,2,512]{3,2,1,0:T(2,128)S(1)}, f32[3,16,2,512]{3,2,1,0:T(2,128)S(1)}, u32[]{:S(2)}, u32[]{:S(2)}) %collective-permute-start.2) | collective-permute-done | bytes 196640 | tf_op jit(solution)/shard_map/ppermute | solution.py:510
  15.4 2.2 %collective-permute-done.3.yhi_ref = f32[3,16,2,512]{3,2,1,0:T(2,128)S(1)} collective-permute-done((f32[3,16,2,512]{3,2,1,0:T(2,128)S(1)}, f32[3,16,2,512]{3,2,1,0:T(2,128)S(1)}, u32[]{:S(2)}, u32[]{:S(2)}) %collective-permute-start.3) | collective-permute-done | bytes 196640 | tf_op jit(solution)/shard_map/ppermute | solution.py:511
  17.6 0.1 collective-permute-start.4
  17.6 1.7 %collective-permute-start.5 = (f32[3,2,512]{2,1,0:T(2,128)S(1)}, f32[3,2,512]{2,1,0:T(2,128)S(1)}, u32[]{:S(2)}, u32[]{:S(2)}) collective-permute-start(f32[3,2,512]{2,1,0:T(2,128)S(1)} %get-tuple-element.27.own_lo_ref), channel_id=1, source_target_pairs={{0,3},{1,0},{2,1},{3,2},{4,7},{5,4},{6,5},{7,6},{8,11},{9,8},{10,9... | collective-permute-start | bytes 36872 | tf_op jit(solution)/shard_map/ppermute | solution.py:520
  19.4 0.0 collective-permute-done.xlo_ref
  19.4 0.0 collective-permute-done.1.xhi_ref
  19.4 0.0 copy-done
  19.4 7.0 %substeps.1 = (f32[3,16,32,512]{3,2,1,0:T(8,128)}, f32[3,18,40,512]{3,2,1,0:T(8,128)S(1)}, f32[3,2,32,512]{3,2,1,0:T(8,128)S(1)}, f32[3,2048,128]{2,1,0:T(8,128)S(1)}) custom-call(f32[3,16,32,512]{3,2,1,0:T(8,128)S(1)} %copy-done, f32[3,2,32,512]{3,2,1,0:T(8,128)S(1)} %collective-permute-done.xlo_ref, f32[3,2,32,512]{3,2,1,0:T(8,128)S(1)} %collective-permute-done.1.xhi_ref, ...), custom_call_target="tpu_custom_call" | custom-call | flops 47185920 | bytes 6291456 | tf_op jit(solution)/shard_map/substeps/pallas_call | solution.py:213
  26.4 0.0 collective-permute-done.4.clo_ref
  26.4 0.0 collective-permute-done.5.chi_ref
  26.4 0.0 copy-done.2
  26.4 5.9 %sample_and_gram.1 = (f32[3,16,32,512]{3,2,1,0:T(8,128)}, f32[3,2,32,512]{3,2,1,0:T(8,128)S(1)}, f32[3,2048,128]{2,1,0:T(8,128)S(1)}, f32[64,3072]{1,0:T(8,128)S...) custom-call(s32[1024]{0:T(1024)S(1)} %copy-done.2, ...), custom_call_target="tpu_custom_call", output_to_operand_aliasing={{0}: (13, {}), {1}: (14, {}), {2}: (15, {})} | custom-call | flops 15728640 | bytes 1572864 | tf_op jit(solution)/shard_map/sample_and_gram/pallas_call | solution.py:351
  32.3 0.1 collective-permute-start.6
  32.4 1.2 %collective-permute-done.6 = f32[96,128]{1,0:T(8,128)S(1)} collective-permute-done((f32[96,128]{1,0:T(8,128)S(1)}, f32[96,128]{1,0:T(8,128)S(1)}, u32[]{:S(2)}, u32[]{:S(2)}) %collective-permute-start.6) | collective-permute-done | bytes 49184 | tf_op jit(solution)/shard_map/ppermute | solution.py:503
  33.6 0.3 collective-permute-start.9
  33.9 1.7 %collective-permute-start.8 = (f32[96,128]{1,0:T(8,128)S(1)}, f32[96,128]{1,0:T(8,128)S(1)}, u32[]{:S(2)}, u32[]{:S(2)}) collective-permute-start(f32[96,128]{1,0:T(8,128)S(1)} %add.21), channel_id=1, source_target_pairs={{0,4},{1,5},{2,6},{3,7},{4,0},{5,1},{6,2},{7,3},{8,12},{9,13},{10,... | collective-permute-start | bytes 147464 | tf_op jit(solution)/shard_map/ppermute | solution.py:503
  35.7 1.5 %collective-permute-start.7 = (f32[96,128]{1,0:T(8,128)S(1)}, f32[96,128]{1,0:T(8,128)S(1)}, u32[]{:S(2)}, u32[]{:S(2)}) collective-permute-start(f32[96,128]{1,0:T(8,128)S(1)} %add.21), channel_id=1, source_target_pairs={{0,2},{1,3},{2,0},{3,1},{4,6},{5,7},{6,4},{7,5},{8,10},{9,11},{10,... | collective-permute-start | bytes 147464 | tf_op jit(solution)/shard_map/ppermute | solution.py:503
  37.2 1.7 %collective-permute-done.9 = f32[96,128]{1,0:T(8,128)S(1)} collective-permute-done((f32[96,128]{1,0:T(8,128)S(1)}, f32[96,128]{1,0:T(8,128)S(1)}, u32[]{:S(2)}, u32[]{:S(2)}) %collective-permute-start.9) | collective-permute-done | bytes 49184 | tf_op jit(solution)/shard_map/ppermute | solution.py:503
  38.8 0.0 collective-permute-done.8
  38.8 0.9 %collective-permute-done.7 = f32[96,128]{1,0:T(8,128)S(1)} collective-permute-done((f32[96,128]{1,0:T(8,128)S(1)}, f32[96,128]{1,0:T(8,128)S(1)}, u32[]{:S(2)}, u32[]{:S(2)}) %collective-permute-start.7) | collective-permute-done | bytes 49184 | tf_op jit(solution)/shard_map/ppermute | solution.py:503
  39.8 3.3 %collective-permute-start.12 = (f32[96,128]{1,0:T(8,128)S(1)}, f32[96,128]{1,0:T(8,128)S(1)}, u32[]{:S(2)}, u32[]{:S(2)}) collective-permute-start(f32[96,128]{1,0:T(8,128)S(1)} %add_add_fusion.1), channel_id=1, source_target_pairs={{0,24},{1,25},{2,26},{3,27},{4,28},{5,29},{6,30},{7,31},{8,16},{9,... | collective-permute-start | bytes 147464 | tf_op jit(solution)/shard_map/ppermute | solution.py:503
  43.1 0.0 collective-permute-start.11
  43.1 1.1 %collective-permute-start.10 = (f32[96,128]{1,0:T(8,128)S(1)}, f32[96,128]{1,0:T(8,128)S(1)}, u32[]{:S(2)}, u32[]{:S(2)}) collective-permute-start(f32[96,128]{1,0:T(8,128)S(1)} %add_add_fusion.1), channel_id=1, source_target_pairs={{0,8},{1,9},{2,10},{3,11},{4,12},{5,13},{6,14},{7,15},{8,0},{9,1},... | collective-permute-start | bytes 147464 | tf_op jit(solution)/shard_map/ppermute | solution.py:503
  44.2 1.6 %collective-permute-done.12 = f32[96,128]{1,0:T(8,128)S(1)} collective-permute-done((f32[96,128]{1,0:T(8,128)S(1)}, f32[96,128]{1,0:T(8,128)S(1)}, u32[]{:S(2)}, u32[]{:S(2)}) %collective-permute-start.12) | collective-permute-done | bytes 49184 | tf_op jit(solution)/shard_map/ppermute | solution.py:503
  45.8 2.3 %collective-permute-done.11 = f32[96,128]{1,0:T(8,128)S(1)} collective-permute-done((f32[96,128]{1,0:T(8,128)S(1)}, f32[96,128]{1,0:T(8,128)S(1)}, u32[]{:S(2)}, u32[]{:S(2)}) %collective-permute-start.11) | collective-permute-done | bytes 49184 | tf_op jit(solution)/shard_map/ppermute | solution.py:503
  48.1 0.0 collective-permute-done.10
  48.1 0.1 collective-permute-start.13
  48.2 1.2 %collective-permute-done.13.other_ref = f32[96,128]{1,0:T(8,128)S(1)} collective-permute-done((f32[96,128]{1,0:T(8,128)S(1)}, f32[96,128]{1,0:T(8,128)S(1)}, u32[]{:S(2)}, u32[]{:S(2)}) %collective-permute-start.13) | collective-permute-done | bytes 49184 | tf_op jit(solution)/shard_map/ppermute | solution.py:503
  49.4 8.2 %factor_and_basis.1 = (f32[192,192]{1,0:T(8,128)}, f32[192,3072]{1,0:T(8,128)}) custom-call(f32[1,128]{1,0:T(1,128)S(1)} %bitcast.3, f32[96,128]{1,0:T(8,128)S(1)} %add_add_fusion.mine_ref, f32[96,128]{1,0:T(8,128)S(1)} %collective-permute-done.13.other_ref, f32[128,3072]{1,0:T(8,128)S(1)} %copy-done.1, f32[64,3072]{1,0:T(8,128)S(1)} %get-tuple-element.36.snaps_ref), custom_call_target="tpu_custom_call" | custom-call | flops 1358954496 | bytes 4718592 | tf_op jit(solution)/shard_map/factor_and_basis/pallas_call | solution.py:474
  (4 shorter events, 0.0 us)
Async XLA Ops:
  0.6 9.4 %copy-start.1 = (f32[128,3072]{1,0:T(8,128)S(1)}, f32[128,3072]{1,0:T(8,128)}, u32[]{:S(2)}) copy-start(f32[128,3072]{1,0:T(8,128)} %modes_ref.5) | copy-start | bytes 4718596
  0.6 9.4 %copy-start.3 = (s32[64]{0:T(128)S(1)}, s32[64]{0:T(128)}, u32[]{:S(2)}) copy-start(s32[64]{0:T(128)} %steps_ref.3) | copy-start | bytes 772
  0.7 9.4 %copy-start.5 = (f32[63,3072]{1,0:T(8,128)S(1)}, f32[63,3072]{1,0:T(8,128)}, u32[]{:S(2)}) copy-start(f32[63,3072]{1,0:T(8,128)} %history_ref.1) | copy-start | bytes 2322436
  0.7 9.3 %copy-start.4 = (f32[128]{0:T(128)S(1)}, f32[128]{0:T(128)}, u32[]{:S(2)}) copy-start(f32[128]{0:T(128)} %param.8) | copy-start | bytes 1540
  2.2 17.2 %copy-start = (f32[3,16,32,512]{3,2,1,0:T(8,128)S(1)}, f32[3,16,32,512]{3,2,1,0:T(8,128)}, u32[]{:S(2)}) copy-start(f32[3,16,32,512]{3,2,1,0:T(8,128)} %velocity_ref.3) | copy-start | bytes 9437188
  2.2 17.2 %collective-permute-start = (f32[3,2,32,512]{3,2,1,0:T(8,128)S(1)}, f32[3,2,32,512]{3,2,1,0:T(8,128)S(1)}, u32[]{:S(2)}, u32[]{:S(2)}) collective-permute-start(f32[3,2,32,512]{3,2,1,0:T(8,128)S(1)} %get-tuple-element.21), channel_id=1, source_target_pairs={{0,1},{1,2},{2,3},{3,0},{4,5},{5,6},{6,7},{7,4},{8,9},{9,10},{10,1... | collective-permute-start | bytes 1179656 | tf_op jit(solution)/shard_map/ppermute | solution.py:512
  2.7 16.7 %collective-permute-start.1 = (f32[3,2,32,512]{3,2,1,0:T(8,128)S(1)}, f32[3,2,32,512]{3,2,1,0:T(8,128)S(1)}, u32[]{:S(2)}, u32[]{:S(2)}) collective-permute-start(f32[3,2,32,512]{3,2,1,0:T(8,128)S(1)} %get-tuple-element.22), channel_id=1, source_target_pairs={{0,3},{1,0},{2,1},{3,2},{4,7},{5,4},{6,5},{7,6},{8,11},{9,8},{10,9... | collective-permute-start | bytes 1179656 | tf_op jit(solution)/shard_map/ppermute | solution.py:513
  4.7 10.7 %collective-permute-start.2 = (f32[3,16,2,512]{3,2,1,0:T(2,128)S(1)}, f32[3,16,2,512]{3,2,1,0:T(2,128)S(1)}, u32[]{:S(2)}, u32[]{:S(2)}) collective-permute-start(f32[3,16,2,512]{3,2,1,0:T(2,128)S(1)} %get-tuple-element.23), channel_id=1, source_target_pairs={{0,4},{4,8},{8,12},{12,16},{16,20},{20,24},{24,28},{28,0},{1,5},{5... | collective-permute-start | bytes 589832 | tf_op jit(solution)/shard_map/ppermute | solution.py:510
  7.0 10.6 %collective-permute-start.3 = (f32[3,16,2,512]{3,2,1,0:T(2,128)S(1)}, f32[3,16,2,512]{3,2,1,0:T(2,128)S(1)}, u32[]{:S(2)}, u32[]{:S(2)}) collective-permute-start(f32[3,16,2,512]{3,2,1,0:T(2,128)S(1)} %get-tuple-element.24), channel_id=1, source_target_pairs={{0,28},{4,0},{8,4},{12,8},{16,12},{20,16},{24,20},{28,24},{1,29},{... | collective-permute-start | bytes 589832 | tf_op jit(solution)/shard_map/ppermute | solution.py:511
  14.1 12.3 %copy-start.2 = (s32[1024]{0:T(1024)S(1)}, s32[1024]{0:T(1024)}, u32[]{:S(2)}) copy-start(s32[1024]{0:T(1024)} %ids_ref.1) | copy-start | bytes 12292
  17.6 8.8 %collective-permute-start.4 = (f32[3,2,512]{2,1,0:T(2,128)S(1)}, f32[3,2,512]{2,1,0:T(2,128)S(1)}, u32[]{:S(2)}, u32[]{:S(2)}) collective-permute-start(f32[3,2,512]{2,1,0:T(2,128)S(1)} %get-tuple-element.26.own_hi_ref), channel_id=1, source_target_pairs={{0,1},{1,2},{2,3},{3,0},{4,5},{5,6},{6,7},{7,4},{8,9},{9,10},{10,1... | collective-permute-start | bytes 36872 | tf_op jit(solution)/shard_map/ppermute | solution.py:519
  17.6 8.8 %collective-permute-start.5 = (f32[3,2,512]{2,1,0:T(2,128)S(1)}, f32[3,2,512]{2,1,0:T(2,128)S(1)}, u32[]{:S(2)}, u32[]{:S(2)}) collective-permute-start(f32[3,2,512]{2,1,0:T(2,128)S(1)} %get-tuple-element.27.own_lo_ref), channel_id=1, source_target_pairs={{0,3},{1,0},{2,1},{3,2},{4,7},{5,4},{6,5},{7,6},{8,11},{9,8},{10,9... | collective-permute-start | bytes 36872 | tf_op jit(solution)/shard_map/ppermute | solution.py:520
  32.3 1.3 %collective-permute-start.6 = (f32[96,128]{1,0:T(8,128)S(1)}, f32[96,128]{1,0:T(8,128)S(1)}, u32[]{:S(2)}, u32[]{:S(2)}) collective-permute-start(f32[96,128]{1,0:T(8,128)S(1)} %get-tuple-element.35), channel_id=1, source_target_pairs={{0,1},{1,0},{2,3},{3,2},{4,5},{5,4},{6,7},{7,6},{8,9},{9,8},{10,11... | collective-permute-start | bytes 147464 | tf_op jit(solution)/shard_map/ppermute | solution.py:503
  33.6 5.2 %collective-permute-start.9 = (f32[96,128]{1,0:T(8,128)S(1)}, f32[96,128]{1,0:T(8,128)S(1)}, u32[]{:S(2)}, u32[]{:S(2)}) collective-permute-start(f32[96,128]{1,0:T(8,128)S(1)} %add.21), channel_id=1, source_target_pairs={{0,6},{1,7},{2,4},{3,5},{4,2},{5,3},{6,0},{7,1},{8,14},{9,15},{10,... | collective-permute-start | bytes 147464 | tf_op jit(solution)/shard_map/ppermute | solution.py:503
  33.9 4.9 %collective-permute-start.8 = (f32[96,128]{1,0:T(8,128)S(1)}, f32[96,128]{1,0:T(8,128)S(1)}, u32[]{:S(2)}, u32[]{:S(2)}) collective-permute-start(f32[96,128]{1,0:T(8,128)S(1)} %add.21), channel_id=1, source_target_pairs={{0,4},{1,5},{2,6},{3,7},{4,0},{5,1},{6,2},{7,3},{8,12},{9,13},{10,... | collective-permute-start | bytes 147464 | tf_op jit(solution)/shard_map/ppermute | solution.py:503
  35.7 4.1 %collective-permute-start.7 = (f32[96,128]{1,0:T(8,128)S(1)}, f32[96,128]{1,0:T(8,128)S(1)}, u32[]{:S(2)}, u32[]{:S(2)}) collective-permute-start(f32[96,128]{1,0:T(8,128)S(1)} %add.21), channel_id=1, source_target_pairs={{0,2},{1,3},{2,0},{3,1},{4,6},{5,7},{6,4},{7,5},{8,10},{9,11},{10,... | collective-permute-start | bytes 147464 | tf_op jit(solution)/shard_map/ppermute | solution.py:503
  39.8 6.1 %collective-permute-start.12 = (f32[96,128]{1,0:T(8,128)S(1)}, f32[96,128]{1,0:T(8,128)S(1)}, u32[]{:S(2)}, u32[]{:S(2)}) collective-permute-start(f32[96,128]{1,0:T(8,128)S(1)} %add_add_fusion.1), channel_id=1, source_target_pairs={{0,24},{1,25},{2,26},{3,27},{4,28},{5,29},{6,30},{7,31},{8,16},{9,... | collective-permute-start | bytes 147464 | tf_op jit(solution)/shard_map/ppermute | solution.py:503
  43.1 5.0 %collective-permute-start.11 = (f32[96,128]{1,0:T(8,128)S(1)}, f32[96,128]{1,0:T(8,128)S(1)}, u32[]{:S(2)}, u32[]{:S(2)}) collective-permute-start(f32[96,128]{1,0:T(8,128)S(1)} %add_add_fusion.1), channel_id=1, source_target_pairs={{0,16},{1,17},{2,18},{3,19},{4,20},{5,21},{6,22},{7,23},{8,24},{9,... | collective-permute-start | bytes 147464 | tf_op jit(solution)/shard_map/ppermute | solution.py:503
  43.1 5.0 %collective-permute-start.10 = (f32[96,128]{1,0:T(8,128)S(1)}, f32[96,128]{1,0:T(8,128)S(1)}, u32[]{:S(2)}, u32[]{:S(2)}) collective-permute-start(f32[96,128]{1,0:T(8,128)S(1)} %add_add_fusion.1), channel_id=1, source_target_pairs={{0,8},{1,9},{2,10},{3,11},{4,12},{5,13},{6,14},{7,15},{8,0},{9,1},... | collective-permute-start | bytes 147464 | tf_op jit(solution)/shard_map/ppermute | solution.py:503
  48.1 1.3 %collective-permute-start.13 = (f32[96,128]{1,0:T(8,128)S(1)}, f32[96,128]{1,0:T(8,128)S(1)}, u32[]{:S(2)}, u32[]{:S(2)}) collective-permute-start(f32[96,128]{1,0:T(8,128)S(1)} %add_add_fusion.mine_ref), channel_id=1, source_target_pairs={{0,1},{1,0},{2,3},{3,2},{4,5},{5,4},{6,7},{7,6},{8,9},{9,8},{10,11... | collective-permute-start | bytes 147464 | tf_op jit(solution)/shard_map/ppermute | solution.py:503

commit v4 on v3

--- a/solution.py
+++ b/solution.py
@@ -60,65 +60,76 @@
     )(in_hbm(velocity))
 
 
-def corners_kernel(ylo_ref, yhi_ref, gram_ref, low_ref, high_ref):
-    nx = ylo_ref.shape[1]
-    for c in range(ylo_ref.shape[0]):
-        low_ref[c, 0:1, :] = ylo_ref[c, 0, 1:2, :]
-        low_ref[c, 1:2, :] = yhi_ref[c, 0, 0:1, :]
-        high_ref[c, 0:1, :] = ylo_ref[c, nx - 1, 1:2, :]
-        high_ref[c, 1:2, :] = yhi_ref[c, nx - 1, 0:1, :]
-
-
-def corners(ylo, yhi, gram):
-    comps, _, _, nz = ylo.shape
-    vmem = pl.BlockSpec(memory_space=pltpu.VMEM)
-    return pl.pallas_call(
-        corners_kernel,
-        in_specs=[vmem, vmem, pl.BlockSpec(memory_space=pl.ANY)],
-        out_specs=[vmem, vmem],
-        out_shape=[pltpu.VMEM((comps, 2, nz), jnp.float32)] * 2,
-        compiler_params=pltpu.CompilerParams(vmem_limit_bytes=4 * 2**20),
-        name="corners",
-    )(in_vmem(ylo), in_vmem(yhi), in_vmem(gram))
-
-
-def gram_kernel(steps_ref, w_ref, modes_ref, history_ref, gram_ref, snaps_ref):
+def split(array):
+    high = array.astype(jnp.bfloat16)
+    rest = array - high.astype(jnp.float32)
+    mid = rest.astype(jnp.bfloat16)
+    return high, mid, (rest - mid.astype(jnp.float32)).astype(jnp.bfloat16)
+
+
+def gram_kernel(
+    lines, steps_ref, w_ref, modes_ref, history_ref, ids_ref, gram_ref, snaps_ref, tall_ref, at_ref, mask_ref
+):
     k = modes_ref.shape[0]
     count = snaps_ref.shape[0]
     last = count - 1
+    place = jnp.int32(0)
     for j in range(count):
         step = steps_ref[j]
-        source = jnp.minimum(step, last - 1)
-        row = history_ref[pl.ds(source, 1), :]
+        place = jnp.where(step == last, j, place)
+        row = history_ref[pl.ds(jnp.minimum(step, last - 1), 1), :]
         snaps_ref[j : j + 1, :] = jnp.where(step == last, 0.0, row)
-    modes = modes_ref[...]
-    snaps = snaps_ref[...]
+    total = k + count
+    nt = (((1,), (1,)), ((), ()))
+    high, mid, low = split(jnp.concatenate([modes_ref[...], snaps_ref[...]], axis=0))
+    first = lax.dot_general(
+        jnp.concatenate([high, mid, low], axis=0), high, nt, preferred_element_type=jnp.float32
+    )
+    second = lax.dot_general(mid, mid, nt, preferred_element_type=jnp.float32)
+    side = first[total : 2 * total] + first[2 * total :]
+    gram = first[0:total] + (second + (side + jnp.transpose(side)))
     wide = jnp.broadcast_to(w_ref[...], (k, k))
     tall = jnp.transpose(wide)
-    gram_ref[0:k, 0:k] = dot(modes, modes, 1, 1) * wide * tall
-    gram_ref[0:k, k:] = dot(modes, snaps, 1, 1) * tall[:, 0:count]
+    tall_ref[...] = tall
+    gram_ref[0:k, 0:k] = gram[0:k, 0:k] * wide * tall
+    gram_ref[0:k, k:] = gram[0:k, k:] * tall[:, 0:count]
     gram_ref[k:, 0:k] = jnp.zeros((count, k), jnp.float32)
-    gram_ref[k:, k:] = dot(snaps, snaps, 1, 1)
-
-
-def early_gram(steps, weights, modes, history):
+    gram_ref[k:, k:] = gram[k:, k:]
+    ids = ids_ref[...]
+    groups = ids.shape[0]
+    tiles = lines[1]
+    line = lax.shift_right_logical(ids, int(math.log2(LANES)))
+    at_ref[0:groups, :] = (line & (tiles - 1)) * lines[0] + lax.shift_right_logical(line, int(math.log2(tiles)))
+    at_ref[groups:, :] = jnp.broadcast_to(place, (at_ref.shape[0] - groups, LANES))
+    lane = (ids & (LANES - 1)).astype(jnp.float32)
+    here = lax.broadcasted_iota(jnp.int32, (LANES, LANES), 1).astype(jnp.float32)
+    for i in range(groups):
+        there = jnp.transpose(jnp.broadcast_to(lane[i : i + 1, :], (LANES, LANES)))
+        mask_ref[i * LANES : (i + 1) * LANES, :] = (here == there).astype(jnp.float32)
+
+
+def early_gram(lines, steps, weights, modes, history, ids):
     k, width = modes.shape
     count = steps.shape[0]
     total = k + count
+    vmem = pl.BlockSpec(memory_space=pltpu.VMEM)
     return pl.pallas_call(
-        gram_kernel,
-        in_specs=[pl.BlockSpec(memory_space=pltpu.SMEM)] + [pl.BlockSpec(memory_space=pltpu.VMEM)] * 3,
-        out_specs=[pl.BlockSpec(memory_space=pltpu.VMEM)] * 2,
+        functools.partial(gram_kernel, lines),
+        in_specs=[pl.BlockSpec(memory_space=pltpu.SMEM)] + [vmem] * 4,
+        out_specs=[vmem] * 5,
         out_shape=[
             pltpu.VMEM((total, total), jnp.float32),
             pltpu.VMEM((count, width), jnp.float32),
+            pltpu.VMEM((k, k), jnp.float32),
+            pltpu.VMEM((ids.shape[0] + 8, LANES), jnp.int32),
+            pltpu.VMEM((ids.size, LANES), jnp.float32),
         ],
-        compiler_params=pltpu.CompilerParams(vmem_limit_bytes=10 * 2**20),
+        compiler_params=pltpu.CompilerParams(vmem_limit_bytes=16 * 2**20),
         cost_estimate=pl.CostEstimate(
-            flops=12 * total * total * width, bytes_accessed=12 * total * width, transcendentals=0
+            flops=8 * total * total * width, bytes_accessed=12 * total * width, transcendentals=0
         ),
         name="early_gram",
-    )(in_vmem(steps), in_vmem(weights), in_vmem(modes), in_vmem(history))
+    )(*(in_vmem(a) for a in (steps, weights, modes, history, ids)))
 
 
 def stencil(tile, which, inner, store):
@@ -143,19 +154,81 @@
             store(c, t, out)
 
 
-def field_kernel(
-    velocity_ref, xlo_ref, xhi_ref, ylo_ref, yhi_ref,
-    advanced_ref, p1, ends_ref, flat, ring_tile, u2, out_sems,
+def inner_kernel(velocity_ref, p1, flat, u2):
+    comps, nx, ny, nz = velocity_ref.shape
+    inner = ny // 8
+    zero = jnp.zeros((8, nz), jnp.float32)
+
+    def first_layer(x):
+        def tile(k, c, t):
+            if t == inner or (isinstance(x, int) and not 0 <= x + k < nx):
+                return zero
+            return velocity_ref[c, x + k, 8 * t : 8 * t + 8, :]
+
+        def store(c, t, value):
+            p1[c, x + 1, 8 * t : 8 * t + 8, :] = value
+
+        stencil(tile, range(inner), inner, store)
+
+    first_layer(0)
+
+    @pl.loop(1, nx - 1)
+    def _(x):
+        first_layer(x)
+
+    first_layer(nx - 1)
+
+    @pl.loop(2, nx - 2)
+    def _(x):
+        second_layer(p1, u2, flat, x, range(1, inner - 1))
+
+
+def second_layer(p1, u2, flat, x, which):
+    comps, nx, ny, nz = u2.shape
+
+    def tile(k, c, t):
+        return p1[c, x + 1 + k, 8 * t : 8 * t + 8, :]
+
+    def store(c, t, value):
+        u2[c, x, 8 * t : 8 * t + 8, :] = value
+        for k in range(nz // LANES):
+            at = (k * nx + x) * ny + 8 * t
+            flat[c, pl.ds(at if isinstance(at, int) else pl.multiple_of(at, 8), 8), :] = value[
+                :, k * LANES : (k + 1) * LANES
+            ]
+
+    stencil(tile, which, ny // 8, store)
+
+
+def halo_kernel(
+    velocity_ref, xlo_ref, xhi_ref, ylo_ref, yhi_ref, gram_ref, p1_in, p1, clow_ref, chigh_ref, ring_tile
 ):
     comps, nx, ny, nz = velocity_ref.shape
     inner = ny // 8
-    tiles = nz // LANES
+    adv = 0.5 * time_step
+    diff = time_step * viscosity
+    vel = velocity_ref
     for c in range(comps):
+        clow_ref[c, 0:1, :] = ylo_ref[c, 0, 1:2, :]
+        clow_ref[c, 1:2, :] = yhi_ref[c, 0, 0:1, :]
+        chigh_ref[c, 0:1, :] = ylo_ref[c, nx - 1, 1:2, :]
+        chigh_ref[c, 1:2, :] = yhi_ref[c, nx - 1, 0:1, :]
         for x in range(nx):
             ring_tile[c, x, 0:2, :] = yhi_ref[c, x]
             ring_tile[c, x, 6:8, :] = ylo_ref[c, x]
-
-    def first_layer(x, refs, layers, count):
+    for x in range(nx):
+        low = diff + adv * vel[1, x, 0:1, :]
+        high = diff - adv * vel[1, x, ny - 1 : ny, :]
+        for c in range(comps):
+            p1[c, x + 1, 0:1, :] = p1[c, x + 1, 0:1, :] + low * ylo_ref[c, x, 1:2, :]
+            p1[c, x + 1, ny - 1 : ny, :] = p1[c, x + 1, ny - 1 : ny, :] + high * yhi_ref[c, x, 0:1, :]
+    low = diff + adv * vel[0, 0]
+    high = diff - adv * vel[0, nx - 1]
+    for c in range(comps):
+        p1[c, 1, 0:ny, :] = p1[c, 1, 0:ny, :] + low * xlo_ref[c, 1]
+        p1[c, nx, 0:ny, :] = p1[c, nx, 0:ny, :] + high * xhi_ref[c, 0]
+
+    def layer(x, refs, layers, which):
         def tile(k, c, t):
             if t == inner:
                 if isinstance(x, int) and not 0 <= x + k < nx:
@@ -166,77 +239,107 @@
         def store(c, t, value):
             p1[c, x + 1, 8 * t : 8 * t + 8, :] = value
 
-        stencil(tile, range(count), inner, store)
-
-    vel = velocity_ref
-    first_layer(-1, (xlo_ref, xlo_ref, vel), (0, 1, 0), inner)
-    first_layer(0, (xlo_ref, vel, vel), (1, 0, 1), inner + 1)
+        stencil(tile, which, inner, store)
+
+    layer(-1, (xlo_ref, xlo_ref, vel), (0, 1, 0), range(inner))
+    layer(nx, (vel, xhi_ref, xhi_ref), (nx - 1, 0, 1), range(inner))
+    layer(0, (vel, vel, vel), (0, 0, 1), (inner,))
 
     @pl.loop(1, nx - 1)
     def _(x):
-        first_layer(x, (vel, vel, vel), (x - 1, x, x + 1), inner + 1)
-
-    first_layer(nx - 1, (vel, vel, xhi_ref), (nx - 2, nx - 1, 0), inner + 1)
-    first_layer(nx, (vel, xhi_ref, xhi_ref), (nx - 1, 0, 1), inner)
-
-    def second_layer(x, out, layer):
-        def tile(k, c, t):
-            return p1[c, x + 1 + k, 8 * t : 8 * t + 8, :]
-
-        def store(c, t, value):
-            out[c, layer, 8 * t : 8 * t + 8, :] = value
-            for k in range(tiles):
-                at = pl.multiple_of((k * nx + x) * ny + 8 * t, 8)
-                flat[c, pl.ds(at, 8), :] = value[:, k * LANES : (k + 1) * LANES]
-
-        stencil(tile, range(inner), inner, store)
+        layer(x, (vel, vel, vel), (x - 1, x, x + 1), (inner,))
+
+    layer(nx - 1, (vel, vel, vel), (nx - 2, nx - 1, nx - 1), (inner,))
+
+
+def outer_kernel(p1, flat_in, u2_in, flat, u2, advanced_ref, out_sems):
+    comps, nx, ny, nz = u2.shape
+    inner = ny // 8
 
     def out_copy(x):
         return pltpu.make_async_copy(u2.at[:, x], advanced_ref.at[:, x], out_sems.at[x])
 
-    @pl.loop(1, nx - 1)
+    @pl.loop(2, nx - 2)
     def _(x):
-        second_layer(x, u2, x)
+        second_layer(p1, u2, flat, x, (0, inner - 1))
         out_copy(x).start()
 
-    second_layer(0, ends_ref, 0)
-    second_layer(nx - 1, ends_ref, 1)
+    for x in (1, nx - 2):
+        second_layer(p1, u2, flat, x, range(inner))
+        out_copy(x).start()
+    for x in (0, nx - 1):
+        second_layer(p1, u2, flat, x, range(inner))
 
     @pl.loop(1, nx - 1)
     def _(x):
         out_copy(x).wait()
 
 
-def field_call(velocity, xlo, xhi, ylo, yhi):
+def spaces(velocity):
+    comps, nx, ny, nz = velocity.shape
+    return (
+        pltpu.VMEM((comps, nx + 2, ny + 8, nz), jnp.float32),
+        pltpu.VMEM((comps, nx * ny * nz // LANES, LANES), jnp.float32),
+        pltpu.VMEM((comps, nx, ny, nz), jnp.float32),
+    )
+
+
+def inner_call(velocity):
+    vmem = pl.BlockSpec(memory_space=pltpu.VMEM)
+    return pl.pallas_call(
+        inner_kernel,
+        in_specs=[vmem],
+        out_specs=[vmem] * 3,
+        out_shape=list(spaces(velocity)),
+        compiler_params=pltpu.CompilerParams(vmem_limit_bytes=2 * 2**20),
+        cost_estimate=pl.CostEstimate(
+            flops=60 * velocity.size, bytes_accessed=4 * velocity.size, transcendentals=0
+        ),
+        name="inner_cells",
+    )(in_vmem(velocity))
+
+
+def halo_call(velocity, xlo, xhi, ylo, yhi, gram, p1):
     comps, nx, ny, nz = velocity.shape
     vmem = pl.BlockSpec(memory_space=pltpu.VMEM)
+    line = pltpu.VMEM((comps, 2, nz), jnp.float32)
     return pl.pallas_call(
-        field_kernel,
-        in_specs=[vmem] * 5,
-        out_specs=[pl.BlockSpec(memory_space=pl.ANY), vmem, vmem, vmem],
-        out_shape=[
-            pltpu.HBM(velocity.shape, jnp.float32),
-            pltpu.VMEM((comps, nx + 2, ny + 8, nz), jnp.float32),
-            pltpu.VMEM((comps, 2, ny, nz), jnp.float32),
-            pltpu.VMEM((comps, nx * ny * nz // LANES, LANES), jnp.float32),
-        ],
-        scratch_shapes=[
-            pltpu.VMEM((comps, nx, 8, nz), jnp.float32),
-            pltpu.VMEM((comps, nx, ny, nz), jnp.float32),
-            pltpu.SemaphoreType.DMA((nx,)),
-        ],
-        compiler_params=pltpu.CompilerParams(vmem_limit_bytes=8 * 2**20),
+        halo_kernel,
+        in_specs=[vmem] * 7,
+        out_specs=[vmem] * 3,
+        out_shape=[spaces(velocity)[0], line, line],
+        input_output_aliases={6: 0},
+        scratch_shapes=[pltpu.VMEM((comps, nx, 8, nz), jnp.float32)],
+        compiler_params=pltpu.CompilerParams(vmem_limit_bytes=4 * 2**20),
         cost_estimate=pl.CostEstimate(
-            flops=60 * velocity.size, bytes_accessed=8 * velocity.size, transcendentals=0
+            flops=15 * velocity.size, bytes_accessed=velocity.size, transcendentals=0
         ),
-        name="substeps",
-    )(*(in_vmem(a) for a in (velocity, xlo, xhi, ylo, yhi)))
+        name="halo_part",
+    )(*(in_vmem(a) for a in (velocity, xlo, xhi, ylo, yhi, gram, p1)))
+
+
+def outer_call(velocity, p1, flat, u2):
+    nx = velocity.shape[1]
+    vmem = pl.BlockSpec(memory_space=pltpu.VMEM)
+    return pl.pallas_call(
+        outer_kernel,
+        in_specs=[vmem] * 3,
+        out_specs=[vmem, vmem, pl.BlockSpec(memory_space=pl.ANY)],
+        out_shape=[*spaces(velocity)[1:], pltpu.HBM(velocity.shape, jnp.float32)],
+        input_output_aliases={1: 0, 2: 1},
+        scratch_shapes=[pltpu.SemaphoreType.DMA((nx,))],
+        compiler_params=pltpu.CompilerParams(vmem_limit_bytes=2 * 2**20),
+        cost_estimate=pl.CostEstimate(
+            flops=20 * velocity.size, bytes_accessed=4 * velocity.size, transcendentals=0
+        ),
+        name="outer_cells",
+    )(in_vmem(p1), in_vmem(flat), in_vmem(u2))
 
 
 def sample_kernel(
-    ids_ref, steps_ref, w_ref, xlo_ref, xhi_ref, clo_ref, chi_ref, own_lo_ref, own_hi_ref,
-    p1, modes_ref, snaps_ref, gram_ref, advanced_in, ends_in, flat_in,
-    advanced_ref, ends_ref, flat, snaps_out_ref, mine_ref, other_ref,
+    at_ref, mask_ref, tall_ref, xlo_ref, xhi_ref, clo_ref, chi_ref, own_lo_ref, own_hi_ref,
+    p1, modes_ref, gram_ref, advanced_in, u2_in, flat_in, snaps_in,
+    advanced_ref, u2, flat, snaps_ref, mine_ref, other_ref,
     fixed, picked, packed, sems,
 ):
     comps, _, ny, nz = xlo_ref.shape
@@ -274,49 +377,45 @@
             return p1[c, layer + 1 + k, 8 * t : 8 * t + 8, :]
 
         def store(c, t, value):
-            ends_ref[c, end, 8 * t : 8 * t + 8, :] = value
+            u2[c, layer, 8 * t : 8 * t + 8, :] = value
             for k in range(tiles):
                 at = (k * nx + layer) * ny + 8 * t
                 flat[c, at : at + 8, :] = value[:, k * LANES : (k + 1) * LANES]
 
         stencil(tile, (0, inner - 1), inner, store)
     out_copies = [
-        pltpu.make_async_copy(ends_ref.at[:, 0], advanced_ref.at[:, 0], sems.at[0]),
-        pltpu.make_async_copy(ends_ref.at[:, 1], advanced_ref.at[:, nx - 1], sems.at[1]),
+        pltpu.make_async_copy(u2.at[:, 0], advanced_ref.at[:, 0], sems.at[0]),
+        pltpu.make_async_copy(u2.at[:, nx - 1], advanced_ref.at[:, nx - 1], sems.at[1]),
     ]
     for copy in out_copies:
         copy.start()
 
-    count = ids_ref.shape[0]
-    lane = lax.broadcasted_iota(jnp.int32, (1, LANES), 1)
-
-    @pl.loop(0, count // 8)
-    def _(i):
-        for k in range(8):
-            cell = ids_ref[i * 8 + k]
-            line = lax.shift_right_logical(cell, int(math.log2(LANES)))
-            at = (line & (tiles - 1)) * (nx * ny) + lax.shift_right_logical(line, int(math.log2(tiles)))
-            hit = lane == (cell & (LANES - 1))
+    count = mask_ref.shape[0]
+    groups = count // LANES
+
+    @pl.loop(0, groups)
+    def _(g):
+        for first in range(0, LANES, 8):
+            ats = [at_ref[g, first + k] for k in range(8)]
+            to = pl.multiple_of(g * LANES + first, 8)
             for c in range(comps):
-                row = flat[c, pl.ds(at, 1), :]
-                picked[c, pl.ds(i * 8 + k, 1), :] = jnp.where(hit, row, 0.0)
-
-    ones = jnp.ones((8, LANES), jnp.float32)
-    parts = [dot(ones, picked[c], 1, 1)[0:1] for c in range(comps)]
+                picked[c, pl.ds(to, 8), :] = jnp.concatenate([flat[c, pl.ds(at, 1), :] for at in ats], axis=0)
+
+    ones = jnp.ones((16, 3 * LANES), jnp.bfloat16)
+    parts = []
+    for c in range(comps):
+        pieces = jnp.concatenate(split(picked[c] * mask_ref[...]), axis=1)
+        parts.append(
+            lax.dot_general(ones, pieces, (((1,), (1,)), ((), ())), preferred_element_type=jnp.float32)[0:1]
+        )
     sample = jnp.concatenate(parts, axis=1)
-
-    snaps_count = steps_ref.shape[0]
-    place = jnp.int32(0)
-    for j in range(snaps_count):
-        place = jnp.where(steps_ref[j] == snaps_count - 1, j, place)
-    snaps_out_ref[...] = snaps_ref[...]
-    snaps_out_ref[pl.ds(place, 1), :] = sample
+    place = at_ref[groups, 0]
+    snaps_ref[pl.ds(place, 1), :] = sample
 
     k = modes_ref.shape[0]
-    half = snaps_count
-    tall = jnp.transpose(jnp.broadcast_to(w_ref[...], (k, k)))
-    with_modes = jnp.sum(modes_ref[...] * sample, axis=1, keepdims=True) * tall
-    with_snaps = jnp.sum(snaps_out_ref[...] * sample, axis=1, keepdims=True)
+    half = snaps_ref.shape[0]
+    with_modes = jnp.sum(modes_ref[...] * sample, axis=1, keepdims=True) * tall_ref[...]
+    with_snaps = jnp.sum(snaps_ref[...] * sample, axis=1, keepdims=True)
     col = lax.broadcasted_iota(jnp.int32, (half, half), 1)
     row = lax.broadcasted_iota(jnp.int32, (half, half), 0)
     col_k = lax.broadcasted_iota(jnp.int32, (k, half), 1)
@@ -339,43 +438,38 @@
 
 
 def sample_call(
-    ids, steps, weights, xlo, xhi, clo, chi, own_lo, own_hi, p1, modes, snaps, gram, advanced, ends, flat
+    at, mask, tall, xlo, xhi, clo, chi, own_lo, own_hi, p1, modes, gram, advanced, u2, flat, snaps
 ):
     comps, _, _, nz = xlo.shape
-    total = gram.shape[0]
-    part = total // 2
-    smem = pl.BlockSpec(memory_space=pltpu.SMEM)
+    part = gram.shape[0] // 2
     vmem = pl.BlockSpec(memory_space=pltpu.VMEM)
     hbm = pl.BlockSpec(memory_space=pl.ANY)
-    tail = (weights, xlo, xhi, clo, chi, own_lo, own_hi, p1, modes, snaps, gram)
+    ins = (at, mask, tall, xlo, xhi, clo, chi, own_lo, own_hi, p1, modes, gram)
     return pl.pallas_call(
         sample_kernel,
-        in_specs=[smem] * 2 + [vmem] * 11 + [hbm, vmem, vmem],
-        out_specs=[hbm, vmem, vmem, vmem, vmem, vmem],
+        in_specs=[pl.BlockSpec(memory_space=pltpu.SMEM)] + [vmem] * 11 + [hbm, vmem, vmem, vmem],
+        out_specs=[hbm] + [vmem] * 5,
         out_shape=[
             pltpu.HBM(advanced.shape, jnp.float32),
-            pltpu.VMEM(ends.shape, jnp.float32),
+            pltpu.VMEM(u2.shape, jnp.float32),
             pltpu.VMEM(flat.shape, jnp.float32),
             pltpu.VMEM(snaps.shape, jnp.float32),
             pltpu.VMEM((part, LANES), jnp.float32),
             pltpu.VMEM((part, LANES), jnp.float32),
         ],
-        input_output_aliases={13: 0, 14: 1, 15: 2},
+        input_output_aliases={12: 0, 13: 1, 14: 2, 15: 3},
         scratch_shapes=[
             pltpu.VMEM((comps, 2, 3, 8, nz), jnp.float32),
-            pltpu.VMEM((comps, ids.shape[0], LANES), jnp.float32),
-            pltpu.VMEM((total, LANES), jnp.float32),
+            pltpu.VMEM((comps, mask.shape[0], LANES), jnp.float32),
+            pltpu.VMEM((2 * part, LANES), jnp.float32),
             pltpu.SemaphoreType.DMA((2,)),
         ],
-        compiler_params=pltpu.CompilerParams(vmem_limit_bytes=6 * 2**20),
+        compiler_params=pltpu.CompilerParams(vmem_limit_bytes=8 * 2**20),
         cost_estimate=pl.CostEstimate(
             flops=20 * flat.size, bytes_accessed=2 * flat.size, transcendentals=0
         ),
         name="sample_and_gram",
-    )(
-        in_vmem(ids), in_vmem(steps), *(in_vmem(a) for a in tail),
-        in_hbm(advanced), in_vmem(ends), in_vmem(flat),
-    )
+    )(*(in_vmem(a) for a in ins), in_hbm(advanced), in_vmem(u2), in_vmem(flat), in_vmem(snaps))
 
 
 def eliminate(pieces, start):
@@ -513,15 +607,18 @@
     xhi = lax.ppermute(xlow, "grp", down)
 
     weights = mode_weights.reshape(1, -1)
-    gram, snaps = early_gram(snap_steps, weights, modes, history)
-
-    clow, chigh = corners(ylo, yhi, gram)
+    comps, nx, ny, nz = velocity.shape
+    gram, snaps, tall, at, mask = early_gram(
+        (nx * ny, nz // LANES), snap_steps, weights, modes, history, slab_ids.reshape(-1, LANES)
+    )
+
+    p1, flat, u2 = inner_call(velocity)
+    p1, clow, chigh = halo_call(velocity, xlo, xhi, ylo, yhi, gram, p1)
     clo = lax.ppermute(chigh, "grp", up)
     chi = lax.ppermute(clow, "grp", down)
-
-    advanced, p1, ends, flat = field_call(velocity, xlo, xhi, ylo, yhi)
+    flat, u2, advanced = outer_call(velocity, p1, flat, u2)
     advanced, _, _, snaps, mine, other = sample_call(
-        slab_ids, snap_steps, weights, xlo, xhi, clo, chi, clow, chigh, p1, modes, snaps, gram, advanced, ends, flat
+        at, mask, tall, xlo, xhi, clo, chi, clow, chigh, p1, modes, gram, advanced, u2, flat, snaps
     )
 
     devices = lax.axis_size("tile") * lax.axis_size("grp")

time: 57.9 us -> 53.5 us (0.924)
  waiting for transfers between devices: 12.3 us -> 9.63 us
  Pallas kernels: 26.7 us -> 24.9 us
    pallas_call x4 -> x5, Pallas kernels: 17 us -> 15.2 us  [the longest x1 4.3 us: inner_call(): pl.pallas_call(inner_kernel, in_specs=[vmem], out_specs=[vmem] * 3, out_s...]
    ppermute x1, waiting for transfers between devices: 2.2 us -> 0.72 us  [per_device(): yhi = lax.ppermute(ylow, 'tile', down_y)]
    ppermute x1, waiting for transfers between devices: 1.22 us -> 0.01 us  [per_device(): ylo = lax.ppermute(yhigh, 'tile', up_y)]
  transfers between devices with their start and end apart: 14 -> 14, of which waited for: 8 -> 7; matrix products, arithmetic and copies ran while one was open for 0% -> 0% of each run, Pallas kernels for 19% -> 18%
where the time goes in v4:
time: 53.5 us; the launch traced here: 53.3 us
  Pallas kernels  24.9 us (47%)
  starting transfers between devices  17.7 us (33%)
  waiting for transfers between devices  9.63 us (18%)
  between operations  0.99 us (2%)
    ppermute x8, waiting for transfers between devices, swap(): lax.ppermute(array, ('tile', 'grp'), [(i, i ^ bits) for i in range(device...  8.9 us
    pallas_call x1, Pallas kernels, basis_call(): pl.pallas_call(functools.partial(basis_kernel, root), in_specs=[vmem] * 5...  8.24 us
    ppermute x8, starting transfers between devices, swap(): lax.ppermute(array, ('tile', 'grp'), [(i, i ^ bits) for i in range(device...  8.14 us
    pallas_call x1, Pallas kernels, inner_call(): pl.pallas_call(inner_kernel, in_specs=[vmem], out_specs=[vmem] * 3, out_s...  4.3 us
    pallas_call x1, Pallas kernels, sample_call(): pl.pallas_call(sample_kernel, in_specs=[pl.BlockSpec(memory_space=pltpu.S...  3.66 us
    ppermute x1, starting transfers between devices, per_device(): yhi = lax.ppermute(ylow, 'tile', down_y)  3.04 us
    pallas_call x1, Pallas kernels, outer_call(): pl.pallas_call(outer_kernel, in_specs=[vmem] * 3, out_specs=[vmem, vmem,...  2.63 us
    pallas_call x1, Pallas kernels, early_gram(): pl.pallas_call(functools.partial(gram_kernel, lines), in_specs=[pl.BlockS...  2.46 us
  transfers between devices with their start and end apart: 14, of which 7 were waited for; matrix products, arithmetic and copies ran while one was open for 0% of the time, Pallas kernels for 18%

profile of v4, /device:TPU:0, one launch (start us, length us, event | category | flops | bytes accessed | tf_op | source)
XLA Modules:
  0.0 53.3 jit_solution(12826272918128823630)
XLA Ops:
  0.6 0.0 copy-start
  0.6 0.0 copy-start.1
  0.7 0.0 copy-start.4
  0.7 0.0 copy-start.3
  0.7 0.0 copy-start.2
  0.7 0.0 copy-start.5
  0.7 1.5 %faces.1 = (f32[3,16,2,512]{3,2,1,0:T(2,128)S(1)}, f32[3,16,2,512]{3,2,1,0:T(2,128)S(1)}, f32[3,2,32,512]{3,2,1,0:T(8,128)S(1)}, f32[3,2,32,512]{3,2,1,0:T(8,128)S(1)}) custom-call(f32[3,16,32,512]{3,2,1,0:T(8,128)} %velocity_ref.5), custom_call_target="tpu_custom_call" | custom-call | tf_op jit(solution)/shard_map/faces/pallas_call | solution.py:52
  2.2 0.5 collective-permute-start
  2.7 2.0 %collective-permute-start.1 = (f32[3,2,32,512]{3,2,1,0:T(8,128)S(1)}, f32[3,2,32,512]{3,2,1,0:T(8,128)S(1)}, u32[]{:S(2)}, u32[]{:S(2)}) collective-permute-start(f32[3,2,32,512]{3,2,1,0:T(8,128)S(1)} %get-tuple-element.31), channel_id=1, source_target_pairs={{0,3},{1,0},{2,1},{3,2},{4,7},{5,4},{6,5},{7,6},{8,11},{9,8},{10,9... | collective-permute-start | bytes 1179656 | tf_op jit(solution)/shard_map/ppermute | solution.py:607
  4.7 2.3 %collective-permute-start.2 = (f32[3,16,2,512]{3,2,1,0:T(2,128)S(1)}, f32[3,16,2,512]{3,2,1,0:T(2,128)S(1)}, u32[]{:S(2)}, u32[]{:S(2)}) collective-permute-start(f32[3,16,2,512]{3,2,1,0:T(2,128)S(1)} %get-tuple-element.32), channel_id=1, source_target_pairs={{0,4},{4,8},{8,12},{12,16},{16,20},{20,24},{24,28},{28,0},{1,5},{5... | collective-permute-start | bytes 589832 | tf_op jit(solution)/shard_map/ppermute | solution.py:604
  7.0 3.0 %collective-permute-start.3 = (f32[3,16,2,512]{3,2,1,0:T(2,128)S(1)}, f32[3,16,2,512]{3,2,1,0:T(2,128)S(1)}, u32[]{:S(2)}, u32[]{:S(2)}) collective-permute-start(f32[3,16,2,512]{3,2,1,0:T(2,128)S(1)} %get-tuple-element.33), channel_id=1, source_target_pairs={{0,28},{4,0},{8,4},{12,8},{16,12},{20,16},{24,20},{28,24},{1,29},{... | collective-permute-start | bytes 589832 | tf_op jit(solution)/shard_map/ppermute | solution.py:605
  10.0 0.0 copy-done
  10.0 4.3 %inner_cells.1 = (f32[3,18,40,512]{3,2,1,0:T(8,128)S(1)}, f32[3,2048,128]{2,1,0:T(8,128)S(1)}, f32[3,16,32,512]{3,2,1,0:T(8,128)S(1)}) custom-call(f32[3,16,32,512]{3,2,1,0:T(8,128)S(1)} %copy-done), custom_call_target="tpu_custom_call" | custom-call | flops 47185920 | bytes 3145728 | tf_op jit(solution)/shard_map/inner_cells/pallas_call | solution.py:289
  14.3 0.0 copy-done.1
  14.3 0.0 copy-done.4
  14.3 0.0 copy-done.3
  14.3 0.0 copy-done.2
  14.4 0.0 copy-done.5
  14.4 2.5 %early_gram.1 = (f32[192,192]{1,0:T(8,128)S(1)}, f32[64,3072]{1,0:T(8,128)S(1)}, f32[128,128]{1,0:T(8,128)S(1)}, s32[16,128]{1,0:T(8,128)S(1)}, f32[1024,128]{1,0:T(8,128)S(1)}) custom-call(s32[64]{0:T(128)S(1)} %copy-done.4, f32[1,128]{1,0:T(1,128)S(1)} %bitcast.3, f32[128,3072]{1,0:T(8,128)S(1)} %copy-done.1, f32[63,3072]{1,0:T(8,128)S(1)} %copy-done.2, ...), custom_call_target="tpu_custom_call" | custom-call | flops 905969664 | bytes 7077888 | tf_op jit(solution)/shard_map/early_gram/pallas_call | solution.py:116
  16.8 0.0 collective-permute-done.2.ylo_ref
  16.8 0.7 %collective-permute-done.3.yhi_ref = f32[3,16,2,512]{3,2,1,0:T(2,128)S(1)} collective-permute-done((f32[3,16,2,512]{3,2,1,0:T(2,128)S(1)}, f32[3,16,2,512]{3,2,1,0:T(2,128)S(1)}, u32[]{:S(2)}, u32[]{:S(2)}) %collective-permute-start.3) | collective-permute-done | bytes 196640 | tf_op jit(solution)/shard_map/ppermute | solution.py:605
  17.6 0.0 collective-permute-done.xlo_ref
  17.6 0.0 collective-permute-done.1.xhi_ref
  17.6 2.1 %halo_part.1 = (f32[3,18,40,512]{3,2,1,0:T(8,128)S(1)}, f32[3,2,512]{2,1,0:T(2,128)S(1)}, f32[3,2,512]{2,1,0:T(2,128)S(1)}) custom-call(f32[3,16,32,512]{3,2,1,0:T(8,128)S(1)} %copy-done, f32[3,2,32,512]{3,2,1,0:T(8,128)S(1)} %collective-permute-done.xlo_ref, f32[3,2,32,512]{3,2,1,0:T(8,128)S(1)} %collective-permute-done.1.xhi_ref, ...), custom_call_target="tpu_custom_call", output_to_operand_aliasing={{0}: (6, {})} | custom-call | flops 11796480 | bytes 786432 | tf_op jit(solution)/shard_map/halo_part/pallas_call | solution.py:306
  19.7 0.1 collective-permute-start.4
  19.7 1.7 %collective-permute-start.5 = (f32[3,2,512]{2,1,0:T(2,128)S(1)}, f32[3,2,512]{2,1,0:T(2,128)S(1)}, u32[]{:S(2)}, u32[]{:S(2)}) collective-permute-start(f32[3,2,512]{2,1,0:T(2,128)S(1)} %get-tuple-element.37.own_lo_ref), channel_id=1, source_target_pairs={{0,3},{1,0},{2,1},{3,2},{4,7},{5,4},{6,5},{7,6},{8,11},{9,8},{10,9... | collective-permute-start | bytes 36872 | tf_op jit(solution)/shard_map/ppermute | solution.py:618
  21.5 2.6 %outer_cells.1 = (f32[3,2048,128]{2,1,0:T(8,128)S(1)}, f32[3,16,32,512]{3,2,1,0:T(8,128)S(1)}, f32[3,16,32,512]{3,2,1,0:T(8,128)}) custom-call(f32[3,18,40,512]{3,2,1,0:T(8,128)S(1)} %get-tuple-element.38.p1, f32[3,2048,128]{2,1,0:T(8,128)S(1)} %get-tuple-element.39.flat_in, ...), custom_call_target="tpu_custom_call", output_to_operand_aliasing={{0}: (1, {}), {1}: (2, {})} | custom-call | flops 15728640 | bytes 3145728 | tf_op jit(solution)/shard_map/outer_cells/pallas_call | solution.py:324
  24.1 0.0 collective-permute-done.4.clo_ref
  24.1 0.0 collective-permute-done.5.chi_ref
  24.1 3.7 %sample_and_gram.1 = (f32[3,16,32,512]{3,2,1,0:T(8,128)}, f32[3,16,32,512]{3,2,1,0:T(8,128)S(1)}, f32[3,2048,128]{2,1,0:T(8,128)S(1)}, f32[64,3072]{1,0:T(8,128)...) custom-call(s32[16,128]{1,0:T(8,128)S(1)} %get-tuple-element.27.at_r, ...), custom_call_target="tpu_custom_call", output_to_operand_aliasing={{0}: (12, {}), {1}: (13, {}), {2}: (14, {}), {3}: (15, {})} | custom-call | flops 15728640 | bytes 1572864 | tf_op jit(solution)/shard_map/sample_and_gram/pallas_call | solution.py:448
  27.8 0.1 collective-permute-start.6
  27.9 1.2 %collective-permute-done.6 = f32[96,128]{1,0:T(8,128)S(1)} collective-permute-done((f32[96,128]{1,0:T(8,128)S(1)}, f32[96,128]{1,0:T(8,128)S(1)}, u32[]{:S(2)}, u32[]{:S(2)}) %collective-permute-start.6) | collective-permute-done | bytes 49184 | tf_op jit(solution)/shard_map/ppermute | solution.py:597
  29.1 0.3 collective-permute-start.9
  29.4 2.2 %collective-permute-start.8 = (f32[96,128]{1,0:T(8,128)S(1)}, f32[96,128]{1,0:T(8,128)S(1)}, u32[]{:S(2)}, u32[]{:S(2)}) collective-permute-start(f32[96,128]{1,0:T(8,128)S(1)} %add.21), channel_id=1, source_target_pairs={{0,4},{1,5},{2,6},{3,7},{4,0},{5,1},{6,2},{7,3},{8,12},{9,13},{10,... | collective-permute-start | bytes 147464 | tf_op jit(solution)/shard_map/ppermute | solution.py:597
  31.6 1.1 %collective-permute-start.7 = (f32[96,128]{1,0:T(8,128)S(1)}, f32[96,128]{1,0:T(8,128)S(1)}, u32[]{:S(2)}, u32[]{:S(2)}) collective-permute-start(f32[96,128]{1,0:T(8,128)S(1)} %add.21), channel_id=1, source_target_pairs={{0,2},{1,3},{2,0},{3,1},{4,6},{5,7},{6,4},{7,5},{8,10},{9,11},{10,... | collective-permute-start | bytes 147464 | tf_op jit(solution)/shard_map/ppermute | solution.py:597
  32.7 1.8 %collective-permute-done.9 = f32[96,128]{1,0:T(8,128)S(1)} collective-permute-done((f32[96,128]{1,0:T(8,128)S(1)}, f32[96,128]{1,0:T(8,128)S(1)}, u32[]{:S(2)}, u32[]{:S(2)}) %collective-permute-start.9) | collective-permute-done | bytes 49184 | tf_op jit(solution)/shard_map/ppermute | solution.py:597
  34.5 0.0 collective-permute-done.8
  34.5 1.2 %collective-permute-done.7 = f32[96,128]{1,0:T(8,128)S(1)} collective-permute-done((f32[96,128]{1,0:T(8,128)S(1)}, f32[96,128]{1,0:T(8,128)S(1)}, u32[]{:S(2)}, u32[]{:S(2)}) %collective-permute-start.7) | collective-permute-done | bytes 49184 | tf_op jit(solution)/shard_map/ppermute | solution.py:597
  35.7 2.9 %collective-permute-start.12 = (f32[96,128]{1,0:T(8,128)S(1)}, f32[96,128]{1,0:T(8,128)S(1)}, u32[]{:S(2)}, u32[]{:S(2)}) collective-permute-start(f32[96,128]{1,0:T(8,128)S(1)} %add_add_fusion.1), channel_id=1, source_target_pairs={{0,24},{1,25},{2,26},{3,27},{4,28},{5,29},{6,30},{7,31},{8,16},{9,... | collective-permute-start | bytes 147464 | tf_op jit(solution)/shard_map/ppermute | solution.py:597
  38.6 0.0 collective-permute-start.11
  38.6 1.5 %collective-permute-start.10 = (f32[96,128]{1,0:T(8,128)S(1)}, f32[96,128]{1,0:T(8,128)S(1)}, u32[]{:S(2)}, u32[]{:S(2)}) collective-permute-start(f32[96,128]{1,0:T(8,128)S(1)} %add_add_fusion.1), channel_id=1, source_target_pairs={{0,8},{1,9},{2,10},{3,11},{4,12},{5,13},{6,14},{7,15},{8,0},{9,1},... | collective-permute-start | bytes 147464 | tf_op jit(solution)/shard_map/ppermute | solution.py:597
  40.2 1.6 %collective-permute-done.12 = f32[96,128]{1,0:T(8,128)S(1)} collective-permute-done((f32[96,128]{1,0:T(8,128)S(1)}, f32[96,128]{1,0:T(8,128)S(1)}, u32[]{:S(2)}, u32[]{:S(2)}) %collective-permute-start.12) | collective-permute-done | bytes 49184 | tf_op jit(solution)/shard_map/ppermute | solution.py:597
  41.8 1.8 %collective-permute-done.11 = f32[96,128]{1,0:T(8,128)S(1)} collective-permute-done((f32[96,128]{1,0:T(8,128)S(1)}, f32[96,128]{1,0:T(8,128)S(1)}, u32[]{:S(2)}, u32[]{:S(2)}) %collective-permute-start.11) | collective-permute-done | bytes 49184 | tf_op jit(solution)/shard_map/ppermute | solution.py:597
  43.6 0.0 collective-permute-done.10
  43.6 0.1 collective-permute-start.13
  43.7 1.2 %collective-permute-done.13.other_ref = f32[96,128]{1,0:T(8,128)S(1)} collective-permute-done((f32[96,128]{1,0:T(8,128)S(1)}, f32[96,128]{1,0:T(8,128)S(1)}, u32[]{:S(2)}, u32[]{:S(2)}) %collective-permute-start.13) | collective-permute-done | bytes 49184 | tf_op jit(solution)/shard_map/ppermute | solution.py:597
  44.9 8.2 %factor_and_basis.1 = (f32[192,192]{1,0:T(8,128)}, f32[192,3072]{1,0:T(8,128)}) custom-call(f32[1,128]{1,0:T(1,128)S(1)} %bitcast.4, f32[96,128]{1,0:T(8,128)S(1)} %add_add_fusion.mine_ref, f32[96,128]{1,0:T(8,128)S(1)} %collective-permute-done.13.other_ref, f32[128,3072]{1,0:T(8,128)S(1)} %copy-done.1, f32[64,3072]{1,0:T(8,128)S(1)} %get-tuple-element.48.snaps_ref), custom_call_target="tpu_custom_call" | custom-call | flops 1358954496 | bytes 4718592 | tf_op jit(solution)/shard_map/factor_and_basis/pallas_call | solution.py:568
  (3 shorter events, 0.0 us)
Async XLA Ops:
  0.6 9.4 %copy-start = (f32[3,16,32,512]{3,2,1,0:T(8,128)S(1)}, f32[3,16,32,512]{3,2,1,0:T(8,128)}, u32[]{:S(2)}) copy-start(f32[3,16,32,512]{3,2,1,0:T(8,128)} %velocity_ref.5) | copy-start | bytes 9437188
  0.6 13.7 %copy-start.1 = (f32[128,3072]{1,0:T(8,128)S(1)}, f32[128,3072]{1,0:T(8,128)}, u32[]{:S(2)}) copy-start(f32[128,3072]{1,0:T(8,128)} %modes_ref.5) | copy-start | bytes 4718596
  0.7 13.7 %copy-start.4 = (s32[64]{0:T(128)S(1)}, s32[64]{0:T(128)}, u32[]{:S(2)}) copy-start(s32[64]{0:T(128)} %steps_ref.1) | copy-start | bytes 772
  0.7 13.7 %copy-start.3 = (s32[1024]{0:T(1024)S(1)}, s32[1024]{0:T(1024)}, u32[]{:S(2)}) copy-start(s32[1024]{0:T(1024)} %param.10) | copy-start | bytes 12292
  0.7 13.7 %copy-start.2 = (f32[63,3072]{1,0:T(8,128)S(1)}, f32[63,3072]{1,0:T(8,128)}, u32[]{:S(2)}) copy-start(f32[63,3072]{1,0:T(8,128)} %history_ref.1) | copy-start | bytes 2322436
  0.7 13.7 %copy-start.5 = (f32[128]{0:T(128)S(1)}, f32[128]{0:T(128)}, u32[]{:S(2)}) copy-start(f32[128]{0:T(128)} %param.8) | copy-start | bytes 1540
  2.2 15.4 %collective-permute-start = (f32[3,2,32,512]{3,2,1,0:T(8,128)S(1)}, f32[3,2,32,512]{3,2,1,0:T(8,128)S(1)}, u32[]{:S(2)}, u32[]{:S(2)}) collective-permute-start(f32[3,2,32,512]{3,2,1,0:T(8,128)S(1)} %get-tuple-element.30), channel_id=1, source_target_pairs={{0,1},{1,2},{2,3},{3,0},{4,5},{5,6},{6,7},{7,4},{8,9},{9,10},{10,1... | collective-permute-start | bytes 1179656 | tf_op jit(solution)/shard_map/ppermute | solution.py:606
  2.7 14.9 %collective-permute-start.1 = (f32[3,2,32,512]{3,2,1,0:T(8,128)S(1)}, f32[3,2,32,512]{3,2,1,0:T(8,128)S(1)}, u32[]{:S(2)}, u32[]{:S(2)}) collective-permute-start(f32[3,2,32,512]{3,2,1,0:T(8,128)S(1)} %get-tuple-element.31), channel_id=1, source_target_pairs={{0,3},{1,0},{2,1},{3,2},{4,7},{5,4},{6,5},{7,6},{8,11},{9,8},{10,9... | collective-permute-start | bytes 1179656 | tf_op jit(solution)/shard_map/ppermute | solution.py:607
  4.7 12.1 %collective-permute-start.2 = (f32[3,16,2,512]{3,2,1,0:T(2,128)S(1)}, f32[3,16,2,512]{3,2,1,0:T(2,128)S(1)}, u32[]{:S(2)}, u32[]{:S(2)}) collective-permute-start(f32[3,16,2,512]{3,2,1,0:T(2,128)S(1)} %get-tuple-element.32), channel_id=1, source_target_pairs={{0,4},{4,8},{8,12},{12,16},{16,20},{20,24},{24,28},{28,0},{1,5},{5... | collective-permute-start | bytes 589832 | tf_op jit(solution)/shard_map/ppermute | solution.py:604
  7.0 10.6 %collective-permute-start.3 = (f32[3,16,2,512]{3,2,1,0:T(2,128)S(1)}, f32[3,16,2,512]{3,2,1,0:T(2,128)S(1)}, u32[]{:S(2)}, u32[]{:S(2)}) collective-permute-start(f32[3,16,2,512]{3,2,1,0:T(2,128)S(1)} %get-tuple-element.33), channel_id=1, source_target_pairs={{0,28},{4,0},{8,4},{12,8},{16,12},{20,16},{24,20},{28,24},{1,29},{... | collective-permute-start | bytes 589832 | tf_op jit(solution)/shard_map/ppermute | solution.py:605
  19.7 4.4 %collective-permute-start.4 = (f32[3,2,512]{2,1,0:T(2,128)S(1)}, f32[3,2,512]{2,1,0:T(2,128)S(1)}, u32[]{:S(2)}, u32[]{:S(2)}) collective-permute-start(f32[3,2,512]{2,1,0:T(2,128)S(1)} %get-tuple-element.36.own_hi_ref), channel_id=1, source_target_pairs={{0,1},{1,2},{2,3},{3,0},{4,5},{5,6},{6,7},{7,4},{8,9},{9,10},{10,1... | collective-permute-start | bytes 36872 | tf_op jit(solution)/shard_map/ppermute | solution.py:617
  19.7 4.4 %collective-permute-start.5 = (f32[3,2,512]{2,1,0:T(2,128)S(1)}, f32[3,2,512]{2,1,0:T(2,128)S(1)}, u32[]{:S(2)}, u32[]{:S(2)}) collective-permute-start(f32[3,2,512]{2,1,0:T(2,128)S(1)} %get-tuple-element.37.own_lo_ref), channel_id=1, source_target_pairs={{0,3},{1,0},{2,1},{3,2},{4,7},{5,4},{6,5},{7,6},{8,11},{9,8},{10,9... | collective-permute-start | bytes 36872 | tf_op jit(solution)/shard_map/ppermute | solution.py:618
  27.8 1.3 %collective-permute-start.6 = (f32[96,128]{1,0:T(8,128)S(1)}, f32[96,128]{1,0:T(8,128)S(1)}, u32[]{:S(2)}, u32[]{:S(2)}) collective-permute-start(f32[96,128]{1,0:T(8,128)S(1)} %get-tuple-element.47), channel_id=1, source_target_pairs={{0,1},{1,0},{2,3},{3,2},{4,5},{5,4},{6,7},{7,6},{8,9},{9,8},{10,11... | collective-permute-start | bytes 147464 | tf_op jit(solution)/shard_map/ppermute | solution.py:597
  29.1 5.4 %collective-permute-start.9 = (f32[96,128]{1,0:T(8,128)S(1)}, f32[96,128]{1,0:T(8,128)S(1)}, u32[]{:S(2)}, u32[]{:S(2)}) collective-permute-start(f32[96,128]{1,0:T(8,128)S(1)} %add.21), channel_id=1, source_target_pairs={{0,6},{1,7},{2,4},{3,5},{4,2},{5,3},{6,0},{7,1},{8,14},{9,15},{10,... | collective-permute-start | bytes 147464 | tf_op jit(solution)/shard_map/ppermute | solution.py:597
  29.4 5.1 %collective-permute-start.8 = (f32[96,128]{1,0:T(8,128)S(1)}, f32[96,128]{1,0:T(8,128)S(1)}, u32[]{:S(2)}, u32[]{:S(2)}) collective-permute-start(f32[96,128]{1,0:T(8,128)S(1)} %add.21), channel_id=1, source_target_pairs={{0,4},{1,5},{2,6},{3,7},{4,0},{5,1},{6,2},{7,3},{8,12},{9,13},{10,... | collective-permute-start | bytes 147464 | tf_op jit(solution)/shard_map/ppermute | solution.py:597
  31.6 4.1 %collective-permute-start.7 = (f32[96,128]{1,0:T(8,128)S(1)}, f32[96,128]{1,0:T(8,128)S(1)}, u32[]{:S(2)}, u32[]{:S(2)}) collective-permute-start(f32[96,128]{1,0:T(8,128)S(1)} %add.21), channel_id=1, source_target_pairs={{0,2},{1,3},{2,0},{3,1},{4,6},{5,7},{6,4},{7,5},{8,10},{9,11},{10,... | collective-permute-start | bytes 147464 | tf_op jit(solution)/shard_map/ppermute | solution.py:597
  35.7 6.1 %collective-permute-start.12 = (f32[96,128]{1,0:T(8,128)S(1)}, f32[96,128]{1,0:T(8,128)S(1)}, u32[]{:S(2)}, u32[]{:S(2)}) collective-permute-start(f32[96,128]{1,0:T(8,128)S(1)} %add_add_fusion.1), channel_id=1, source_target_pairs={{0,24},{1,25},{2,26},{3,27},{4,28},{5,29},{6,30},{7,31},{8,16},{9,... | collective-permute-start | bytes 147464 | tf_op jit(solution)/shard_map/ppermute | solution.py:597
  38.6 5.0 %collective-permute-start.11 = (f32[96,128]{1,0:T(8,128)S(1)}, f32[96,128]{1,0:T(8,128)S(1)}, u32[]{:S(2)}, u32[]{:S(2)}) collective-permute-start(f32[96,128]{1,0:T(8,128)S(1)} %add_add_fusion.1), channel_id=1, source_target_pairs={{0,16},{1,17},{2,18},{3,19},{4,20},{5,21},{6,22},{7,23},{8,24},{9,... | collective-permute-start | bytes 147464 | tf_op jit(solution)/shard_map/ppermute | solution.py:597
  38.6 5.0 %collective-permute-start.10 = (f32[96,128]{1,0:T(8,128)S(1)}, f32[96,128]{1,0:T(8,128)S(1)}, u32[]{:S(2)}, u32[]{:S(2)}) collective-permute-start(f32[96,128]{1,0:T(8,128)S(1)} %add_add_fusion.1), channel_id=1, source_target_pairs={{0,8},{1,9},{2,10},{3,11},{4,12},{5,13},{6,14},{7,15},{8,0},{9,1},... | collective-permute-start | bytes 147464 | tf_op jit(solution)/shard_map/ppermute | solution.py:597
  43.6 1.3 %collective-permute-start.13 = (f32[96,128]{1,0:T(8,128)S(1)}, f32[96,128]{1,0:T(8,128)S(1)}, u32[]{:S(2)}, u32[]{:S(2)}) collective-permute-start(f32[96,128]{1,0:T(8,128)S(1)} %add_add_fusion.mine_ref), channel_id=1, source_target_pairs={{0,1},{1,0},{2,3},{3,2},{4,5},{5,4},{6,7},{7,6},{8,9},{9,8},{10,11... | collective-permute-start | bytes 147464 | tf_op jit(solution)/shard_map/ppermute | solution.py:597

commit v5 on v4

--- a/solution.py
+++ b/solution.py
@@ -68,7 +68,8 @@
 
 
 def gram_kernel(
-    lines, steps_ref, w_ref, modes_ref, history_ref, ids_ref, gram_ref, snaps_ref, tall_ref, at_ref, mask_ref
+    lines, steps_ref, w_ref, modes_ref, history_ref, ids_ref, p1_ref,
+    mine_ref, other_ref, snaps_ref, tall_ref, at_ref, mask_ref, gram_ref,
 ):
     k = modes_ref.shape[0]
     count = snaps_ref.shape[0]
@@ -91,10 +92,18 @@
     wide = jnp.broadcast_to(w_ref[...], (k, k))
     tall = jnp.transpose(wide)
     tall_ref[...] = tall
-    gram_ref[0:k, 0:k] = gram[0:k, 0:k] * wide * tall
-    gram_ref[0:k, k:] = gram[0:k, k:] * tall[:, 0:count]
-    gram_ref[k:, 0:k] = jnp.zeros((count, k), jnp.float32)
-    gram_ref[k:, k:] = gram[k:, k:]
+    first_rows = gram[0:k, 0:k] * wide * tall
+    cross = gram[0:k, k:] * tall[:, 0:count]
+    gram_ref[0:count, 0:count] = first_rows[0:count, count:]
+    gram_ref[0:count, count:] = cross[0:count]
+    gram_ref[count:k, 0:count] = first_rows[count:, count:]
+    gram_ref[count:k, count:] = cross[count:]
+    gram_ref[k:, 0:count] = first_rows[0:count, 0:count]
+    gram_ref[k:, count:] = gram[k:, k:]
+    part = mine_ref.shape[0]
+    core = lax.axis_index("grp") & 1
+    mine_ref[...] = gram_ref[pl.ds(pl.multiple_of(core * part, 8), part), :]
+    other_ref[...] = gram_ref[pl.ds(pl.multiple_of((1 - core) * part, 8), part), :]
     ids = ids_ref[...]
     groups = ids.shape[0]
     tiles = lines[1]
@@ -108,28 +117,30 @@
         mask_ref[i * LANES : (i + 1) * LANES, :] = (here == there).astype(jnp.float32)
 
 
-def early_gram(lines, steps, weights, modes, history, ids):
+def early_gram(lines, steps, weights, modes, history, ids, p1):
     k, width = modes.shape
     count = steps.shape[0]
     total = k + count
     vmem = pl.BlockSpec(memory_space=pltpu.VMEM)
     return pl.pallas_call(
         functools.partial(gram_kernel, lines),
-        in_specs=[pl.BlockSpec(memory_space=pltpu.SMEM)] + [vmem] * 4,
-        out_specs=[vmem] * 5,
+        in_specs=[pl.BlockSpec(memory_space=pltpu.SMEM)] + [vmem] * 5,
+        out_specs=[vmem] * 6,
         out_shape=[
-            pltpu.VMEM((total, total), jnp.float32),
+            pltpu.VMEM((total // 2, LANES), jnp.float32),
+            pltpu.VMEM((total // 2, LANES), jnp.float32),
             pltpu.VMEM((count, width), jnp.float32),
             pltpu.VMEM((k, k), jnp.float32),
             pltpu.VMEM((ids.shape[0] + 8, LANES), jnp.int32),
             pltpu.VMEM((ids.size, LANES), jnp.float32),
         ],
+        scratch_shapes=[pltpu.VMEM((total, LANES), jnp.float32)],
         compiler_params=pltpu.CompilerParams(vmem_limit_bytes=16 * 2**20),
         cost_estimate=pl.CostEstimate(
             flops=8 * total * total * width, bytes_accessed=12 * total * width, transcendentals=0
         ),
         name="early_gram",
-    )(*(in_vmem(a) for a in (steps, weights, modes, history, ids)))
+    )(*(in_vmem(a) for a in (steps, weights, modes, history, ids, p1)))
 
 
 def stencil(tile, which, inner, store):
@@ -200,8 +211,31 @@
     stencil(tile, which, ny // 8, store)
 
 
-def halo_kernel(
-    velocity_ref, xlo_ref, xhi_ref, ylo_ref, yhi_ref, gram_ref, p1_in, p1, clow_ref, chigh_ref, ring_tile
+def corners_kernel(ylo_ref, yhi_ref, gram_ref, p1_ref, low_ref, high_ref):
+    nx = ylo_ref.shape[1]
+    for c in range(ylo_ref.shape[0]):
+        low_ref[c, 0:1, :] = ylo_ref[c, 0, 1:2, :]
+        low_ref[c, 1:2, :] = yhi_ref[c, 0, 0:1, :]
+        high_ref[c, 0:1, :] = ylo_ref[c, nx - 1, 1:2, :]
+        high_ref[c, 1:2, :] = yhi_ref[c, nx - 1, 0:1, :]
+
+
+def corners(ylo, yhi, gram, p1):
+    comps, _, _, nz = ylo.shape
+    vmem = pl.BlockSpec(memory_space=pltpu.VMEM)
+    return pl.pallas_call(
+        corners_kernel,
+        in_specs=[vmem] * 4,
+        out_specs=[vmem, vmem],
+        out_shape=[pltpu.VMEM((comps, 2, nz), jnp.float32)] * 2,
+        compiler_params=pltpu.CompilerParams(vmem_limit_bytes=1 * 2**20),
+        name="corners",
+    )(*(in_vmem(a) for a in (ylo, yhi, gram, p1)))
+
+
+def outer_kernel(
+    velocity_ref, xlo_ref, xhi_ref, ylo_ref, yhi_ref, p1_in, flat_in, u2_in,
+    p1, flat, u2, advanced_ref, ring_tile, out_sems,
 ):
     comps, nx, ny, nz = velocity_ref.shape
     inner = ny // 8
@@ -209,10 +243,6 @@
     diff = time_step * viscosity
     vel = velocity_ref
     for c in range(comps):
-        clow_ref[c, 0:1, :] = ylo_ref[c, 0, 1:2, :]
-        clow_ref[c, 1:2, :] = yhi_ref[c, 0, 0:1, :]
-        chigh_ref[c, 0:1, :] = ylo_ref[c, nx - 1, 1:2, :]
-        chigh_ref[c, 1:2, :] = yhi_ref[c, nx - 1, 0:1, :]
         for x in range(nx):
             ring_tile[c, x, 0:2, :] = yhi_ref[c, x]
             ring_tile[c, x, 6:8, :] = ylo_ref[c, x]
@@ -251,11 +281,6 @@
 
     layer(nx - 1, (vel, vel, vel), (nx - 2, nx - 1, nx - 1), (inner,))
 
-
-def outer_kernel(p1, flat_in, u2_in, flat, u2, advanced_ref, out_sems):
-    comps, nx, ny, nz = u2.shape
-    inner = ny // 8
-
     def out_copy(x):
         return pltpu.make_async_copy(u2.at[:, x], advanced_ref.at[:, x], out_sems.at[x])
 
@@ -299,48 +324,29 @@
     )(in_vmem(velocity))
 
 
-def halo_call(velocity, xlo, xhi, ylo, yhi, gram, p1):
-    comps, nx, ny, nz = velocity.shape
-    vmem = pl.BlockSpec(memory_space=pltpu.VMEM)
-    line = pltpu.VMEM((comps, 2, nz), jnp.float32)
-    return pl.pallas_call(
-        halo_kernel,
-        in_specs=[vmem] * 7,
-        out_specs=[vmem] * 3,
-        out_shape=[spaces(velocity)[0], line, line],
-        input_output_aliases={6: 0},
-        scratch_shapes=[pltpu.VMEM((comps, nx, 8, nz), jnp.float32)],
-        compiler_params=pltpu.CompilerParams(vmem_limit_bytes=4 * 2**20),
-        cost_estimate=pl.CostEstimate(
-            flops=15 * velocity.size, bytes_accessed=velocity.size, transcendentals=0
-        ),
-        name="halo_part",
-    )(*(in_vmem(a) for a in (velocity, xlo, xhi, ylo, yhi, gram, p1)))
-
-
-def outer_call(velocity, p1, flat, u2):
-    nx = velocity.shape[1]
+def outer_call(velocity, xlo, xhi, ylo, yhi, p1, flat, u2):
+    comps, nx, _, nz = velocity.shape
     vmem = pl.BlockSpec(memory_space=pltpu.VMEM)
     return pl.pallas_call(
         outer_kernel,
-        in_specs=[vmem] * 3,
-        out_specs=[vmem, vmem, pl.BlockSpec(memory_space=pl.ANY)],
-        out_shape=[*spaces(velocity)[1:], pltpu.HBM(velocity.shape, jnp.float32)],
-        input_output_aliases={1: 0, 2: 1},
-        scratch_shapes=[pltpu.SemaphoreType.DMA((nx,))],
-        compiler_params=pltpu.CompilerParams(vmem_limit_bytes=2 * 2**20),
+        in_specs=[vmem] * 8,
+        out_specs=[vmem, vmem, vmem, pl.BlockSpec(memory_space=pl.ANY)],
+        out_shape=[*spaces(velocity), pltpu.HBM(velocity.shape, jnp.float32)],
+        input_output_aliases={5: 0, 6: 1, 7: 2},
+        scratch_shapes=[pltpu.VMEM((comps, nx, 8, nz), jnp.float32), pltpu.SemaphoreType.DMA((nx,))],
+        compiler_params=pltpu.CompilerParams(vmem_limit_bytes=4 * 2**20),
         cost_estimate=pl.CostEstimate(
-            flops=20 * velocity.size, bytes_accessed=4 * velocity.size, transcendentals=0
+            flops=40 * velocity.size, bytes_accessed=4 * velocity.size, transcendentals=0
         ),
         name="outer_cells",
-    )(in_vmem(p1), in_vmem(flat), in_vmem(u2))
+    )(*(in_vmem(a) for a in (velocity, xlo, xhi, ylo, yhi, p1, flat, u2)))
 
 
 def sample_kernel(
     at_ref, mask_ref, tall_ref, xlo_ref, xhi_ref, clo_ref, chi_ref, own_lo_ref, own_hi_ref,
-    p1, modes_ref, gram_ref, advanced_in, u2_in, flat_in, snaps_in,
-    advanced_ref, u2, flat, snaps_ref, mine_ref, other_ref,
-    fixed, picked, packed, sems,
+    p1, modes_ref, early_ref, beside_ref, advanced_in, u2_in, flat_in, snaps_in,
+    advanced_ref, u2, flat, snaps_ref, sum_ref,
+    fixed, picked, sems,
 ):
     comps, _, ny, nz = xlo_ref.shape
     nx = flat.shape[1] * LANES // (ny * nz)
@@ -416,52 +422,37 @@
     half = snaps_ref.shape[0]
     with_modes = jnp.sum(modes_ref[...] * sample, axis=1, keepdims=True) * tall_ref[...]
     with_snaps = jnp.sum(snaps_ref[...] * sample, axis=1, keepdims=True)
-    col = lax.broadcasted_iota(jnp.int32, (half, half), 1)
-    row = lax.broadcasted_iota(jnp.int32, (half, half), 0)
-    col_k = lax.broadcasted_iota(jnp.int32, (k, half), 1)
-    cross = jnp.where(col_k == place, with_modes[:, 0:half], gram_ref[0:k, k:])
-    splat = jnp.broadcast_to(with_snaps, (half, LANES))[:, 0:half]
-    low = jnp.where(col == place, splat, gram_ref[k:, k:])
-    low = jnp.where(row == place, jnp.transpose(splat), low)
-    packed[0:half, 0:half] = gram_ref[0:half, half:k]
-    packed[0:half, half:k] = cross[0:half]
-    packed[half:k, 0:half] = gram_ref[half:k, half:k]
-    packed[half:k, half:k] = cross[half:k]
-    packed[k:, 0:half] = gram_ref[0:half, 0:half]
-    packed[k:, half:k] = low
-    part = mine_ref.shape[0]
-    core = lax.axis_index("grp") & 1
-    mine_ref[...] = packed[pl.ds(pl.multiple_of(core * part, 8), part), :]
-    other_ref[...] = packed[pl.ds(pl.multiple_of((1 - core) * part, 8), part), :]
+    part = early_ref.shape[0]
+    sum_ref[0:part, :] = early_ref[...] + beside_ref[...]
+    sum_ref[part:, :] = jnp.zeros((sum_ref.shape[0] - part, LANES), jnp.float32)
+    sum_ref[part : part + 1, :] = jnp.transpose(with_modes)[0:1, :]
+    sum_ref[part + 1 : part + 2, 0:half] = jnp.transpose(jnp.broadcast_to(with_snaps, (half, LANES)))[0:1, :]
     for copy in out_copies:
         copy.wait()
 
 
 def sample_call(
-    at, mask, tall, xlo, xhi, clo, chi, own_lo, own_hi, p1, modes, gram, advanced, u2, flat, snaps
+    at, mask, tall, xlo, xhi, clo, chi, own_lo, own_hi, p1, modes, early, beside, advanced, u2, flat, snaps
 ):
     comps, _, _, nz = xlo.shape
-    part = gram.shape[0] // 2
     vmem = pl.BlockSpec(memory_space=pltpu.VMEM)
     hbm = pl.BlockSpec(memory_space=pl.ANY)
-    ins = (at, mask, tall, xlo, xhi, clo, chi, own_lo, own_hi, p1, modes, gram)
+    ins = (at, mask, tall, xlo, xhi, clo, chi, own_lo, own_hi, p1, modes, early, beside)
     return pl.pallas_call(
         sample_kernel,
-        in_specs=[pl.BlockSpec(memory_space=pltpu.SMEM)] + [vmem] * 11 + [hbm, vmem, vmem, vmem],
-        out_specs=[hbm] + [vmem] * 5,
+        in_specs=[pl.BlockSpec(memory_space=pltpu.SMEM)] + [vmem] * 12 + [hbm, vmem, vmem, vmem],
+        out_specs=[hbm] + [vmem] * 4,
         out_shape=[
             pltpu.HBM(advanced.shape, jnp.float32),
             pltpu.VMEM(u2.shape, jnp.float32),
             pltpu.VMEM(flat.shape, jnp.float32),
             pltpu.VMEM(snaps.shape, jnp.float32),
-            pltpu.VMEM((part, LANES), jnp.float32),
-            pltpu.VMEM((part, LANES), jnp.float32),
+            pltpu.VMEM((early.shape[0] + 8, LANES), jnp.float32),
         ],
-        input_output_aliases={12: 0, 13: 1, 14: 2, 15: 3},
+        input_output_aliases={13: 0, 14: 1, 15: 2, 16: 3},
         scratch_shapes=[
             pltpu.VMEM((comps, 2, 3, 8, nz), jnp.float32),
             pltpu.VMEM((comps, mask.shape[0], LANES), jnp.float32),
-            pltpu.VMEM((2 * part, LANES), jnp.float32),
             pltpu.SemaphoreType.DMA((2,)),
         ],
         compiler_params=pltpu.CompilerParams(vmem_limit_bytes=8 * 2**20),
@@ -488,11 +479,18 @@
             column = start + j + k
             spread.append(jnp.broadcast_to(pieces[0][:, column : column + 1], (h, LANES)))
         for k in range(GROUP):
-            pivot = spread[k][k : k + 1, :]
+            if k and k % 8 == 0:
+                done.append([piece[:8] for piece in pieces])
+                pieces = [piece[8:] for piece in pieces]
+                spread = [column[8:] for column in spread]
+                rows = rows[8:]
+                base += 8
+            i = k % 8
+            pivot = spread[k][i : i + 1, :]
             ratio = jnp.where(rows > j + k, spread[k], 0.0) * (1.0 / pivot)
             for l in range(k + 1, GROUP):
-                spread[l] = spread[l] - ratio * spread[l][k : k + 1, :]
-            pieces = [piece - ratio * piece[k : k + 1, :] for piece in pieces]
+                spread[l] = spread[l] - ratio * spread[l][i : i + 1, :]
+            pieces = [piece - ratio * piece[i : i + 1, :] for piece in pieces]
     done.append(pieces)
     pieces = [jnp.concatenate([d[q] for d in done], axis=0) for q in range(len(pieces))]
     row = lax.broadcasted_iota(jnp.int32, (n, LANES), 0)
@@ -503,24 +501,32 @@
 
 
 def basis_kernel(
-    root, w_ref, mine_ref, other_ref, modes_ref, snaps_ref, factor_ref, basis_ref, packed, inverse, factor, basis, sems
+    root, w_ref, mine_ref, other_ref, at_ref, modes_ref, snaps_ref, factor_ref, basis_ref, packed, inverse, factor, basis, sems
 ):
     total = factor.shape[0]
     half = total // 3
     two = 2 * half
-    part = mine_ref.shape[0]
+    part = total // 2
     core = lax.axis_index("grp") & 1
-    packed[pl.ds(pl.multiple_of(core * part, 8), part), :] = mine_ref[...]
-    packed[pl.ds(pl.multiple_of((1 - core) * part, 8), part), :] = other_ref[...]
+    packed[pl.ds(pl.multiple_of(core * part, 8), part), :] = mine_ref[0:part, :]
+    packed[pl.ds(pl.multiple_of((1 - core) * part, 8), part), :] = other_ref[0:part, :]
     row = lax.broadcasted_iota(jnp.int32, (half, LANES), 0)
     lane = lax.broadcasted_iota(jnp.int32, (half, LANES), 1)
+    place = at_ref[at_ref.shape[0] - 8 : at_ref.shape[0] - 7, :]
+    late = mine_ref[part:, :] + other_ref[part:, :]
+    with_modes = jnp.transpose(jnp.broadcast_to(late[0:1], (LANES, LANES)))
+    with_snaps = jnp.transpose(jnp.broadcast_to(late[1:2], (LANES, LANES)))[0:half]
+    here = lane == half + place
+    first_rows = jnp.where(here, with_modes[0:half], packed[0:half, :])
+    second_rows = jnp.where(here, with_modes[half:two], packed[half:two, :])
+    ends = jnp.where(here, with_snaps, packed[two:, :])
+    ends = jnp.where((row == place) & (lane >= half), pltpu.roll(late[1:2], half, 1), ends)
     left = lane < half
     eye = (row == lane).astype(jnp.float32)
     eye_right = (row + half == lane).astype(jnp.float32)
-    ends = packed[two:, :]
-    r0, w0 = eliminate([jnp.where(left, ends, eye_right), packed[0:half, :]], 0)
+    r0, w0 = eliminate([jnp.where(left, ends, eye_right), first_rows], 0)
     d = dot(w0, jnp.concatenate([r0, w0], axis=1), 0, 0)
-    r1, m1 = eliminate([packed[half:two, :] - d[0:half, LANES:], jnp.where(left, eye, -d[0:half, 0:LANES])], 0)
+    r1, m1 = eliminate([second_rows - d[0:half, LANES:], jnp.where(left, eye, -d[0:half, 0:LANES])], 0)
     e = dot(r1, jnp.concatenate([r1, m1], axis=1), 0, 0)[half:two]
     r2, m2 = eliminate(
         [
@@ -560,14 +566,14 @@
         copy.wait()
 
 
-def basis_call(root, weights, mine, other, modes, snaps):
+def basis_call(root, weights, mine, other, at, modes, snaps):
     k, width = modes.shape
     total = k + snaps.shape[0]
     vmem = pl.BlockSpec(memory_space=pltpu.VMEM)
     hbm = pl.BlockSpec(memory_space=pl.ANY)
     return pl.pallas_call(
         functools.partial(basis_kernel, root),
-        in_specs=[vmem] * 5,
+        in_specs=[vmem] * 6,
         out_specs=[hbm, hbm],
         out_shape=[pltpu.HBM((total, total), jnp.float32), pltpu.HBM((total, width), jnp.float32)],
         scratch_shapes=[
@@ -582,7 +588,7 @@
             flops=12 * total * total * width, bytes_accessed=8 * total * width, transcendentals=0
         ),
         name="factor_and_basis",
-    )(in_vmem(weights), in_vmem(mine), in_vmem(other), in_vmem(modes), in_vmem(snaps))
+    )(*(in_vmem(a) for a in (weights, mine, other, at, modes, snaps)))
 
 
 def ring(axis):
@@ -601,39 +607,41 @@
     ylow, yhigh, xlow, xhigh = faces(velocity)
     up_y, down_y = ring("tile")
     up, down = ring("grp")
+    xlo = lax.ppermute(xhigh, "grp", up)
+    xhi = lax.ppermute(xlow, "grp", down)
     ylo = lax.ppermute(yhigh, "tile", up_y)
     yhi = lax.ppermute(ylow, "tile", down_y)
-    xlo = lax.ppermute(xhigh, "grp", up)
-    xhi = lax.ppermute(xlow, "grp", down)
 
     weights = mode_weights.reshape(1, -1)
     comps, nx, ny, nz = velocity.shape
-    gram, snaps, tall, at, mask = early_gram(
-        (nx * ny, nz // LANES), snap_steps, weights, modes, history, slab_ids.reshape(-1, LANES)
+    p1, flat, u2 = inner_call(velocity)
+    early, beside, snaps, tall, at, mask = early_gram(
+        (nx * ny, nz // LANES), snap_steps, weights, modes, history, slab_ids.reshape(-1, LANES), p1
     )
 
-    p1, flat, u2 = inner_call(velocity)
-    p1, clow, chigh = halo_call(velocity, xlo, xhi, ylo, yhi, gram, p1)
+    clow, chigh = corners(ylo, yhi, early, p1)
+    beside = swap(beside, 1)
     clo = lax.ppermute(chigh, "grp", up)
     chi = lax.ppermute(clow, "grp", down)
-    flat, u2, advanced = outer_call(velocity, p1, flat, u2)
-    advanced, _, _, snaps, mine, other = sample_call(
-        at, mask, tall, xlo, xhi, clo, chi, clow, chigh, p1, modes, gram, advanced, u2, flat, snaps
+    p1, flat, u2, advanced = outer_call(velocity, xlo, xhi, ylo, yhi, p1, flat, u2)
+    advanced, _, _, snaps, mine = sample_call(
+        at, mask, tall, xlo, xhi, clo, chi, clow, chigh, p1, modes, early, beside, advanced, u2, flat, snaps
     )
 
     devices = lax.axis_size("tile") * lax.axis_size("grp")
-    mine = mine + swap(other, 1)
     bit = 2
     while bit < devices:
-        total = mine + swap(mine, bit)
         if 2 * bit < devices:
-            total = total + (swap(mine, 2 * bit) + swap(mine, 3 * bit))
+            far = swap(mine, 3 * bit)
+            total = mine + ((far + swap(mine, 2 * bit)) + swap(mine, bit))
+        else:
+            total = mine + swap(mine, bit)
         mine = total
         bit *= 4
     other = swap(mine, 1)
 
     root = math.sqrt(modes.shape[1] * devices)
-    factor, basis = basis_call(root, weights, mine, other, modes, snaps)
+    factor, basis = basis_call(root, weights, mine, other, at, modes, snaps)
     return (advanced, basis, factor)
 
 

time: 53.5 us -> 52.3 us (0.978)
  waiting for transfers between devices: 9.63 us -> 8.29 us
    ppermute x8, waiting for transfers between devices: 8.9 us -> 7.78 us  [swap(): lax.ppermute(array, ('tile', 'grp'), [(i, i ^ bits) for i in range(device...]
  transfers between devices with their start and end apart: 14 -> 14, of which waited for: 7 -> 7; matrix products, arithmetic and copies ran while one was open for 0% -> 0% of each run, Pallas kernels for 18% -> 22%
where the time goes in v5:
time: 52.3 us; the launch traced here: 52.1 us
  Pallas kernels  25 us (48%)
  starting transfers between devices  17.7 us (34%)
  waiting for transfers between devices  8.29 us (16%)
  between operations  0.99 us (2%)
    pallas_call x1, Pallas kernels, basis_call(): pl.pallas_call(functools.partial(basis_kernel, root), in_specs=[vmem] * 6...  8.34 us
    ppermute x8, starting transfers between devices, swap(): lax.ppermute(array, ('tile', 'grp'), [(i, i ^ bits) for i in range(device...  8.15 us
    ppermute x8, waiting for transfers between devices, swap(): lax.ppermute(array, ('tile', 'grp'), [(i, i ^ bits) for i in range(device...  7.78 us
    pallas_call x1, Pallas kernels, outer_call(): pl.pallas_call(outer_kernel, in_specs=[vmem] * 8, out_specs=[vmem, vmem,...  4.71 us
    pallas_call x1, Pallas kernels, inner_call(): pl.pallas_call(inner_kernel, in_specs=[vmem], out_specs=[vmem] * 3, out_s...  4.33 us
    pallas_call x1, Pallas kernels, sample_call(): pl.pallas_call(sample_kernel, in_specs=[pl.BlockSpec(memory_space=pltpu.S...  3.56 us
    ppermute x1, starting transfers between devices, per_device(): yhi = lax.ppermute(ylow, 'tile', down_y)  3.04 us
    pallas_call x1, Pallas kernels, early_gram(): pl.pallas_call(functools.partial(gram_kernel, lines), in_specs=[pl.BlockS...  2.58 us
  transfers between devices with their start and end apart: 14, of which 7 were waited for; matrix products, arithmetic and copies ran while one was open for 0% of the time, Pallas kernels for 22%

profile of v5, /device:TPU:0, one launch (start us, length us, event | category | flops | bytes accessed | tf_op | source)
XLA Modules:
  0.0 52.1 jit_solution(8680046726366751843)
XLA Ops:
  0.6 0.0 copy-start
  0.6 0.0 copy-start.5
  0.7 0.0 copy-start.3
  0.7 0.0 copy-start.4
  0.7 0.0 copy-start.1
  0.7 0.0 copy-start.2
  0.7 1.5 %faces.1 = (f32[3,16,2,512]{3,2,1,0:T(2,128)S(1)}, f32[3,16,2,512]{3,2,1,0:T(2,128)S(1)}, f32[3,2,32,512]{3,2,1,0:T(8,128)S(1)}, f32[3,2,32,512]{3,2,1,0:T(8,128)S(1)}) custom-call(f32[3,16,32,512]{3,2,1,0:T(8,128)} %velocity_ref.5), custom_call_target="tpu_custom_call" | custom-call | tf_op jit(solution)/shard_map/faces/pallas_call | solution.py:52
  2.2 0.5 collective-permute-start
  2.7 2.0 %collective-permute-start.1 = (f32[3,2,32,512]{3,2,1,0:T(8,128)S(1)}, f32[3,2,32,512]{3,2,1,0:T(8,128)S(1)}, u32[]{:S(2)}, u32[]{:S(2)}) collective-permute-start(f32[3,2,32,512]{3,2,1,0:T(8,128)S(1)} %get-tuple-element.32), channel_id=1, source_target_pairs={{0,3},{1,0},{2,1},{3,2},{4,7},{5,4},{6,5},{7,6},{8,11},{9,8},{10,9... | collective-permute-start | bytes 1179656 | tf_op jit(solution)/shard_map/ppermute | solution.py:611
  4.7 2.3 %collective-permute-start.2 = (f32[3,16,2,512]{3,2,1,0:T(2,128)S(1)}, f32[3,16,2,512]{3,2,1,0:T(2,128)S(1)}, u32[]{:S(2)}, u32[]{:S(2)}) collective-permute-start(f32[3,16,2,512]{3,2,1,0:T(2,128)S(1)} %get-tuple-element.33), channel_id=1, source_target_pairs={{0,4},{4,8},{8,12},{12,16},{16,20},{20,24},{24,28},{28,0},{1,5},{5... | collective-permute-start | bytes 589832 | tf_op jit(solution)/shard_map/ppermute | solution.py:612
  7.0 3.0 %collective-permute-start.3 = (f32[3,16,2,512]{3,2,1,0:T(2,128)S(1)}, f32[3,16,2,512]{3,2,1,0:T(2,128)S(1)}, u32[]{:S(2)}, u32[]{:S(2)}) collective-permute-start(f32[3,16,2,512]{3,2,1,0:T(2,128)S(1)} %get-tuple-element.34), channel_id=1, source_target_pairs={{0,28},{4,0},{8,4},{12,8},{16,12},{20,16},{24,20},{28,24},{1,29},{... | collective-permute-start | bytes 589832 | tf_op jit(solution)/shard_map/ppermute | solution.py:613
  10.0 0.0 copy-done
  10.0 4.3 %inner_cells.1 = (f32[3,18,40,512]{3,2,1,0:T(8,128)S(1)}, f32[3,2048,128]{2,1,0:T(8,128)S(1)}, f32[3,16,32,512]{3,2,1,0:T(8,128)S(1)}) custom-call(f32[3,16,32,512]{3,2,1,0:T(8,128)S(1)} %copy-done), custom_call_target="tpu_custom_call" | custom-call | flops 47185920 | bytes 3145728 | tf_op jit(solution)/shard_map/inner_cells/pallas_call | solution.py:314
  14.3 0.0 copy-done.5
  14.4 0.0 copy-done.3
  14.4 0.0 copy-done.4
  14.4 0.0 copy-done.1
  14.4 0.0 copy-done.2
  14.4 2.6 %early_gram.1 = (f32[96,128]{1,0:T(8,128)S(1)}, f32[96,128]{1,0:T(8,128)S(1)}, f32[64,3072]{1,0:T(8,128)S(1)}, f32[128,128]{1,0:T(8,128)S(1)}, s32[16,128]{1,0:T(8,128)S(1)}, /*index=5*/f32[1024,128]{1,0:T(8,128)S(1)}) custom-call(s32[64]{0:T(128)S(1)} %copy-done.4, f32[1,128]{1,0:T(1,128)S(1)} %bitcast.3, f32[128,3072]{1,0:T(8,128)S(1)} %copy-done.1, ...), custom_call_target="tpu_custom_call" | custom-call | flops 905969664 | bytes 7077888 | tf_op jit(solution)/shard_map/early_gram/pallas_call | solution.py:125
  17.0 0.1 collective-permute-start.6
  17.1 0.0 collective-permute-done.2.ylo_ref
  17.1 0.5 collective-permute-done.3.yhi_ref
  17.6 0.1 collective-permute-start.4
  17.6 1.7 %collective-permute-start.5 = (f32[3,2,512]{2,1,0:T(2,128)S(1)}, f32[3,2,512]{2,1,0:T(2,128)S(1)}, u32[]{:S(2)}, u32[]{:S(2)}) collective-permute-start(f32[3,2,512]{2,1,0:T(2,128)S(1)} %get-tuple-element.37.own_lo_ref), channel_id=1, source_target_pairs={{0,3},{1,0},{2,1},{3,2},{4,7},{5,4},{6,5},{7,6},{8,11},{9,8},{10,9... | collective-permute-start | bytes 36872 | tf_op jit(solution)/shard_map/ppermute | solution.py:625
  19.4 0.0 collective-permute-done.xlo_ref
  19.4 0.0 collective-permute-done.1.xhi_ref
  19.4 4.7 %outer_cells.1 = (f32[3,18,40,512]{3,2,1,0:T(8,128)S(1)}, f32[3,2048,128]{2,1,0:T(8,128)S(1)}, f32[3,16,32,512]{3,2,1,0:T(8,128)S(1)}, f32[3,16,32,512]{3,2,1,0:T(8,128)}) custom-call(f32[3,16,32,512]{3,2,1,0:T(8,128)S(1)} %copy-done, f32[3,2,32,512]{3,2,1,0:T(8,128)S(1)} %collective-permute-done.xlo_ref, ...), custom_call_target="tpu_custom_call", output_to_operand_aliasing={{0}: (5, {}), {1}: (6, {}), {2}: (7, {})} | custom-call | flops 31457280 | bytes 3145728 | tf_op jit(solution)/shard_map/outer_cells/pallas_call | solution.py:330
  24.1 0.0 collective-permute-done.6.beside_ref
  24.1 0.0 collective-permute-done.4.clo_ref
  24.1 0.0 collective-permute-done.5.chi_ref
  24.1 3.6 %sample_and_gram.1 = (f32[3,16,32,512]{3,2,1,0:T(8,128)}, f32[3,16,32,512]{3,2,1,0:T(8,128)S(1)}, f32[3,2048,128]{2,1,0:T(8,128)S(1)}, f32[64,3072]{1,0:T(8,128)S(1)}, f32[104,128]{1,0:T(8,128)S(1)}) custom-call(s32[16,128]{1,0:T(8,128)S(1)} %get-tuple-element.28.at_ref, ...), custom_call_target="tpu_custom_call", output_to_operand_aliasing={{0}: (13, {}), {1}: (14, {}), {2}: (15, {}), {3}: (16, {})} | custom-call | flops 15728640 | bytes 1572864 | tf_op jit(solution)/shard_map/sample_and_gram/pallas_call | solution.py:441
  27.7 0.3 collective-permute-start.7
  28.0 2.4 %collective-permute-start.8 = (f32[104,128]{1,0:T(8,128)S(1)}, f32[104,128]{1,0:T(8,128)S(1)}, u32[]{:S(2)}, u32[]{:S(2)}) collective-permute-start(f32[104,128]{1,0:T(8,128)S(1)} %get-tuple-element.47), channel_id=1, source_target_pairs={{0,4},{1,5},{2,6},{3,7},{4,0},{5,1},{6,2},{7,3},{8,12},{9,13},{10,... | collective-permute-start | bytes 159752 | tf_op jit(solution)/shard_map/ppermute | solution.py:603
  30.4 0.9 %collective-permute-start.9 = (f32[104,128]{1,0:T(8,128)S(1)}, f32[104,128]{1,0:T(8,128)S(1)}, u32[]{:S(2)}, u32[]{:S(2)}) collective-permute-start(f32[104,128]{1,0:T(8,128)S(1)} %get-tuple-element.47), channel_id=1, source_target_pairs={{0,2},{1,3},{2,0},{3,1},{4,6},{5,7},{6,4},{7,5},{8,10},{9,11},{10,... | collective-permute-start | bytes 159752 | tf_op jit(solution)/shard_map/ppermute | solution.py:603
  31.3 1.7 %collective-permute-done.7 = f32[104,128]{1,0:T(8,128)S(1)} collective-permute-done((f32[104,128]{1,0:T(8,128)S(1)}, f32[104,128]{1,0:T(8,128)S(1)}, u32[]{:S(2)}, u32[]{:S(2)}) %collective-permute-start.7) | collective-permute-done | bytes 53280 | tf_op jit(solution)/shard_map/ppermute | solution.py:603
  32.9 0.2 collective-permute-done.8
  33.1 1.5 %collective-permute-done.9 = f32[104,128]{1,0:T(8,128)S(1)} collective-permute-done((f32[104,128]{1,0:T(8,128)S(1)}, f32[104,128]{1,0:T(8,128)S(1)}, u32[]{:S(2)}, u32[]{:S(2)}) %collective-permute-start.9) | collective-permute-done | bytes 53280 | tf_op jit(solution)/shard_map/ppermute | solution.py:603
  34.6 2.7 %collective-permute-start.10 = (f32[104,128]{1,0:T(8,128)S(1)}, f32[104,128]{1,0:T(8,128)S(1)}, u32[]{:S(2)}, u32[]{:S(2)}) collective-permute-start(f32[104,128]{1,0:T(8,128)S(1)} %add_add_fusion.1), channel_id=1, source_target_pairs={{0,24},{1,25},{2,26},{3,27},{4,28},{5,29},{6,30},{7,31},{8,16},{9,... | collective-permute-start | bytes 159752 | tf_op jit(solution)/shard_map/ppermute | solution.py:603
  37.2 0.0 collective-permute-start.11
  37.2 1.8 %collective-permute-start.12 = (f32[104,128]{1,0:T(8,128)S(1)}, f32[104,128]{1,0:T(8,128)S(1)}, u32[]{:S(2)}, u32[]{:S(2)}) collective-permute-start(f32[104,128]{1,0:T(8,128)S(1)} %add_add_fusion.1), channel_id=1, source_target_pairs={{0,8},{1,9},{2,10},{3,11},{4,12},{5,13},{6,14},{7,15},{8,0},{9,1},... | collective-permute-start | bytes 159752 | tf_op jit(solution)/shard_map/ppermute | solution.py:603
  39.0 1.8 %collective-permute-done.10 = f32[104,128]{1,0:T(8,128)S(1)} collective-permute-done((f32[104,128]{1,0:T(8,128)S(1)}, f32[104,128]{1,0:T(8,128)S(1)}, u32[]{:S(2)}, u32[]{:S(2)}) %collective-permute-start.10) | collective-permute-done | bytes 53280 | tf_op jit(solution)/shard_map/ppermute | solution.py:603
  40.8 1.5 %collective-permute-done.11 = f32[104,128]{1,0:T(8,128)S(1)} collective-permute-done((f32[104,128]{1,0:T(8,128)S(1)}, f32[104,128]{1,0:T(8,128)S(1)}, u32[]{:S(2)}, u32[]{:S(2)}) %collective-permute-start.11) | collective-permute-done | bytes 53280 | tf_op jit(solution)/shard_map/ppermute | solution.py:603
  42.3 0.0 collective-permute-done.12
  42.3 0.1 collective-permute-start.13
  42.4 1.2 %collective-permute-done.13.other_ref = f32[104,128]{1,0:T(8,128)S(1)} collective-permute-done((f32[104,128]{1,0:T(8,128)S(1)}, f32[104,128]{1,0:T(8,128)S(1)}, u32[]{:S(2)}, u32[]{:S(2)}) %collective-permute-start.13) | collective-permute-done | bytes 53280 | tf_op jit(solution)/shard_map/ppermute | solution.py:603
  43.6 8.3 %factor_and_basis.1 = (f32[192,192]{1,0:T(8,128)}, f32[192,3072]{1,0:T(8,128)}) custom-call(f32[1,128]{1,0:T(1,128)S(1)} %bitcast.4, f32[104,128]{1,0:T(8,128)S(1)} %add_add_fusion.mine_ref, f32[104,128]{1,0:T(8,128)S(1)} %collective-permute-done.13.other_ref, s32[16,128]{1,0:T(8,128)S(1)} %get-tuple-element.28.at_ref, f32[128,3072]{1,0:T(8,128)S(1)} %copy-done.1, ...), custom_call_target="tpu_custom_call" | custom-call | flops 1358954496 | bytes 4718592 | tf_op jit(solution)/shard_map/factor_and_basis/pallas_call | solution.py:574
  (3 shorter events, 0.0 us)
Async XLA Ops:
  0.6 9.4 %copy-start = (f32[3,16,32,512]{3,2,1,0:T(8,128)S(1)}, f32[3,16,32,512]{3,2,1,0:T(8,128)}, u32[]{:S(2)}) copy-start(f32[3,16,32,512]{3,2,1,0:T(8,128)} %velocity_ref.5) | copy-start | bytes 9437188
  0.6 13.7 %copy-start.5 = (f32[128]{0:T(128)S(1)}, f32[128]{0:T(128)}, u32[]{:S(2)}) copy-start(f32[128]{0:T(128)} %param.8) | copy-start | bytes 1540
  0.7 13.7 %copy-start.3 = (s32[1024]{0:T(1024)S(1)}, s32[1024]{0:T(1024)}, u32[]{:S(2)}) copy-start(s32[1024]{0:T(1024)} %param.10) | copy-start | bytes 12292
  0.7 13.7 %copy-start.4 = (s32[64]{0:T(128)S(1)}, s32[64]{0:T(128)}, u32[]{:S(2)}) copy-start(s32[64]{0:T(128)} %steps_ref.1) | copy-start | bytes 772
  0.7 13.7 %copy-start.1 = (f32[128,3072]{1,0:T(8,128)S(1)}, f32[128,3072]{1,0:T(8,128)}, u32[]{:S(2)}) copy-start(f32[128,3072]{1,0:T(8,128)} %modes_ref.5) | copy-start | bytes 4718596
  0.7 13.7 %copy-start.2 = (f32[63,3072]{1,0:T(8,128)S(1)}, f32[63,3072]{1,0:T(8,128)}, u32[]{:S(2)}) copy-start(f32[63,3072]{1,0:T(8,128)} %history_ref.1) | copy-start | bytes 2322436
  2.2 17.2 %collective-permute-start = (f32[3,2,32,512]{3,2,1,0:T(8,128)S(1)}, f32[3,2,32,512]{3,2,1,0:T(8,128)S(1)}, u32[]{:S(2)}, u32[]{:S(2)}) collective-permute-start(f32[3,2,32,512]{3,2,1,0:T(8,128)S(1)} %get-tuple-element.31), channel_id=1, source_target_pairs={{0,1},{1,2},{2,3},{3,0},{4,5},{5,6},{6,7},{7,4},{8,9},{9,10},{10,1... | collective-permute-start | bytes 1179656 | tf_op jit(solution)/shard_map/ppermute | solution.py:610
  2.7 16.7 %collective-permute-start.1 = (f32[3,2,32,512]{3,2,1,0:T(8,128)S(1)}, f32[3,2,32,512]{3,2,1,0:T(8,128)S(1)}, u32[]{:S(2)}, u32[]{:S(2)}) collective-permute-start(f32[3,2,32,512]{3,2,1,0:T(8,128)S(1)} %get-tuple-element.32), channel_id=1, source_target_pairs={{0,3},{1,0},{2,1},{3,2},{4,7},{5,4},{6,5},{7,6},{8,11},{9,8},{10,9... | collective-permute-start | bytes 1179656 | tf_op jit(solution)/shard_map/ppermute | solution.py:611
  4.7 12.4 %collective-permute-start.2 = (f32[3,16,2,512]{3,2,1,0:T(2,128)S(1)}, f32[3,16,2,512]{3,2,1,0:T(2,128)S(1)}, u32[]{:S(2)}, u32[]{:S(2)}) collective-permute-start(f32[3,16,2,512]{3,2,1,0:T(2,128)S(1)} %get-tuple-element.33), channel_id=1, source_target_pairs={{0,4},{4,8},{8,12},{12,16},{16,20},{20,24},{24,28},{28,0},{1,5},{5... | collective-permute-start | bytes 589832 | tf_op jit(solution)/shard_map/ppermute | solution.py:612
  7.0 10.6 %collective-permute-start.3 = (f32[3,16,2,512]{3,2,1,0:T(2,128)S(1)}, f32[3,16,2,512]{3,2,1,0:T(2,128)S(1)}, u32[]{:S(2)}, u32[]{:S(2)}) collective-permute-start(f32[3,16,2,512]{3,2,1,0:T(2,128)S(1)} %get-tuple-element.34), channel_id=1, source_target_pairs={{0,28},{4,0},{8,4},{12,8},{16,12},{20,16},{24,20},{28,24},{1,29},{... | collective-permute-start | bytes 589832 | tf_op jit(solution)/shard_map/ppermute | solution.py:613
  17.0 7.1 %collective-permute-start.6 = (f32[96,128]{1,0:T(8,128)S(1)}, f32[96,128]{1,0:T(8,128)S(1)}, u32[]{:S(2)}, u32[]{:S(2)}) collective-permute-start(f32[96,128]{1,0:T(8,128)S(1)} %get-tuple-element.41), channel_id=1, source_target_pairs={{0,1},{1,0},{2,3},{3,2},{4,5},{5,4},{6,7},{7,6},{8,9},{9,8},{10,11... | collective-permute-start | bytes 147464 | tf_op jit(solution)/shard_map/ppermute | solution.py:603
  17.6 6.5 %collective-permute-start.4 = (f32[3,2,512]{2,1,0:T(2,128)S(1)}, f32[3,2,512]{2,1,0:T(2,128)S(1)}, u32[]{:S(2)}, u32[]{:S(2)}) collective-permute-start(f32[3,2,512]{2,1,0:T(2,128)S(1)} %get-tuple-element.36.own_hi_ref), channel_id=1, source_target_pairs={{0,1},{1,2},{2,3},{3,0},{4,5},{5,6},{6,7},{7,4},{8,9},{9,10},{10,1... | collective-permute-start | bytes 36872 | tf_op jit(solution)/shard_map/ppermute | solution.py:624
  17.6 6.5 %collective-permute-start.5 = (f32[3,2,512]{2,1,0:T(2,128)S(1)}, f32[3,2,512]{2,1,0:T(2,128)S(1)}, u32[]{:S(2)}, u32[]{:S(2)}) collective-permute-start(f32[3,2,512]{2,1,0:T(2,128)S(1)} %get-tuple-element.37.own_lo_ref), channel_id=1, source_target_pairs={{0,3},{1,0},{2,1},{3,2},{4,7},{5,4},{6,5},{7,6},{8,11},{9,8},{10,9... | collective-permute-start | bytes 36872 | tf_op jit(solution)/shard_map/ppermute | solution.py:625
  27.7 5.2 %collective-permute-start.7 = (f32[104,128]{1,0:T(8,128)S(1)}, f32[104,128]{1,0:T(8,128)S(1)}, u32[]{:S(2)}, u32[]{:S(2)}) collective-permute-start(f32[104,128]{1,0:T(8,128)S(1)} %get-tuple-element.47), channel_id=1, source_target_pairs={{0,6},{1,7},{2,4},{3,5},{4,2},{5,3},{6,0},{7,1},{8,14},{9,15},{10,... | collective-permute-start | bytes 159752 | tf_op jit(solution)/shard_map/ppermute | solution.py:603
  28.0 5.1 %collective-permute-start.8 = (f32[104,128]{1,0:T(8,128)S(1)}, f32[104,128]{1,0:T(8,128)S(1)}, u32[]{:S(2)}, u32[]{:S(2)}) collective-permute-start(f32[104,128]{1,0:T(8,128)S(1)} %get-tuple-element.47), channel_id=1, source_target_pairs={{0,4},{1,5},{2,6},{3,7},{4,0},{5,1},{6,2},{7,3},{8,12},{9,13},{10,... | collective-permute-start | bytes 159752 | tf_op jit(solution)/shard_map/ppermute | solution.py:603
  30.4 4.1 %collective-permute-start.9 = (f32[104,128]{1,0:T(8,128)S(1)}, f32[104,128]{1,0:T(8,128)S(1)}, u32[]{:S(2)}, u32[]{:S(2)}) collective-permute-start(f32[104,128]{1,0:T(8,128)S(1)} %get-tuple-element.47), channel_id=1, source_target_pairs={{0,2},{1,3},{2,0},{3,1},{4,6},{5,7},{6,4},{7,5},{8,10},{9,11},{10,... | collective-permute-start | bytes 159752 | tf_op jit(solution)/shard_map/ppermute | solution.py:603
  34.6 6.2 %collective-permute-start.10 = (f32[104,128]{1,0:T(8,128)S(1)}, f32[104,128]{1,0:T(8,128)S(1)}, u32[]{:S(2)}, u32[]{:S(2)}) collective-permute-start(f32[104,128]{1,0:T(8,128)S(1)} %add_add_fusion.1), channel_id=1, source_target_pairs={{0,24},{1,25},{2,26},{3,27},{4,28},{5,29},{6,30},{7,31},{8,16},{9,... | collective-permute-start | bytes 159752 | tf_op jit(solution)/shard_map/ppermute | solution.py:603
  37.2 5.0 %collective-permute-start.11 = (f32[104,128]{1,0:T(8,128)S(1)}, f32[104,128]{1,0:T(8,128)S(1)}, u32[]{:S(2)}, u32[]{:S(2)}) collective-permute-start(f32[104,128]{1,0:T(8,128)S(1)} %add_add_fusion.1), channel_id=1, source_target_pairs={{0,16},{1,17},{2,18},{3,19},{4,20},{5,21},{6,22},{7,23},{8,24},{9,... | collective-permute-start | bytes 159752 | tf_op jit(solution)/shard_map/ppermute | solution.py:603
  37.2 5.0 %collective-permute-start.12 = (f32[104,128]{1,0:T(8,128)S(1)}, f32[104,128]{1,0:T(8,128)S(1)}, u32[]{:S(2)}, u32[]{:S(2)}) collective-permute-start(f32[104,128]{1,0:T(8,128)S(1)} %add_add_fusion.1), channel_id=1, source_target_pairs={{0,8},{1,9},{2,10},{3,11},{4,12},{5,13},{6,14},{7,15},{8,0},{9,1},... | collective-permute-start | bytes 159752 | tf_op jit(solution)/shard_map/ppermute | solution.py:603
  42.3 1.3 %collective-permute-start.13 = (f32[104,128]{1,0:T(8,128)S(1)}, f32[104,128]{1,0:T(8,128)S(1)}, u32[]{:S(2)}, u32[]{:S(2)}) collective-permute-start(f32[104,128]{1,0:T(8,128)S(1)} %add_add_fusion.mine_ref), channel_id=1, source_target_pairs={{0,1},{1,0},{2,3},{3,2},{4,5},{5,4},{6,7},{7,6},{8,9},{9,8},{10,11... | collective-permute-start | bytes 159752 | tf_op jit(solution)/shard_map/ppermute | solution.py:603

commit v6 on v5

--- a/solution.py
+++ b/solution.py
@@ -183,13 +183,13 @@
 
     first_layer(0)
 
-    @pl.loop(1, nx - 1)
+    @pl.loop(1, nx - 1, unroll=2)
     def _(x):
         first_layer(x)
 
     first_layer(nx - 1)
 
-    @pl.loop(2, nx - 2)
+    @pl.loop(2, nx - 2, unroll=2)
     def _(x):
         second_layer(p1, u2, flat, x, range(1, inner - 1))
 
@@ -275,7 +275,7 @@
     layer(nx, (vel, xhi_ref, xhi_ref), (nx - 1, 0, 1), range(inner))
     layer(0, (vel, vel, vel), (0, 0, 1), (inner,))
 
-    @pl.loop(1, nx - 1)
+    @pl.loop(1, nx - 1, unroll=True)
     def _(x):
         layer(x, (vel, vel, vel), (x - 1, x, x + 1), (inner,))
 
@@ -284,7 +284,7 @@
     def out_copy(x):
         return pltpu.make_async_copy(u2.at[:, x], advanced_ref.at[:, x], out_sems.at[x])
 
-    @pl.loop(2, nx - 2)
+    @pl.loop(2, nx - 2, unroll=True)
     def _(x):
         second_layer(p1, u2, flat, x, (0, inner - 1))
         out_copy(x).start()
@@ -343,11 +343,13 @@
 
 
 def sample_kernel(
-    at_ref, mask_ref, tall_ref, xlo_ref, xhi_ref, clo_ref, chi_ref, own_lo_ref, own_hi_ref,
+    at_in, mask_ref, tall_ref, xlo_ref, xhi_ref, clo_ref, chi_ref, own_lo_ref, own_hi_ref,
     p1, modes_ref, early_ref, beside_ref, advanced_in, u2_in, flat_in, snaps_in,
     advanced_ref, u2, flat, snaps_ref, sum_ref,
-    fixed, picked, sems,
+    fixed, picked, at_ref, sems,
 ):
+    at_copy = pltpu.make_async_copy(at_in, at_ref, sems.at[2])
+    at_copy.start()
     comps, _, ny, nz = xlo_ref.shape
     nx = flat.shape[1] * LANES // (ny * nz)
     inner = ny // 8
@@ -398,6 +400,7 @@
 
     count = mask_ref.shape[0]
     groups = count // LANES
+    at_copy.wait()
 
     @pl.loop(0, groups)
     def _(g):
@@ -440,7 +443,7 @@
     ins = (at, mask, tall, xlo, xhi, clo, chi, own_lo, own_hi, p1, modes, early, beside)
     return pl.pallas_call(
         sample_kernel,
-        in_specs=[pl.BlockSpec(memory_space=pltpu.SMEM)] + [vmem] * 12 + [hbm, vmem, vmem, vmem],
+        in_specs=[vmem] * 13 + [hbm, vmem, vmem, vmem],
         out_specs=[hbm] + [vmem] * 4,
         out_shape=[
             pltpu.HBM(advanced.shape, jnp.float32),
@@ -453,7 +456,8 @@
         scratch_shapes=[
             pltpu.VMEM((comps, 2, 3, 8, nz), jnp.float32),
             pltpu.VMEM((comps, mask.shape[0], LANES), jnp.float32),
-            pltpu.SemaphoreType.DMA((2,)),
+            pltpu.SMEM(at.shape, jnp.int32),
+            pltpu.SemaphoreType.DMA((3,)),
         ],
         compiler_params=pltpu.CompilerParams(vmem_limit_bytes=8 * 2**20),
         cost_estimate=pl.CostEstimate(

time: 52.3 us -> 51.1 us (0.977)
  Pallas kernels: 25 us -> 23.3 us
  waiting for transfers between devices: 8.29 us -> 8.9 us
    pallas_call x1, Pallas kernels: 4.71 us -> 3.68 us  [outer_call(): pl.pallas_call(outer_kernel, in_specs=[vmem] * 8, out_specs=[vmem, vmem,...]
    pallas_call x1, Pallas kernels: 4.33 us -> 3.71 us  [inner_call(): pl.pallas_call(inner_kernel, in_specs=[vmem], out_specs=[vmem] * 3, out_s...]
    ppermute x1, waiting for transfers between devices: 0.49 us -> 1.11 us  [per_device(): yhi = lax.ppermute(ylow, 'tile', down_y)]
  transfers between devices with their start and end apart: 14 -> 14, of which waited for: 7 -> 6; matrix products, arithmetic and copies ran while one was open for 0% -> 0% of each run, Pallas kernels for 22% -> 20%
where the time goes in v6:
time: 51.1 us; the launch traced here: 51 us
  Pallas kernels  23.3 us (46%)
  starting transfers between devices  17.7 us (35%)
  waiting for transfers between devices  8.9 us (17%)
  between operations  0.99 us (2%)
    pallas_call x1, Pallas kernels, basis_call(): pl.pallas_call(functools.partial(basis_kernel, root), in_specs=[vmem] * 6...  8.34 us
    ppermute x8, starting transfers between devices, swap(): lax.ppermute(array, ('tile', 'grp'), [(i, i ^ bits) for i in range(device...  8.15 us
    ppermute x8, waiting for transfers between devices, swap(): lax.ppermute(array, ('tile', 'grp'), [(i, i ^ bits) for i in range(device...  7.78 us
    pallas_call x1, Pallas kernels, inner_call(): pl.pallas_call(inner_kernel, in_specs=[vmem], out_specs=[vmem] * 3, out_s...  3.71 us
    pallas_call x1, Pallas kernels, outer_call(): pl.pallas_call(outer_kernel, in_specs=[vmem] * 8, out_specs=[vmem, vmem,...  3.68 us
    pallas_call x1, Pallas kernels, sample_call(): pl.pallas_call(sample_kernel, in_specs=[vmem] * 13 + [hbm, vmem, vmem, vm...  3.47 us
    ppermute x1, starting transfers between devices, per_device(): yhi = lax.ppermute(ylow, 'tile', down_y)  3.04 us
    pallas_call x1, Pallas kernels, early_gram(): pl.pallas_call(functools.partial(gram_kernel, lines), in_specs=[pl.BlockS...  2.58 us
  transfers between devices with their start and end apart: 14, of which 6 were waited for; matrix products, arithmetic and copies ran while one was open for 0% of the time, Pallas kernels for 20%

profile of v6, /device:TPU:0, one launch (start us, length us, event | category | flops | bytes accessed | tf_op | source)
XLA Modules:
  0.0 51.0 jit_solution(13518566097719503445)
XLA Ops:
  0.6 0.0 copy-start
  0.6 0.0 copy-start.5
  0.7 0.0 copy-start.3
  0.7 0.0 copy-start.4
  0.7 0.0 copy-start.1
  0.7 0.0 copy-start.2
  0.7 1.5 %faces.1 = (f32[3,16,2,512]{3,2,1,0:T(2,128)S(1)}, f32[3,16,2,512]{3,2,1,0:T(2,128)S(1)}, f32[3,2,32,512]{3,2,1,0:T(8,128)S(1)}, f32[3,2,32,512]{3,2,1,0:T(8,128)S(1)}) custom-call(f32[3,16,32,512]{3,2,1,0:T(8,128)} %velocity_ref.5), custom_call_target="tpu_custom_call" | custom-call | tf_op jit(solution)/shard_map/faces/pallas_call | solution.py:52
  2.2 0.5 collective-permute-start
  2.7 2.0 %collective-permute-start.1 = (f32[3,2,32,512]{3,2,1,0:T(8,128)S(1)}, f32[3,2,32,512]{3,2,1,0:T(8,128)S(1)}, u32[]{:S(2)}, u32[]{:S(2)}) collective-permute-start(f32[3,2,32,512]{3,2,1,0:T(8,128)S(1)} %get-tuple-element.32), channel_id=1, source_target_pairs={{0,3},{1,0},{2,1},{3,2},{4,7},{5,4},{6,5},{7,6},{8,11},{9,8},{10,9... | collective-permute-start | bytes 1179656 | tf_op jit(solution)/shard_map/ppermute | solution.py:615
  4.7 2.3 %collective-permute-start.2 = (f32[3,16,2,512]{3,2,1,0:T(2,128)S(1)}, f32[3,16,2,512]{3,2,1,0:T(2,128)S(1)}, u32[]{:S(2)}, u32[]{:S(2)}) collective-permute-start(f32[3,16,2,512]{3,2,1,0:T(2,128)S(1)} %get-tuple-element.33), channel_id=1, source_target_pairs={{0,4},{4,8},{8,12},{12,16},{16,20},{20,24},{24,28},{28,0},{1,5},{5... | collective-permute-start | bytes 589832 | tf_op jit(solution)/shard_map/ppermute | solution.py:616
  7.0 3.0 %collective-permute-start.3 = (f32[3,16,2,512]{3,2,1,0:T(2,128)S(1)}, f32[3,16,2,512]{3,2,1,0:T(2,128)S(1)}, u32[]{:S(2)}, u32[]{:S(2)}) collective-permute-start(f32[3,16,2,512]{3,2,1,0:T(2,128)S(1)} %get-tuple-element.34), channel_id=1, source_target_pairs={{0,28},{4,0},{8,4},{12,8},{16,12},{20,16},{24,20},{28,24},{1,29},{... | collective-permute-start | bytes 589832 | tf_op jit(solution)/shard_map/ppermute | solution.py:617
  10.0 0.0 copy-done
  10.0 3.7 %inner_cells.1 = (f32[3,18,40,512]{3,2,1,0:T(8,128)S(1)}, f32[3,2048,128]{2,1,0:T(8,128)S(1)}, f32[3,16,32,512]{3,2,1,0:T(8,128)S(1)}) custom-call(f32[3,16,32,512]{3,2,1,0:T(8,128)S(1)} %copy-done), custom_call_target="tpu_custom_call" | custom-call | flops 47185920 | bytes 3145728 | tf_op jit(solution)/shard_map/inner_cells/pallas_call | solution.py:314
  13.7 0.0 copy-done.5
  13.7 0.0 copy-done.3
  13.7 0.0 copy-done.4
  13.8 0.0 copy-done.1
  13.8 0.0 copy-done.2
  13.8 2.6 %early_gram.1 = (f32[96,128]{1,0:T(8,128)S(1)}, f32[96,128]{1,0:T(8,128)S(1)}, f32[64,3072]{1,0:T(8,128)S(1)}, f32[128,128]{1,0:T(8,128)S(1)}, s32[16,128]{1,0:T(8,128)S(1)}, /*index=5*/f32[1024,128]{1,0:T(8,128)S(1)}) custom-call(s32[64]{0:T(128)S(1)} %copy-done.4, f32[1,128]{1,0:T(1,128)S(1)} %bitcast.3, f32[128,3072]{1,0:T(8,128)S(1)} %copy-done.1, ...), custom_call_target="tpu_custom_call" | custom-call | flops 905969664 | bytes 7077888 | tf_op jit(solution)/shard_map/early_gram/pallas_call | solution.py:125
  16.4 0.1 collective-permute-start.6
  16.4 0.0 collective-permute-done.2.ylo_ref
  16.5 1.1 %collective-permute-done.3.yhi_ref = f32[3,16,2,512]{3,2,1,0:T(2,128)S(1)} collective-permute-done((f32[3,16,2,512]{3,2,1,0:T(2,128)S(1)}, f32[3,16,2,512]{3,2,1,0:T(2,128)S(1)}, u32[]{:S(2)}, u32[]{:S(2)}) %collective-permute-start.3) | collective-permute-done | bytes 196640 | tf_op jit(solution)/shard_map/ppermute | solution.py:617
  17.6 0.1 collective-permute-start.4
  17.6 1.7 %collective-permute-start.5 = (f32[3,2,512]{2,1,0:T(2,128)S(1)}, f32[3,2,512]{2,1,0:T(2,128)S(1)}, u32[]{:S(2)}, u32[]{:S(2)}) collective-permute-start(f32[3,2,512]{2,1,0:T(2,128)S(1)} %get-tuple-element.37.own_lo_ref), channel_id=1, source_target_pairs={{0,3},{1,0},{2,1},{3,2},{4,7},{5,4},{6,5},{7,6},{8,11},{9,8},{10,9... | collective-permute-start | bytes 36872 | tf_op jit(solution)/shard_map/ppermute | solution.py:629
  19.4 0.0 collective-permute-done.xlo_ref
  19.4 0.0 collective-permute-done.1.xhi_ref
  19.4 3.7 %outer_cells.1 = (f32[3,18,40,512]{3,2,1,0:T(8,128)S(1)}, f32[3,2048,128]{2,1,0:T(8,128)S(1)}, f32[3,16,32,512]{3,2,1,0:T(8,128)S(1)}, f32[3,16,32,512]{3,2,1,0:T(8,128)}) custom-call(f32[3,16,32,512]{3,2,1,0:T(8,128)S(1)} %copy-done, f32[3,2,32,512]{3,2,1,0:T(8,128)S(1)} %collective-permute-done.xlo_ref, ...), custom_call_target="tpu_custom_call", output_to_operand_aliasing={{0}: (5, {}), {1}: (6, {}), {2}: (7, {})} | custom-call | flops 31457280 | bytes 3145728 | tf_op jit(solution)/shard_map/outer_cells/pallas_call | solution.py:330
  23.1 0.0 collective-permute-done.6.beside_ref
  23.1 0.0 collective-permute-done.4.clo_ref
  23.1 0.0 collective-permute-done.5.chi_ref
  23.1 3.5 %sample_and_gram.1 = (f32[3,16,32,512]{3,2,1,0:T(8,128)}, f32[3,16,32,512]{3,2,1,0:T(8,128)S(1)}, f32[3,2048,128]{2,1,0:T(8,128)S(1)}, f32[64,3072]{1,0:T(8,128)S(1)}, f32[104,128]{1,0:T(8,128)S(1)}) custom-call(s32[16,128]{1,0:T(8,128)S(1)} %get-tuple-element.28.at_in.at_ref, ...), custom_call_target="tpu_custom_call", output_to_operand_aliasing={{0}: (13, {}), {1}: (14, {}), {2}: (15, {}), {3}: (16, {})} | custom-call | flops 15728640 | bytes 1572864 | tf_op jit(solution)/shard_map/sample_and_gram/pallas_call | solution.py:444
  26.6 0.3 collective-permute-start.7
  26.9 1.8 %collective-permute-start.8 = (f32[104,128]{1,0:T(8,128)S(1)}, f32[104,128]{1,0:T(8,128)S(1)}, u32[]{:S(2)}, u32[]{:S(2)}) collective-permute-start(f32[104,128]{1,0:T(8,128)S(1)} %get-tuple-element.47), channel_id=1, source_target_pairs={{0,4},{1,5},{2,6},{3,7},{4,0},{5,1},{6,2},{7,3},{8,12},{9,13},{10,... | collective-permute-start | bytes 159752 | tf_op jit(solution)/shard_map/ppermute | solution.py:607
  28.7 1.5 %collective-permute-start.9 = (f32[104,128]{1,0:T(8,128)S(1)}, f32[104,128]{1,0:T(8,128)S(1)}, u32[]{:S(2)}, u32[]{:S(2)}) collective-permute-start(f32[104,128]{1,0:T(8,128)S(1)} %get-tuple-element.47), channel_id=1, source_target_pairs={{0,2},{1,3},{2,0},{3,1},{4,6},{5,7},{6,4},{7,5},{8,10},{9,11},{10,... | collective-permute-start | bytes 159752 | tf_op jit(solution)/shard_map/ppermute | solution.py:607
  30.1 1.5 %collective-permute-done.7 = f32[104,128]{1,0:T(8,128)S(1)} collective-permute-done((f32[104,128]{1,0:T(8,128)S(1)}, f32[104,128]{1,0:T(8,128)S(1)}, u32[]{:S(2)}, u32[]{:S(2)}) %collective-permute-start.7) | collective-permute-done | bytes 53280 | tf_op jit(solution)/shard_map/ppermute | solution.py:607
  31.7 0.0 collective-permute-done.8
  31.7 1.1 %collective-permute-done.9 = f32[104,128]{1,0:T(8,128)S(1)} collective-permute-done((f32[104,128]{1,0:T(8,128)S(1)}, f32[104,128]{1,0:T(8,128)S(1)}, u32[]{:S(2)}, u32[]{:S(2)}) %collective-permute-start.9) | collective-permute-done | bytes 53280 | tf_op jit(solution)/shard_map/ppermute | solution.py:607
  32.8 3.3 %collective-permute-start.10 = (f32[104,128]{1,0:T(8,128)S(1)}, f32[104,128]{1,0:T(8,128)S(1)}, u32[]{:S(2)}, u32[]{:S(2)}) collective-permute-start(f32[104,128]{1,0:T(8,128)S(1)} %add_add_fusion.1), channel_id=1, source_target_pairs={{0,24},{1,25},{2,26},{3,27},{4,28},{5,29},{6,30},{7,31},{8,16},{9,... | collective-permute-start | bytes 159752 | tf_op jit(solution)/shard_map/ppermute | solution.py:607
  36.1 0.0 collective-permute-start.11
  36.1 1.1 %collective-permute-start.12 = (f32[104,128]{1,0:T(8,128)S(1)}, f32[104,128]{1,0:T(8,128)S(1)}, u32[]{:S(2)}, u32[]{:S(2)}) collective-permute-start(f32[104,128]{1,0:T(8,128)S(1)} %add_add_fusion.1), channel_id=1, source_target_pairs={{0,8},{1,9},{2,10},{3,11},{4,12},{5,13},{6,14},{7,15},{8,0},{9,1},... | collective-permute-start | bytes 159752 | tf_op jit(solution)/shard_map/ppermute | solution.py:607
  37.3 1.6 %collective-permute-done.10 = f32[104,128]{1,0:T(8,128)S(1)} collective-permute-done((f32[104,128]{1,0:T(8,128)S(1)}, f32[104,128]{1,0:T(8,128)S(1)}, u32[]{:S(2)}, u32[]{:S(2)}) %collective-permute-start.10) | collective-permute-done | bytes 53280 | tf_op jit(solution)/shard_map/ppermute | solution.py:607
  38.9 2.2 %collective-permute-done.11 = f32[104,128]{1,0:T(8,128)S(1)} collective-permute-done((f32[104,128]{1,0:T(8,128)S(1)}, f32[104,128]{1,0:T(8,128)S(1)}, u32[]{:S(2)}, u32[]{:S(2)}) %collective-permute-start.11) | collective-permute-done | bytes 53280 | tf_op jit(solution)/shard_map/ppermute | solution.py:607
  41.2 0.0 collective-permute-done.12
  41.2 0.1 collective-permute-start.13
  41.3 1.2 %collective-permute-done.13.other_ref = f32[104,128]{1,0:T(8,128)S(1)} collective-permute-done((f32[104,128]{1,0:T(8,128)S(1)}, f32[104,128]{1,0:T(8,128)S(1)}, u32[]{:S(2)}, u32[]{:S(2)}) %collective-permute-start.13) | collective-permute-done | bytes 53280 | tf_op jit(solution)/shard_map/ppermute | solution.py:607
  42.5 8.3 %factor_and_basis.1 = (f32[192,192]{1,0:T(8,128)}, f32[192,3072]{1,0:T(8,128)}) custom-call(f32[1,128]{1,0:T(1,128)S(1)} %bitcast.4, f32[104,128]{1,0:T(8,128)S(1)} %add_add_fusion.mine_ref, f32[104,128]{1,0:T(8,128)S(1)} %collective-permute-done.13.other_ref, s32[16,128]{1,0:T(8,128)S(1)} %get-tuple-element.28.at_in.at_ref, f32[128,3072]{1,0:T(8,128)S(1)} %copy-done.1, ...), custom_call_target="tpu_custom_call" | custom-call | flops 1358954496 | bytes 4718592 | tf_op jit(solution)/shard_map/factor_and_basis/pallas_call | solution.py:578
  (3 shorter events, 0.0 us)
Async XLA Ops:
  0.6 9.4 %copy-start = (f32[3,16,32,512]{3,2,1,0:T(8,128)S(1)}, f32[3,16,32,512]{3,2,1,0:T(8,128)}, u32[]{:S(2)}) copy-start(f32[3,16,32,512]{3,2,1,0:T(8,128)} %velocity_ref.5) | copy-start | bytes 9437188
  0.6 13.1 %copy-start.5 = (f32[128]{0:T(128)S(1)}, f32[128]{0:T(128)}, u32[]{:S(2)}) copy-start(f32[128]{0:T(128)} %param.8) | copy-start | bytes 1540
  0.7 13.1 %copy-start.3 = (s32[1024]{0:T(1024)S(1)}, s32[1024]{0:T(1024)}, u32[]{:S(2)}) copy-start(s32[1024]{0:T(1024)} %param.10) | copy-start | bytes 12292
  0.7 13.1 %copy-start.4 = (s32[64]{0:T(128)S(1)}, s32[64]{0:T(128)}, u32[]{:S(2)}) copy-start(s32[64]{0:T(128)} %steps_ref.1) | copy-start | bytes 772
  0.7 13.1 %copy-start.1 = (f32[128,3072]{1,0:T(8,128)S(1)}, f32[128,3072]{1,0:T(8,128)}, u32[]{:S(2)}) copy-start(f32[128,3072]{1,0:T(8,128)} %modes_ref.5) | copy-start | bytes 4718596
  0.7 13.1 %copy-start.2 = (f32[63,3072]{1,0:T(8,128)S(1)}, f32[63,3072]{1,0:T(8,128)}, u32[]{:S(2)}) copy-start(f32[63,3072]{1,0:T(8,128)} %history_ref.1) | copy-start | bytes 2322436
  2.2 17.2 %collective-permute-start = (f32[3,2,32,512]{3,2,1,0:T(8,128)S(1)}, f32[3,2,32,512]{3,2,1,0:T(8,128)S(1)}, u32[]{:S(2)}, u32[]{:S(2)}) collective-permute-start(f32[3,2,32,512]{3,2,1,0:T(8,128)S(1)} %get-tuple-element.31), channel_id=1, source_target_pairs={{0,1},{1,2},{2,3},{3,0},{4,5},{5,6},{6,7},{7,4},{8,9},{9,10},{10,1... | collective-permute-start | bytes 1179656 | tf_op jit(solution)/shard_map/ppermute | solution.py:614
  2.7 16.7 %collective-permute-start.1 = (f32[3,2,32,512]{3,2,1,0:T(8,128)S(1)}, f32[3,2,32,512]{3,2,1,0:T(8,128)S(1)}, u32[]{:S(2)}, u32[]{:S(2)}) collective-permute-start(f32[3,2,32,512]{3,2,1,0:T(8,128)S(1)} %get-tuple-element.32), channel_id=1, source_target_pairs={{0,3},{1,0},{2,1},{3,2},{4,7},{5,4},{6,5},{7,6},{8,11},{9,8},{10,9... | collective-permute-start | bytes 1179656 | tf_op jit(solution)/shard_map/ppermute | solution.py:615
  4.7 11.8 %collective-permute-start.2 = (f32[3,16,2,512]{3,2,1,0:T(2,128)S(1)}, f32[3,16,2,512]{3,2,1,0:T(2,128)S(1)}, u32[]{:S(2)}, u32[]{:S(2)}) collective-permute-start(f32[3,16,2,512]{3,2,1,0:T(2,128)S(1)} %get-tuple-element.33), channel_id=1, source_target_pairs={{0,4},{4,8},{8,12},{12,16},{16,20},{20,24},{24,28},{28,0},{1,5},{5... | collective-permute-start | bytes 589832 | tf_op jit(solution)/shard_map/ppermute | solution.py:616
  7.0 10.6 %collective-permute-start.3 = (f32[3,16,2,512]{3,2,1,0:T(2,128)S(1)}, f32[3,16,2,512]{3,2,1,0:T(2,128)S(1)}, u32[]{:S(2)}, u32[]{:S(2)}) collective-permute-start(f32[3,16,2,512]{3,2,1,0:T(2,128)S(1)} %get-tuple-element.34), channel_id=1, source_target_pairs={{0,28},{4,0},{8,4},{12,8},{16,12},{20,16},{24,20},{28,24},{1,29},{... | collective-permute-start | bytes 589832 | tf_op jit(solution)/shard_map/ppermute | solution.py:617
  16.4 6.7 %collective-permute-start.6 = (f32[96,128]{1,0:T(8,128)S(1)}, f32[96,128]{1,0:T(8,128)S(1)}, u32[]{:S(2)}, u32[]{:S(2)}) collective-permute-start(f32[96,128]{1,0:T(8,128)S(1)} %get-tuple-element.41), channel_id=1, source_target_pairs={{0,1},{1,0},{2,3},{3,2},{4,5},{5,4},{6,7},{7,6},{8,9},{9,8},{10,11... | collective-permute-start | bytes 147464 | tf_op jit(solution)/shard_map/ppermute | solution.py:607
  17.6 5.5 %collective-permute-start.4 = (f32[3,2,512]{2,1,0:T(2,128)S(1)}, f32[3,2,512]{2,1,0:T(2,128)S(1)}, u32[]{:S(2)}, u32[]{:S(2)}) collective-permute-start(f32[3,2,512]{2,1,0:T(2,128)S(1)} %get-tuple-element.36.own_hi_ref), channel_id=1, source_target_pairs={{0,1},{1,2},{2,3},{3,0},{4,5},{5,6},{6,7},{7,4},{8,9},{9,10},{10,1... | collective-permute-start | bytes 36872 | tf_op jit(solution)/shard_map/ppermute | solution.py:628
  17.6 5.4 %collective-permute-start.5 = (f32[3,2,512]{2,1,0:T(2,128)S(1)}, f32[3,2,512]{2,1,0:T(2,128)S(1)}, u32[]{:S(2)}, u32[]{:S(2)}) collective-permute-start(f32[3,2,512]{2,1,0:T(2,128)S(1)} %get-tuple-element.37.own_lo_ref), channel_id=1, source_target_pairs={{0,3},{1,0},{2,1},{3,2},{4,7},{5,4},{6,5},{7,6},{8,11},{9,8},{10,9... | collective-permute-start | bytes 36872 | tf_op jit(solution)/shard_map/ppermute | solution.py:629
  26.6 5.1 %collective-permute-start.7 = (f32[104,128]{1,0:T(8,128)S(1)}, f32[104,128]{1,0:T(8,128)S(1)}, u32[]{:S(2)}, u32[]{:S(2)}) collective-permute-start(f32[104,128]{1,0:T(8,128)S(1)} %get-tuple-element.47), channel_id=1, source_target_pairs={{0,6},{1,7},{2,4},{3,5},{4,2},{5,3},{6,0},{7,1},{8,14},{9,15},{10,... | collective-permute-start | bytes 159752 | tf_op jit(solution)/shard_map/ppermute | solution.py:607
  26.9 4.8 %collective-permute-start.8 = (f32[104,128]{1,0:T(8,128)S(1)}, f32[104,128]{1,0:T(8,128)S(1)}, u32[]{:S(2)}, u32[]{:S(2)}) collective-permute-start(f32[104,128]{1,0:T(8,128)S(1)} %get-tuple-element.47), channel_id=1, source_target_pairs={{0,4},{1,5},{2,6},{3,7},{4,0},{5,1},{6,2},{7,3},{8,12},{9,13},{10,... | collective-permute-start | bytes 159752 | tf_op jit(solution)/shard_map/ppermute | solution.py:607
  28.7 4.1 %collective-permute-start.9 = (f32[104,128]{1,0:T(8,128)S(1)}, f32[104,128]{1,0:T(8,128)S(1)}, u32[]{:S(2)}, u32[]{:S(2)}) collective-permute-start(f32[104,128]{1,0:T(8,128)S(1)} %get-tuple-element.47), channel_id=1, source_target_pairs={{0,2},{1,3},{2,0},{3,1},{4,6},{5,7},{6,4},{7,5},{8,10},{9,11},{10,... | collective-permute-start | bytes 159752 | tf_op jit(solution)/shard_map/ppermute | solution.py:607
  32.8 6.1 %collective-permute-start.10 = (f32[104,128]{1,0:T(8,128)S(1)}, f32[104,128]{1,0:T(8,128)S(1)}, u32[]{:S(2)}, u32[]{:S(2)}) collective-permute-start(f32[104,128]{1,0:T(8,128)S(1)} %add_add_fusion.1), channel_id=1, source_target_pairs={{0,24},{1,25},{2,26},{3,27},{4,28},{5,29},{6,30},{7,31},{8,16},{9,... | collective-permute-start | bytes 159752 | tf_op jit(solution)/shard_map/ppermute | solution.py:607
  36.1 5.0 %collective-permute-start.11 = (f32[104,128]{1,0:T(8,128)S(1)}, f32[104,128]{1,0:T(8,128)S(1)}, u32[]{:S(2)}, u32[]{:S(2)}) collective-permute-start(f32[104,128]{1,0:T(8,128)S(1)} %add_add_fusion.1), channel_id=1, source_target_pairs={{0,16},{1,17},{2,18},{3,19},{4,20},{5,21},{6,22},{7,23},{8,24},{9,... | collective-permute-start | bytes 159752 | tf_op jit(solution)/shard_map/ppermute | solution.py:607
  36.1 5.0 %collective-permute-start.12 = (f32[104,128]{1,0:T(8,128)S(1)}, f32[104,128]{1,0:T(8,128)S(1)}, u32[]{:S(2)}, u32[]{:S(2)}) collective-permute-start(f32[104,128]{1,0:T(8,128)S(1)} %add_add_fusion.1), channel_id=1, source_target_pairs={{0,8},{1,9},{2,10},{3,11},{4,12},{5,13},{6,14},{7,15},{8,0},{9,1},... | collective-permute-start | bytes 159752 | tf_op jit(solution)/shard_map/ppermute | solution.py:607
  41.2 1.3 %collective-permute-start.13 = (f32[104,128]{1,0:T(8,128)S(1)}, f32[104,128]{1,0:T(8,128)S(1)}, u32[]{:S(2)}, u32[]{:S(2)}) collective-permute-start(f32[104,128]{1,0:T(8,128)S(1)} %add_add_fusion.mine_ref), channel_id=1, source_target_pairs={{0,1},{1,0},{2,3},{3,2},{4,5},{5,4},{6,7},{7,6},{8,9},{9,8},{10,11... | collective-permute-start | bytes 159752 | tf_op jit(solution)/shard_map/ppermute | solution.py:607

commit v7 on v6

--- a/solution.py
+++ b/solution.py
@@ -58,6 +58,19 @@
         compiler_params=pltpu.CompilerParams(vmem_limit_bytes=2 * 2**20),
         name="faces",
     )(in_hbm(velocity))
+
+
+def product(a, pieces):
+    n = a.shape[0]
+    high, mid, low = split(a)
+    first = bf16_dot(jnp.concatenate([high, mid, low], axis=0), pieces[0])
+    second = bf16_dot(jnp.concatenate([high, mid], axis=0), pieces[1])
+    small = first[2 * n :] + second[n:] + bf16_dot(high, pieces[2])
+    return first[0:n] + (first[n : 2 * n] + second[0:n] + small)
+
+
+def bf16_dot(a, b):
+    return lax.dot_general(a, b, (((1,), (0,)), ((), ())), preferred_element_type=jnp.float32)
 
 
 def split(array):
@@ -505,7 +518,7 @@
 
 
 def basis_kernel(
-    root, w_ref, mine_ref, other_ref, at_ref, modes_ref, snaps_ref, factor_ref, basis_ref, packed, inverse, factor, basis, sems
+    root, w_ref, mine_ref, other_ref, at_ref, modes_ref, snaps_ref, factor_ref, basis_ref, packed, factor, basis, pieces, sems
 ):
     total = factor.shape[0]
     half = total // 3
@@ -532,6 +545,17 @@
     d = dot(w0, jnp.concatenate([r0, w0], axis=1), 0, 0)
     r1, m1 = eliminate([second_rows - d[0:half, LANES:], jnp.where(left, eye, -d[0:half, 0:LANES])], 0)
     e = dot(r1, jnp.concatenate([r1, m1], axis=1), 0, 0)[half:two]
+    wide = pltpu.roll(w_ref[...], half, 1) * root
+    above = jnp.concatenate([jnp.where(left, 0.0, r0) * wide, m1 * wide], axis=0)
+    width = basis.shape[1]
+    parts = sems.shape[0] - 2
+    chunk = width // parts
+    for i in range(parts):
+        at = slice(i * chunk, (i + 1) * chunk)
+        rows = jnp.concatenate([modes_ref[half:two, at], modes_ref[0:half, at], snaps_ref[:, at]], axis=0)
+        for k, piece in enumerate(split(rows)):
+            pieces[k, :, at] = piece
+        basis[0:two, at] = product(above, [pieces[k, 0:two, at] for k in range(3)])
     r2, m2 = eliminate(
         [
             jnp.where(left, eye, ends - d[half:two, LANES:] - e[:, 0:LANES]),
@@ -539,14 +563,10 @@
         ],
         half,
     )
-    wide = pltpu.roll(w_ref[...], half, 1) * root
-    inverse[0:half, 0:two] = jnp.where(left, 0.0, r0) * wide
-    inverse[half:two, 0:two] = m1 * wide
-    inverse[two:, 0:two] = m2 * wide
+    copies = [pltpu.make_async_copy(basis.at[0:two], basis_ref.at[0:two], sems.at[0])]
+    copies[0].start()
+    below = jnp.concatenate([m2 * wide, r2[:, 0:half] * root], axis=1)
     zero = jnp.zeros((half, half), jnp.float32)
-    inverse[0:half, two:total] = zero
-    inverse[half:two, two:total] = zero
-    inverse[two:, two:total] = r2[:, 0:half] * root
     scale = 1.0 / root
     factor[0:half, 0:half] = jnp.where(row <= lane, r0, 0.0)[:, 0:half] * scale
     factor[0:half, half:] = w0 * scale
@@ -555,16 +575,12 @@
     factor[two:, 0:half] = zero
     factor[two:, half:two] = zero
     factor[two:, two:] = jnp.where(row + half <= lane, r2, 0.0)[:, half:] * scale
-    copies = [pltpu.make_async_copy(factor, factor_ref, sems.at[0])]
-    copies[0].start()
-    width = basis.shape[1]
-    parts = sems.shape[0] - 1
-    chunk = width // parts
+    copies.append(pltpu.make_async_copy(factor, factor_ref, sems.at[1]))
+    copies[1].start()
     for i in range(parts):
         at = slice(i * chunk, (i + 1) * chunk)
-        rows = jnp.concatenate([modes_ref[half:two, at], modes_ref[0:half, at], snaps_ref[:, at]], axis=0)
-        basis[:, at] = dot(inverse[:, 0:total], rows)
-        copies.append(pltpu.make_async_copy(basis.at[:, at], basis_ref.at[:, at], sems.at[i + 1]))
+        basis[two:, at] = product(below, [pieces[k, :, at] for k in range(3)])
+        copies.append(pltpu.make_async_copy(basis.at[two:, at], basis_ref.at[two:, at], sems.at[i + 2]))
         copies[-1].start()
     for copy in copies:
         copy.wait()
@@ -582,10 +598,10 @@
         out_shape=[pltpu.HBM((total, total), jnp.float32), pltpu.HBM((total, width), jnp.float32)],
         scratch_shapes=[
             pltpu.VMEM((total, LANES), jnp.float32),
-            pltpu.VMEM((total, 2 * LANES), jnp.float32),
             pltpu.VMEM((total, total), jnp.float32),
             pltpu.VMEM((total, width), jnp.float32),
-            pltpu.SemaphoreType.DMA((PARTS + 1,)),
+            pltpu.VMEM((3, total, width), jnp.bfloat16),
+            pltpu.SemaphoreType.DMA((PARTS + 2,)),
         ],
         compiler_params=pltpu.CompilerParams(vmem_limit_bytes=16 * 2**20),
         cost_estimate=pl.CostEstimate(

time: 51.1 us -> 49.9 us (0.977)
  Pallas kernels: 23.3 us -> 22.1 us
    pallas_call x1, Pallas kernels: 8.34 us -> 7.15 us  [basis_call(): pl.pallas_call(functools.partial(basis_kernel, root), in_specs=[vmem] * 6...]
where the time goes in v7:
time: 49.9 us; the launch traced here: 49.8 us
  Pallas kernels  22.1 us (44%)
  starting transfers between devices  17.7 us (35%)
  waiting for transfers between devices  8.9 us (18%)
  between operations  0.99 us (2%)
    ppermute x8, starting transfers between devices, swap(): lax.ppermute(array, ('tile', 'grp'), [(i, i ^ bits) for i in range(device...  8.15 us
    ppermute x8, waiting for transfers between devices, swap(): lax.ppermute(array, ('tile', 'grp'), [(i, i ^ bits) for i in range(device...  7.78 us
    pallas_call x1, Pallas kernels, basis_call(): pl.pallas_call(functools.partial(basis_kernel, root), in_specs=[vmem] * 6...  7.15 us
    pallas_call x1, Pallas kernels, inner_call(): pl.pallas_call(inner_kernel, in_specs=[vmem], out_specs=[vmem] * 3, out_s...  3.71 us
    pallas_call x1, Pallas kernels, outer_call(): pl.pallas_call(outer_kernel, in_specs=[vmem] * 8, out_specs=[vmem, vmem,...  3.68 us
    pallas_call x1, Pallas kernels, sample_call(): pl.pallas_call(sample_kernel, in_specs=[vmem] * 13 + [hbm, vmem, vmem, vm...  3.47 us
    ppermute x1, starting transfers between devices, per_device(): yhi = lax.ppermute(ylow, 'tile', down_y)  3.04 us
    pallas_call x1, Pallas kernels, early_gram(): pl.pallas_call(functools.partial(gram_kernel, lines), in_specs=[pl.BlockS...  2.58 us
  transfers between devices with their start and end apart: 14, of which 6 were waited for; matrix products, arithmetic and copies ran while one was open for 0% of the time, Pallas kernels for 20%

profile of v7, /device:TPU:0, one launch (start us, length us, event | category | flops | bytes accessed | tf_op | source)
XLA Modules:
  0.0 49.8 jit_solution(12210083972364837535)
XLA Ops:
  0.6 0.0 copy-start
  0.6 0.0 copy-start.5
  0.7 0.0 copy-start.3
  0.7 0.0 copy-start.4
  0.7 0.0 copy-start.1
  0.7 0.0 copy-start.2
  0.7 1.5 %faces.1 = (f32[3,16,2,512]{3,2,1,0:T(2,128)S(1)}, f32[3,16,2,512]{3,2,1,0:T(2,128)S(1)}, f32[3,2,32,512]{3,2,1,0:T(8,128)S(1)}, f32[3,2,32,512]{3,2,1,0:T(8,128)S(1)}) custom-call(f32[3,16,32,512]{3,2,1,0:T(8,128)} %velocity_ref.5), custom_call_target="tpu_custom_call" | custom-call | tf_op jit(solution)/shard_map/faces/pallas_call | solution.py:52
  2.2 0.5 %collective-permute-start = (f32[3,2,32,512]{3,2,1,0:T(8,128)S(1)}, f32[3,2,32,512]{3,2,1,0:T(8,128)S(1)}, u32[]{:S(2)}, u32[]{:S(2)}) collective-permute-start(f32[3,2,32,512]{3,2,1,0:T(8,128)S(1)} %get-tuple-element.31), channel_id=1, source_target_pairs={{0,1},{1,2},{2,3},{3,0},{4,5},{5,6},{6,7},{7,4},{8,9},{9,10},{10,1... | collective-permute-start | bytes 1179656 | tf_op jit(solution)/shard_map/ppermute | solution.py:630
  2.7 2.0 %collective-permute-start.1 = (f32[3,2,32,512]{3,2,1,0:T(8,128)S(1)}, f32[3,2,32,512]{3,2,1,0:T(8,128)S(1)}, u32[]{:S(2)}, u32[]{:S(2)}) collective-permute-start(f32[3,2,32,512]{3,2,1,0:T(8,128)S(1)} %get-tuple-element.32), channel_id=1, source_target_pairs={{0,3},{1,0},{2,1},{3,2},{4,7},{5,4},{6,5},{7,6},{8,11},{9,8},{10,9... | collective-permute-start | bytes 1179656 | tf_op jit(solution)/shard_map/ppermute | solution.py:631
  4.7 2.3 %collective-permute-start.2 = (f32[3,16,2,512]{3,2,1,0:T(2,128)S(1)}, f32[3,16,2,512]{3,2,1,0:T(2,128)S(1)}, u32[]{:S(2)}, u32[]{:S(2)}) collective-permute-start(f32[3,16,2,512]{3,2,1,0:T(2,128)S(1)} %get-tuple-element.33), channel_id=1, source_target_pairs={{0,4},{4,8},{8,12},{12,16},{16,20},{20,24},{24,28},{28,0},{1,5},{5... | collective-permute-start | bytes 589832 | tf_op jit(solution)/shard_map/ppermute | solution.py:632
  7.0 3.0 %collective-permute-start.3 = (f32[3,16,2,512]{3,2,1,0:T(2,128)S(1)}, f32[3,16,2,512]{3,2,1,0:T(2,128)S(1)}, u32[]{:S(2)}, u32[]{:S(2)}) collective-permute-start(f32[3,16,2,512]{3,2,1,0:T(2,128)S(1)} %get-tuple-element.34), channel_id=1, source_target_pairs={{0,28},{4,0},{8,4},{12,8},{16,12},{20,16},{24,20},{28,24},{1,29},{... | collective-permute-start | bytes 589832 | tf_op jit(solution)/shard_map/ppermute | solution.py:633
  10.0 0.0 copy-done
  10.0 3.7 %inner_cells.1 = (f32[3,18,40,512]{3,2,1,0:T(8,128)S(1)}, f32[3,2048,128]{2,1,0:T(8,128)S(1)}, f32[3,16,32,512]{3,2,1,0:T(8,128)S(1)}) custom-call(f32[3,16,32,512]{3,2,1,0:T(8,128)S(1)} %copy-done), custom_call_target="tpu_custom_call" | custom-call | flops 47185920 | bytes 3145728 | tf_op jit(solution)/shard_map/inner_cells/pallas_call | solution.py:327
  13.7 0.0 copy-done.5
  13.7 0.0 copy-done.3
  13.7 0.0 copy-done.4
  13.8 0.0 copy-done.1
  13.8 0.0 copy-done.2
  13.8 2.6 %early_gram.1 = (f32[96,128]{1,0:T(8,128)S(1)}, f32[96,128]{1,0:T(8,128)S(1)}, f32[64,3072]{1,0:T(8,128)S(1)}, f32[128,128]{1,0:T(8,128)S(1)}, s32[16,128]{1,0:T(8,128)S(1)}, /*index=5*/f32[1024,128]{1,0:T(8,128)S(1)}) custom-call(s32[64]{0:T(128)S(1)} %copy-done.4, f32[1,128]{1,0:T(1,128)S(1)} %bitcast.3, f32[128,3072]{1,0:T(8,128)S(1)} %copy-done.1, ...), custom_call_target="tpu_custom_call" | custom-call | flops 905969664 | bytes 7077888 | tf_op jit(solution)/shard_map/early_gram/pallas_call | solution.py:138
  16.4 0.1 collective-permute-start.6
  16.4 0.0 collective-permute-done.2.ylo_ref
  16.5 1.1 %collective-permute-done.3.yhi_ref = f32[3,16,2,512]{3,2,1,0:T(2,128)S(1)} collective-permute-done((f32[3,16,2,512]{3,2,1,0:T(2,128)S(1)}, f32[3,16,2,512]{3,2,1,0:T(2,128)S(1)}, u32[]{:S(2)}, u32[]{:S(2)}) %collective-permute-start.3) | collective-permute-done | bytes 196640 | tf_op jit(solution)/shard_map/ppermute | solution.py:633
  17.6 0.1 collective-permute-start.4
  17.6 1.7 %collective-permute-start.5 = (f32[3,2,512]{2,1,0:T(2,128)S(1)}, f32[3,2,512]{2,1,0:T(2,128)S(1)}, u32[]{:S(2)}, u32[]{:S(2)}) collective-permute-start(f32[3,2,512]{2,1,0:T(2,128)S(1)} %get-tuple-element.37.own_lo_ref), channel_id=1, source_target_pairs={{0,3},{1,0},{2,1},{3,2},{4,7},{5,4},{6,5},{7,6},{8,11},{9,8},{10,9... | collective-permute-start | bytes 36872 | tf_op jit(solution)/shard_map/ppermute | solution.py:645
  19.4 0.0 collective-permute-done.xlo_ref
  19.4 0.0 collective-permute-done.1.xhi_ref
  19.4 3.7 %outer_cells.1 = (f32[3,18,40,512]{3,2,1,0:T(8,128)S(1)}, f32[3,2048,128]{2,1,0:T(8,128)S(1)}, f32[3,16,32,512]{3,2,1,0:T(8,128)S(1)}, f32[3,16,32,512]{3,2,1,0:T(8,128)}) custom-call(f32[3,16,32,512]{3,2,1,0:T(8,128)S(1)} %copy-done, f32[3,2,32,512]{3,2,1,0:T(8,128)S(1)} %collective-permute-done.xlo_ref, ...), custom_call_target="tpu_custom_call", output_to_operand_aliasing={{0}: (5, {}), {1}: (6, {}), {2}: (7, {})} | custom-call | flops 31457280 | bytes 3145728 | tf_op jit(solution)/shard_map/outer_cells/pallas_call | solution.py:343
  23.1 0.0 collective-permute-done.6.beside_ref
  23.1 0.0 collective-permute-done.4.clo_ref
  23.1 0.0 collective-permute-done.5.chi_ref
  23.1 3.5 %sample_and_gram.1 = (f32[3,16,32,512]{3,2,1,0:T(8,128)}, f32[3,16,32,512]{3,2,1,0:T(8,128)S(1)}, f32[3,2048,128]{2,1,0:T(8,128)S(1)}, f32[64,3072]{1,0:T(8,128)S(1)}, f32[104,128]{1,0:T(8,128)S(1)}) custom-call(s32[16,128]{1,0:T(8,128)S(1)} %get-tuple-element.28.at_in.at_ref, ...), custom_call_target="tpu_custom_call", output_to_operand_aliasing={{0}: (13, {}), {1}: (14, {}), {2}: (15, {}), {3}: (16, {})} | custom-call | flops 15728640 | bytes 1572864 | tf_op jit(solution)/shard_map/sample_and_gram/pallas_call | solution.py:457
  26.6 0.3 collective-permute-start.7
  26.9 1.8 %collective-permute-start.8 = (f32[104,128]{1,0:T(8,128)S(1)}, f32[104,128]{1,0:T(8,128)S(1)}, u32[]{:S(2)}, u32[]{:S(2)}) collective-permute-start(f32[104,128]{1,0:T(8,128)S(1)} %get-tuple-element.47), channel_id=1, source_target_pairs={{0,4},{1,5},{2,6},{3,7},{4,0},{5,1},{6,2},{7,3},{8,12},{9,13},{10,... | collective-permute-start | bytes 159752 | tf_op jit(solution)/shard_map/ppermute | solution.py:623
  28.7 1.5 %collective-permute-start.9 = (f32[104,128]{1,0:T(8,128)S(1)}, f32[104,128]{1,0:T(8,128)S(1)}, u32[]{:S(2)}, u32[]{:S(2)}) collective-permute-start(f32[104,128]{1,0:T(8,128)S(1)} %get-tuple-element.47), channel_id=1, source_target_pairs={{0,2},{1,3},{2,0},{3,1},{4,6},{5,7},{6,4},{7,5},{8,10},{9,11},{10,... | collective-permute-start | bytes 159752 | tf_op jit(solution)/shard_map/ppermute | solution.py:623
  30.1 1.5 %collective-permute-done.7 = f32[104,128]{1,0:T(8,128)S(1)} collective-permute-done((f32[104,128]{1,0:T(8,128)S(1)}, f32[104,128]{1,0:T(8,128)S(1)}, u32[]{:S(2)}, u32[]{:S(2)}) %collective-permute-start.7) | collective-permute-done | bytes 53280 | tf_op jit(solution)/shard_map/ppermute | solution.py:623
  31.7 0.0 collective-permute-done.8
  31.7 1.1 %collective-permute-done.9 = f32[104,128]{1,0:T(8,128)S(1)} collective-permute-done((f32[104,128]{1,0:T(8,128)S(1)}, f32[104,128]{1,0:T(8,128)S(1)}, u32[]{:S(2)}, u32[]{:S(2)}) %collective-permute-start.9) | collective-permute-done | bytes 53280 | tf_op jit(solution)/shard_map/ppermute | solution.py:623
  32.8 3.3 %collective-permute-start.10 = (f32[104,128]{1,0:T(8,128)S(1)}, f32[104,128]{1,0:T(8,128)S(1)}, u32[]{:S(2)}, u32[]{:S(2)}) collective-permute-start(f32[104,128]{1,0:T(8,128)S(1)} %add_add_fusion.1), channel_id=1, source_target_pairs={{0,24},{1,25},{2,26},{3,27},{4,28},{5,29},{6,30},{7,31},{8,16},{9,... | collective-permute-start | bytes 159752 | tf_op jit(solution)/shard_map/ppermute | solution.py:623
  36.1 0.0 collective-permute-start.11
  36.1 1.1 %collective-permute-start.12 = (f32[104,128]{1,0:T(8,128)S(1)}, f32[104,128]{1,0:T(8,128)S(1)}, u32[]{:S(2)}, u32[]{:S(2)}) collective-permute-start(f32[104,128]{1,0:T(8,128)S(1)} %add_add_fusion.1), channel_id=1, source_target_pairs={{0,8},{1,9},{2,10},{3,11},{4,12},{5,13},{6,14},{7,15},{8,0},{9,1},... | collective-permute-start | bytes 159752 | tf_op jit(solution)/shard_map/ppermute | solution.py:623
  37.3 1.6 %collective-permute-done.10 = f32[104,128]{1,0:T(8,128)S(1)} collective-permute-done((f32[104,128]{1,0:T(8,128)S(1)}, f32[104,128]{1,0:T(8,128)S(1)}, u32[]{:S(2)}, u32[]{:S(2)}) %collective-permute-start.10) | collective-permute-done | bytes 53280 | tf_op jit(solution)/shard_map/ppermute | solution.py:623
  38.9 2.2 %collective-permute-done.11 = f32[104,128]{1,0:T(8,128)S(1)} collective-permute-done((f32[104,128]{1,0:T(8,128)S(1)}, f32[104,128]{1,0:T(8,128)S(1)}, u32[]{:S(2)}, u32[]{:S(2)}) %collective-permute-start.11) | collective-permute-done | bytes 53280 | tf_op jit(solution)/shard_map/ppermute | solution.py:623
  41.2 0.0 collective-permute-done.12
  41.2 0.1 collective-permute-start.13
  41.3 1.2 %collective-permute-done.13.other_ref = f32[104,128]{1,0:T(8,128)S(1)} collective-permute-done((f32[104,128]{1,0:T(8,128)S(1)}, f32[104,128]{1,0:T(8,128)S(1)}, u32[]{:S(2)}, u32[]{:S(2)}) %collective-permute-start.13) | collective-permute-done | bytes 53280 | tf_op jit(solution)/shard_map/ppermute | solution.py:623
  42.5 7.2 %factor_and_basis.1 = (f32[192,192]{1,0:T(8,128)}, f32[192,3072]{1,0:T(8,128)}) custom-call(f32[1,128]{1,0:T(1,128)S(1)} %bitcast.4, f32[104,128]{1,0:T(8,128)S(1)} %add_add_fusion.mine_ref, f32[104,128]{1,0:T(8,128)S(1)} %collective-permute-done.13.other_ref, s32[16,128]{1,0:T(8,128)S(1)} %get-tuple-element.28.at_in.at_ref, f32[128,3072]{1,0:T(8,128)S(1)} %copy-done.1, ...), custom_call_target="tpu_custom_call" | custom-call | flops 1358954496 | bytes 4718592 | tf_op jit(solution)/shard_map/factor_and_basis/pallas_call | solution.py:594
  (3 shorter events, 0.0 us)
Async XLA Ops:
  0.6 9.4 %copy-start = (f32[3,16,32,512]{3,2,1,0:T(8,128)S(1)}, f32[3,16,32,512]{3,2,1,0:T(8,128)}, u32[]{:S(2)}) copy-start(f32[3,16,32,512]{3,2,1,0:T(8,128)} %velocity_ref.5) | copy-start | bytes 9437188
  0.6 13.1 %copy-start.5 = (f32[128]{0:T(128)S(1)}, f32[128]{0:T(128)}, u32[]{:S(2)}) copy-start(f32[128]{0:T(128)} %param.8) | copy-start | bytes 1540
  0.7 13.1 %copy-start.3 = (s32[1024]{0:T(1024)S(1)}, s32[1024]{0:T(1024)}, u32[]{:S(2)}) copy-start(s32[1024]{0:T(1024)} %param.10) | copy-start | bytes 12292
  0.7 13.1 %copy-start.4 = (s32[64]{0:T(128)S(1)}, s32[64]{0:T(128)}, u32[]{:S(2)}) copy-start(s32[64]{0:T(128)} %steps_ref.1) | copy-start | bytes 772
  0.7 13.1 %copy-start.1 = (f32[128,3072]{1,0:T(8,128)S(1)}, f32[128,3072]{1,0:T(8,128)}, u32[]{:S(2)}) copy-start(f32[128,3072]{1,0:T(8,128)} %modes_ref.5) | copy-start | bytes 4718596
  0.7 13.1 %copy-start.2 = (f32[63,3072]{1,0:T(8,128)S(1)}, f32[63,3072]{1,0:T(8,128)}, u32[]{:S(2)}) copy-start(f32[63,3072]{1,0:T(8,128)} %history_ref.1) | copy-start | bytes 2322436
  2.2 17.2 %collective-permute-start = (f32[3,2,32,512]{3,2,1,0:T(8,128)S(1)}, f32[3,2,32,512]{3,2,1,0:T(8,128)S(1)}, u32[]{:S(2)}, u32[]{:S(2)}) collective-permute-start(f32[3,2,32,512]{3,2,1,0:T(8,128)S(1)} %get-tuple-element.31), channel_id=1, source_target_pairs={{0,1},{1,2},{2,3},{3,0},{4,5},{5,6},{6,7},{7,4},{8,9},{9,10},{10,1... | collective-permute-start | bytes 1179656 | tf_op jit(solution)/shard_map/ppermute | solution.py:630
  2.7 16.7 %collective-permute-start.1 = (f32[3,2,32,512]{3,2,1,0:T(8,128)S(1)}, f32[3,2,32,512]{3,2,1,0:T(8,128)S(1)}, u32[]{:S(2)}, u32[]{:S(2)}) collective-permute-start(f32[3,2,32,512]{3,2,1,0:T(8,128)S(1)} %get-tuple-element.32), channel_id=1, source_target_pairs={{0,3},{1,0},{2,1},{3,2},{4,7},{5,4},{6,5},{7,6},{8,11},{9,8},{10,9... | collective-permute-start | bytes 1179656 | tf_op jit(solution)/shard_map/ppermute | solution.py:631
  4.7 11.8 %collective-permute-start.2 = (f32[3,16,2,512]{3,2,1,0:T(2,128)S(1)}, f32[3,16,2,512]{3,2,1,0:T(2,128)S(1)}, u32[]{:S(2)}, u32[]{:S(2)}) collective-permute-start(f32[3,16,2,512]{3,2,1,0:T(2,128)S(1)} %get-tuple-element.33), channel_id=1, source_target_pairs={{0,4},{4,8},{8,12},{12,16},{16,20},{20,24},{24,28},{28,0},{1,5},{5... | collective-permute-start | bytes 589832 | tf_op jit(solution)/shard_map/ppermute | solution.py:632
  7.0 10.6 %collective-permute-start.3 = (f32[3,16,2,512]{3,2,1,0:T(2,128)S(1)}, f32[3,16,2,512]{3,2,1,0:T(2,128)S(1)}, u32[]{:S(2)}, u32[]{:S(2)}) collective-permute-start(f32[3,16,2,512]{3,2,1,0:T(2,128)S(1)} %get-tuple-element.34), channel_id=1, source_target_pairs={{0,28},{4,0},{8,4},{12,8},{16,12},{20,16},{24,20},{28,24},{1,29},{... | collective-permute-start | bytes 589832 | tf_op jit(solution)/shard_map/ppermute | solution.py:633
  16.4 6.7 %collective-permute-start.6 = (f32[96,128]{1,0:T(8,128)S(1)}, f32[96,128]{1,0:T(8,128)S(1)}, u32[]{:S(2)}, u32[]{:S(2)}) collective-permute-start(f32[96,128]{1,0:T(8,128)S(1)} %get-tuple-element.41), channel_id=1, source_target_pairs={{0,1},{1,0},{2,3},{3,2},{4,5},{5,4},{6,7},{7,6},{8,9},{9,8},{10,11... | collective-permute-start | bytes 147464 | tf_op jit(solution)/shard_map/ppermute | solution.py:623
  17.6 5.5 %collective-permute-start.4 = (f32[3,2,512]{2,1,0:T(2,128)S(1)}, f32[3,2,512]{2,1,0:T(2,128)S(1)}, u32[]{:S(2)}, u32[]{:S(2)}) collective-permute-start(f32[3,2,512]{2,1,0:T(2,128)S(1)} %get-tuple-element.36.own_hi_ref), channel_id=1, source_target_pairs={{0,1},{1,2},{2,3},{3,0},{4,5},{5,6},{6,7},{7,4},{8,9},{9,10},{10,1... | collective-permute-start | bytes 36872 | tf_op jit(solution)/shard_map/ppermute | solution.py:644
  17.6 5.4 %collective-permute-start.5 = (f32[3,2,512]{2,1,0:T(2,128)S(1)}, f32[3,2,512]{2,1,0:T(2,128)S(1)}, u32[]{:S(2)}, u32[]{:S(2)}) collective-permute-start(f32[3,2,512]{2,1,0:T(2,128)S(1)} %get-tuple-element.37.own_lo_ref), channel_id=1, source_target_pairs={{0,3},{1,0},{2,1},{3,2},{4,7},{5,4},{6,5},{7,6},{8,11},{9,8},{10,9... | collective-permute-start | bytes 36872 | tf_op jit(solution)/shard_map/ppermute | solution.py:645
  26.6 5.1 %collective-permute-start.7 = (f32[104,128]{1,0:T(8,128)S(1)}, f32[104,128]{1,0:T(8,128)S(1)}, u32[]{:S(2)}, u32[]{:S(2)}) collective-permute-start(f32[104,128]{1,0:T(8,128)S(1)} %get-tuple-element.47), channel_id=1, source_target_pairs={{0,6},{1,7},{2,4},{3,5},{4,2},{5,3},{6,0},{7,1},{8,14},{9,15},{10,... | collective-permute-start | bytes 159752 | tf_op jit(solution)/shard_map/ppermute | solution.py:623
  26.9 4.8 %collective-permute-start.8 = (f32[104,128]{1,0:T(8,128)S(1)}, f32[104,128]{1,0:T(8,128)S(1)}, u32[]{:S(2)}, u32[]{:S(2)}) collective-permute-start(f32[104,128]{1,0:T(8,128)S(1)} %get-tuple-element.47), channel_id=1, source_target_pairs={{0,4},{1,5},{2,6},{3,7},{4,0},{5,1},{6,2},{7,3},{8,12},{9,13},{10,... | collective-permute-start | bytes 159752 | tf_op jit(solution)/shard_map/ppermute | solution.py:623
  28.7 4.1 %collective-permute-start.9 = (f32[104,128]{1,0:T(8,128)S(1)}, f32[104,128]{1,0:T(8,128)S(1)}, u32[]{:S(2)}, u32[]{:S(2)}) collective-permute-start(f32[104,128]{1,0:T(8,128)S(1)} %get-tuple-element.47), channel_id=1, source_target_pairs={{0,2},{1,3},{2,0},{3,1},{4,6},{5,7},{6,4},{7,5},{8,10},{9,11},{10,... | collective-permute-start | bytes 159752 | tf_op jit(solution)/shard_map/ppermute | solution.py:623
  32.8 6.1 %collective-permute-start.10 = (f32[104,128]{1,0:T(8,128)S(1)}, f32[104,128]{1,0:T(8,128)S(1)}, u32[]{:S(2)}, u32[]{:S(2)}) collective-permute-start(f32[104,128]{1,0:T(8,128)S(1)} %add_add_fusion.1), channel_id=1, source_target_pairs={{0,24},{1,25},{2,26},{3,27},{4,28},{5,29},{6,30},{7,31},{8,16},{9,... | collective-permute-start | bytes 159752 | tf_op jit(solution)/shard_map/ppermute | solution.py:623
  36.1 5.0 %collective-permute-start.11 = (f32[104,128]{1,0:T(8,128)S(1)}, f32[104,128]{1,0:T(8,128)S(1)}, u32[]{:S(2)}, u32[]{:S(2)}) collective-permute-start(f32[104,128]{1,0:T(8,128)S(1)} %add_add_fusion.1), channel_id=1, source_target_pairs={{0,16},{1,17},{2,18},{3,19},{4,20},{5,21},{6,22},{7,23},{8,24},{9,... | collective-permute-start | bytes 159752 | tf_op jit(solution)/shard_map/ppermute | solution.py:623
  36.1 5.0 %collective-permute-start.12 = (f32[104,128]{1,0:T(8,128)S(1)}, f32[104,128]{1,0:T(8,128)S(1)}, u32[]{:S(2)}, u32[]{:S(2)}) collective-permute-start(f32[104,128]{1,0:T(8,128)S(1)} %add_add_fusion.1), channel_id=1, source_target_pairs={{0,8},{1,9},{2,10},{3,11},{4,12},{5,13},{6,14},{7,15},{8,0},{9,1},... | collective-permute-start | bytes 159752 | tf_op jit(solution)/shard_map/ppermute | solution.py:623
  41.2 1.3 %collective-permute-start.13 = (f32[104,128]{1,0:T(8,128)S(1)}, f32[104,128]{1,0:T(8,128)S(1)}, u32[]{:S(2)}, u32[]{:S(2)}) collective-permute-start(f32[104,128]{1,0:T(8,128)S(1)} %add_add_fusion.mine_ref), channel_id=1, source_target_pairs={{0,1},{1,0},{2,3},{3,2},{4,5},{5,4},{6,7},{7,6},{8,9},{9,8},{10,11... | collective-permute-start | bytes 159752 | tf_op jit(solution)/shard_map/ppermute | solution.py:623
